TPU v7x, 256 devices: a whole 4x4x8 slice. The times are simulated.
256 devices in a mesh: gz: 2 (over core), row: 4 (over x), col: 32 (over z, y).
Axes of the slice: x: 4, y: 4, z: 8, core: 2. Of those that a mesh axis runs over, the one named last changes fastest.
Arguments:
- right_sides: float32 [256, 4, 16, 256], P(('gz', 'row', 'col')), may hold values from -6 to 6
- lower_inverse: bfloat16 [256, 4, 256, 256], P(('gz', 'row', 'col')), may hold values from -0.375 to 0.375
- upper_inverse: bfloat16 [256, 4, 256, 256], P(('gz', 'row', 'col')), may hold values from -0.375 to 0.375
- lower_blocks: bfloat16 [256, 4, 2, 256, 256], P(('gz', 'row', 'col')), may hold values from -0.125 to 0.125
- upper_blocks: bfloat16 [256, 4, 2, 256, 256], P(('gz', 'row', 'col')), may hold values from -0.125 to 0.125
- node_widths: int32 [256, 4], P(('gz', 'row', 'col')), may hold values from 128 to 256, as said below
- far_levels: int32 [256, 4], P(('gz', 'row', 'col')), may hold values from 0 to 8, as said below
- owner_level: int32 [256], replicated, may hold values from 0 to 8, as said below
Outputs:
- solution: float32 [256, 4, 16, 256], P(('gz', 'row', 'col'))
Inputs may be any that keep to these rules, and one draw needn't show every extreme that they name: Columns c >= node_widths of a supernode are padding; every device holds a supernode with all 256 columns. `far_levels`: between 2 and 8 where the supernode has two or more ancestors, but never past the root; 1 where it has one; 0 for the root and for the slot of the device that owns no separator. `owner_level`: every separator of level u is owned by exactly one device of its group (the devices t with the same t // 2**u); one device owns none and holds 0.
All inputs are finite; a program needn't handle non-finite values.
Results may differ from a plain program's by a relative error of at most 0.018.
Values may be sent and summed in bfloat16 or wider, within the bound.
No kernel may reach another device: no remote copies, remote signals or barrier semaphores. Data moves between devices by JAX's collectives and lax.ppermute only.
A program may use at most 64 MiB of HBM per device.

v0:
```python
import jax
import jax.numpy as jnp
from jax import lax
from jax.sharding import Mesh
from jax.sharding import PartitionSpec as P

W = 256
RHS = 16
NB = 2
LOCAL_LEVELS = 2
LOCAL_COUNT = 3
ROW_COL = ("row", "col_0", "col_1")
GZ_ROW_COL = ("gz", "row", "col_0", "col_1")
COL = ("col_0", "col_1")


def one_axis_at_a_time(value, axes):
    for axis in axes:
        value = lax.psum(value, axis)
    return value


def from_everyone(value, axis):
    copies = jnp.broadcast_to(value, (lax.axis_size(axis), *value.shape))
    return lax.all_to_all(copies, axis, split_axis=0, concat_axis=0, tiled=True)


def taken_together(value, axis):
    return from_everyone(value, axis).sum(axis=0)


def one_axis_at_a_time_2(value, axes):
    far, near = axes
    nearer = taken_together(value, near)
    return taken_together(nearer, far)


def in_blocks(value, dim, length):
    before, after = (value.shape[:dim], value.shape[dim + 1 :])
    return jnp.moveaxis(value.reshape(*before, length, -1, *after), dim, 0)


def summed_on_arrival(value, axis, dim):
    tiles = in_blocks(value, dim, lax.axis_size(axis))
    arrived = lax.all_to_all(tiles, axis, split_axis=0, concat_axis=0, tiled=True)
    return arrived.astype(jnp.float32).sum(axis=0)


def rows_for(lines, length):
    spare = -len(lines) % length
    return jnp.pad(lines, [(0, spare)] + [(0, 0)] * (lines.ndim - 1))


def joined_along(tiles, dim):
    tiles = jnp.moveaxis(tiles, 0, dim)
    shape = tiles.shape
    return tiles.reshape(*shape[:dim], shape[dim] * shape[dim + 1], *shape[dim + 2 :])


def collect(value, axis, dim):
    return joined_along(from_everyone(value, axis), dim)


def sum_by_parts(value, axes):
    lines = value.reshape(-1)
    own = summed_on_arrival(rows_for(lines, lax.axis_size(axes)), axes, 0)
    whole = collect(own.astype(jnp.bfloat16), axes, 0)
    return whole[: len(lines)].reshape(value.shape).astype(jnp.float32)


def level_start(height):
    return 2**LOCAL_LEVELS - 2 ** (LOCAL_LEVELS - height)


def apply_blocks(vectors, blocks):
    return jnp.einsum("snrk,snak->snra", vectors, blocks, preferred_element_type=jnp.float32)


def apply_single(vectors, blocks):
    return jnp.einsum("srk,sak->sra", vectors, blocks, preferred_element_type=jnp.float32)


def forward_local(right_sides, lower_inverse, lower_blocks, padding, far_levels, upper_levels):
    batch_size = right_sides.shape[0]
    pending = jnp.zeros((batch_size, LOCAL_COUNT, RHS, W), jnp.float32)
    upper_pending = jnp.zeros((batch_size, upper_levels, RHS, W), jnp.float32)
    solved = []
    for height in range(LOCAL_LEVELS):
        offset = level_start(height)
        amount = 2 ** (LOCAL_LEVELS - 1 - height)
        residue = (
            right_sides[:, offset : offset + amount] - pending[:, offset : offset + amount]
        ).astype(jnp.bfloat16)
        solved_now = padding[:, offset : offset + amount] * apply_blocks(
            residue, lower_inverse[:, offset : offset + amount]
        )
        solved.append(solved_now)
        rounded = solved_now.astype(jnp.bfloat16)
        for block_id in range(NB):
            product = apply_blocks(rounded, lower_blocks[:, offset : offset + amount, block_id])
            for distance in range(1, upper_levels + 1):
                if block_id == 0 and distance > 1:
                    continue
                if block_id == 0:
                    chosen = product
                else:
                    matches = far_levels[:, offset : offset + amount] == distance
                    chosen = jnp.where(matches[:, :, None, None], product, 0.0)
                target = height + distance
                if target < LOCAL_LEVELS:
                    target_count = amount // 2**distance
                    folded = chosen.reshape(batch_size, target_count, 2**distance, RHS, W).sum(
                        axis=2
                    )
                    begin_at = level_start(target)
                    pending = pending.at[:, begin_at : begin_at + target_count].add(folded)
                else:
                    upper_pending = upper_pending.at[:, target - LOCAL_LEVELS].add(
                        chosen.sum(axis=1)
                    )
    return (jnp.concatenate(solved, axis=1), upper_pending)


def backward_local(forward, upper_inverse, upper_blocks, padding, far_levels, upper_known):
    upper_levels = upper_known.shape[1]
    solutions = [None] * LOCAL_LEVELS
    for height in reversed(range(LOCAL_LEVELS)):
        offset = level_start(height)
        amount = 2 ** (LOCAL_LEVELS - 1 - height)
        residue = forward[:, offset : offset + amount]
        for block_id in range(NB):
            operand = jnp.zeros(residue.shape, jnp.float32)
            for distance in range(1, upper_levels + 1):
                if block_id == 0 and distance > 1:
                    continue
                target = height + distance
                if target < LOCAL_LEVELS:
                    known_part = jnp.repeat(solutions[target], 2**distance, axis=1)
                else:
                    known_part = jnp.broadcast_to(
                        upper_known[:, target - LOCAL_LEVELS][:, None], residue.shape
                    )
                if block_id == 0:
                    operand = known_part
                else:
                    matches = far_levels[:, offset : offset + amount] == distance
                    operand = operand + jnp.where(matches[:, :, None, None], known_part, 0.0)
            residue = residue - apply_blocks(
                operand.astype(jnp.bfloat16), upper_blocks[:, offset : offset + amount, block_id]
            )
        solutions[height] = padding[:, offset : offset + amount] * apply_blocks(
            residue.astype(jnp.bfloat16), upper_inverse[:, offset : offset + amount]
        )
    return jnp.concatenate(solutions, axis=1)


def spread_slots(partial_value, slot_count, slot_at):
    chosen = (jnp.arange(slot_count, dtype=jnp.int32) == slot_at)[:, None, None]
    return jnp.where(chosen, partial_value, 0.0)


def group_total(partial_value, height, layout, places):
    col_levels, grid_levels, col_span, grid_span, total_span = layout
    if height <= grid_levels:
        slot_at = places[1] // 2**height
        summed = one_axis_at_a_time(
            spread_slots(partial_value, grid_span // 2**height, slot_at), ROW_COL
        )
    else:
        slot_at = places[2] // 2**height
        summed = one_axis_at_a_time_2(
            spread_slots(partial_value, total_span // 2**height, slot_at),
            (("gz", "row", "col_0"), "col_1"),
        )
    return lax.dynamic_index_in_dim(summed, slot_at, 0, keepdims=True)


def owner_total(partial_value, height, layout, places, owner_level):
    col_levels, grid_levels, col_span, grid_span, total_span = layout
    if height > col_levels:
        return group_total(partial_value, height, layout, places)
    identities = jnp.arange(owner_level.shape[0], dtype=jnp.int32)
    same_group = identities // 2**height == places[2] // 2**height
    owner_id = jnp.sum(jnp.where(same_group & (owner_level == height), identities, 0))
    return summed_on_arrival(
        spread_slots(partial_value, col_span, owner_id % col_span).astype(jnp.bfloat16), COL, 0
    )


def group_share(partial_value, height, layout, places):
    col_levels, grid_levels, col_span, grid_span, total_span = layout
    if height <= col_levels:
        slot_at = places[0] // 2**height
        summed = sum_by_parts(
            spread_slots(partial_value, col_span // 2**height, slot_at).astype(jnp.bfloat16), COL
        )
    elif height <= grid_levels:
        slot_at = places[1] // 2**height
        summed = one_axis_at_a_time(
            spread_slots(partial_value, grid_span // 2**height, slot_at), ROW_COL
        )
    else:
        slot_at = places[2] // 2**height
        summed = one_axis_at_a_time_2(
            spread_slots(partial_value, total_span // 2**height, slot_at),
            (("gz", "row", "col_0"), "col_1"),
        )
    return lax.dynamic_index_in_dim(summed, slot_at, 0, keepdims=True)


def local(
    right_sides,
    lower_inverse,
    upper_inverse,
    lower_blocks,
    upper_blocks,
    node_widths,
    far_levels,
    owner_level,
):
    col_span = lax.axis_size(COL)
    row_span = lax.axis_size("row")
    layer_span = lax.axis_size("gz")
    col_levels = col_span.bit_length() - 1
    grid_levels = col_levels + row_span.bit_length() - 1
    upper_levels = grid_levels + layer_span.bit_length() - 1
    col_place = lax.axis_index(COL)
    grid_place = lax.axis_index("row") * col_span + col_place
    device = lax.axis_index("gz") * row_span * col_span + grid_place
    layout = (
        col_levels,
        grid_levels,
        col_span,
        row_span * col_span,
        layer_span * row_span * col_span,
    )
    places = (col_place, grid_place, device)
    columns = jnp.arange(W, dtype=jnp.int32)
    padding = (columns[None, None, None, :] < node_widths[:, :, None, None]).astype(jnp.float32)
    forward_nodes, upper_pending = forward_local(
        right_sides[:, :LOCAL_COUNT],
        lower_inverse[:, :LOCAL_COUNT],
        lower_blocks[:, :LOCAL_COUNT],
        padding[:, :LOCAL_COUNT],
        far_levels[:, :LOCAL_COUNT],
        upper_levels,
    )
    own_rights = right_sides[:, LOCAL_COUNT]
    own_padding = padding[:, LOCAL_COUNT]
    own_far = far_levels[:, LOCAL_COUNT]
    my_level = lax.dynamic_index_in_dim(owner_level, device, 0, keepdims=False)
    own_forward = jnp.zeros((1, RHS, W), jnp.float32)
    for height in range(1, upper_levels + 1):
        gathered = owner_total(upper_pending[:, height - 1], height, layout, places, owner_level)
        owner_here = my_level == height
        residue = (own_rights - gathered).astype(jnp.bfloat16)
        solved_now = jnp.where(
            owner_here, own_padding * apply_single(residue, lower_inverse[:, LOCAL_COUNT]), 0.0
        )
        own_forward = own_forward + solved_now
        rounded = solved_now.astype(jnp.bfloat16)
        for block_id in range(NB):
            product = apply_single(rounded, lower_blocks[:, LOCAL_COUNT, block_id])
            for distance in range(1, upper_levels + 1):
                if block_id == 0 and distance > 1:
                    continue
                target = height + distance
                if target > upper_levels:
                    continue
                if block_id == 0:
                    chosen = product
                else:
                    chosen = jnp.where((own_far == distance)[:, None, None], product, 0.0)
                upper_pending = upper_pending.at[:, target - 1].add(chosen)
    upper_known = jnp.zeros((1, upper_levels, RHS, W), jnp.float32)
    own_solution = jnp.zeros((1, RHS, W), jnp.float32)
    for height in range(upper_levels, 0, -1):
        owner_here = my_level == height
        residue = own_forward
        for block_id in range(NB):
            operand = jnp.zeros((1, RHS, W), jnp.float32)
            for distance in range(1, upper_levels + 1):
                if block_id == 0 and distance > 1:
                    continue
                target = height + distance
                if target > upper_levels:
                    continue
                known_part = upper_known[:, target - 1]
                if block_id == 0:
                    operand = known_part
                else:
                    operand = operand + jnp.where(
                        (own_far == distance)[:, None, None], known_part, 0.0
                    )
            residue = residue - apply_single(
                operand.astype(jnp.bfloat16), upper_blocks[:, LOCAL_COUNT, block_id]
            )
        solved_now = jnp.where(
            owner_here,
            own_padding * apply_single(residue.astype(jnp.bfloat16), upper_inverse[:, LOCAL_COUNT]),
            0.0,
        )
        own_solution = own_solution + solved_now
        shared = group_share(solved_now, height, layout, places)
        upper_known = upper_known.at[:, height - 1].set(shared)
    local_solution = backward_local(
        forward_nodes,
        upper_inverse[:, :LOCAL_COUNT],
        upper_blocks[:, :LOCAL_COUNT],
        padding[:, :LOCAL_COUNT],
        far_levels[:, :LOCAL_COUNT],
        upper_known,
    )
    return jnp.concatenate([local_solution, own_solution[:, None]], axis=1)


def solution(mesh):
    finer = Mesh(
        mesh.devices.reshape(mesh.shape["gz"], mesh.shape["row"], 8, 4),
        ("gz", "row", "col_0", "col_1"),
    )
    in_specs = (
        P(GZ_ROW_COL, None, None, None),
        P(GZ_ROW_COL, None, None, None),
        P(GZ_ROW_COL, None, None, None),
        P(GZ_ROW_COL, None, None, None, None),
        P(GZ_ROW_COL, None, None, None, None),
        P(GZ_ROW_COL, None),
        P(GZ_ROW_COL, None),
        P(),
    )
    out_specs = P(GZ_ROW_COL, None, None, None)
    return jax.shard_map(local, mesh=finer, in_specs=in_specs, out_specs=out_specs, check_vma=False)
```

profile of v0, /device:TPU:24, one launch (start us, length us, event | category | flops | bytes accessed | tf_op | source)
XLA Modules:
  0.0 595.2 jit_solution(13964215281555827067)
XLA Ops:
  0.0 1.5 fusion.480
  4.9 1.4 fusion.503
  6.3 1.1 convolution_multiply_fusion.1
  7.4 1.2 select_reduce_fusion.7
  8.7 1.2 convolution_multiply_fusion.19
  16.0 0.8 select_convert_fusion.4
  16.8 11.5 %all-to-all-start = ((bf16[32,1,16,256]{3,2,1,0:T(8,128)(2,1)}), bf16[32,1,16,256]{3,2,1,0:T(8,128)(2,1)S(1)}, u32[]{:S(2)}, u32[]{:S(2)}) async-start(bf16[32,1,16,256]{3,2,1,0:T(8,128)(2,1)} %select_convert_fusion.4), calls=%async_computation | async-start | bytes 524288 | tf_op jit(solution)/shard_map/all_to_all | solution.py:45
  36.8 2.7 all-to-all-done
  40.2 0.8 select_convert_fusion.3
  41.0 7.1 %all-to-all-start.1 = ((bf16[32,1,16,256]{3,2,1,0:T(8,128)(2,1)}), bf16[32,1,16,256]{3,2,1,0:T(8,128)(2,1)S(1)}, u32[]{:S(2)}, u32[]{:S(2)}) async-start(bf16[32,1,16,256]{3,2,1,0:T(8,128)(2,1)} %select_convert_fusion.3), calls=%async_computation.1 | async-start | bytes 524288 | tf_op jit(solution)/shard_map/all_to_all | solution.py:45
  50.4 8.4 %all-to-all-done.1 = bf16[32,1,16,256]{3,2,1,0:T(8,128)(2,1)S(1)} async-done(((bf16[32,1,16,256]{3,2,1,0:T(8,128)(2,1)}), bf16[32,1,16,256]{3,2,1,0:T(8,128)(2,1)S(1)}, u32[]{:S(2)}, u32[]{:S(2)}) %all-to-all-start.1) | async-done | bytes 262176 | tf_op jit(solution)/shard_map/all_to_all | solution.py:45
  59.5 0.8 select_convert_fusion.2
  60.3 5.5 all-to-all-start.2
  68.4 7.6 %all-to-all-done.2 = bf16[32,1,16,256]{3,2,1,0:T(8,128)(2,1)S(1)} async-done(((bf16[32,1,16,256]{3,2,1,0:T(8,128)(2,1)}), bf16[32,1,16,256]{3,2,1,0:T(8,128)(2,1)S(1)}, u32[]{:S(2)}, u32[]{:S(2)}) %all-to-all-start.2) | async-done | bytes 262176 | tf_op jit(solution)/shard_map/all_to_all | solution.py:45
  76.7 0.8 select_convert_fusion.1
  77.5 5.7 all-to-all-start.3
  85.7 7.5 %all-to-all-done.3 = bf16[32,1,16,256]{3,2,1,0:T(8,128)(2,1)S(1)} async-done(((bf16[32,1,16,256]{3,2,1,0:T(8,128)(2,1)}), bf16[32,1,16,256]{3,2,1,0:T(8,128)(2,1)S(1)}, u32[]{:S(2)}, u32[]{:S(2)}) %all-to-all-start.3) | async-done | bytes 262176 | tf_op jit(solution)/shard_map/all_to_all | solution.py:45
  93.8 0.8 select_convert_fusion
  94.6 5.6 all-to-all-start.4
  102.2 7.9 %all-to-all-done.4 = bf16[32,1,16,256]{3,2,1,0:T(8,128)(2,1)S(1)} async-done(((bf16[32,1,16,256]{3,2,1,0:T(8,128)(2,1)}), bf16[32,1,16,256]{3,2,1,0:T(8,128)(2,1)S(1)}, u32[]{:S(2)}, u32[]{:S(2)}) %all-to-all-start.4) | async-done | bytes 262176 | tf_op jit(solution)/shard_map/all_to_all | solution.py:45
  110.9 17.1 %psum.84 = f32[2,16,256]{2,1,0:T(8,128)S(1)} all-reduce(f32[2,16,256]{2,1,0:T(8,128)S(1)} %broadcast_select_fusion.2), channel_id=1, replica_groups=mesh['gz'=2,'row'=4,'col_0'=8,'col_1'=4] {'row'}, use_global_device_ids=true, to_apply=%region_18.19 | all-reduce | flops 8192 | bytes 65536 | tf_op jit(solution)/shard_map/psum | solution.py:19
  128.0 27.6 %psum.85 = f32[2,16,256]{2,1,0:T(8,128)S(1)} all-reduce(f32[2,16,256]{2,1,0:T(8,128)S(1)} %psum.84), channel_id=1, replica_groups=mesh['gz'=2,'row'=4,'col_0'=8,'col_1'=4] {'col_0'}, use_global_device_ids=true, to_apply=%region_19.20 | all-reduce | flops 8192 | bytes 65536 | tf_op jit(solution)/shard_map/psum | solution.py:19
  155.5 15.4 %psum.86 = f32[2,16,256]{2,1,0:T(8,128)S(1)} all-reduce(f32[2,16,256]{2,1,0:T(8,128)S(1)} %psum.85), channel_id=1, replica_groups=mesh['gz'=2,'row'=4,'col_0'=8,'col_1'=4] {'col_1'}, use_global_device_ids=true, to_apply=%region_20.21 | all-reduce | flops 8192 | bytes 65536 | tf_op jit(solution)/shard_map/psum | solution.py:19
  171.4 14.3 %psum.87 = f32[1,16,256]{2,1,0:T(8,128)S(1)} all-reduce(f32[1,16,256]{2,1,0:T(8,128)S(1)} %fusion.21), channel_id=1, replica_groups=mesh['gz'=2,'row'=4,'col_0'=8,'col_1'=4] {'row'}, use_global_device_ids=true, to_apply=%region_21.22 | all-reduce | flops 4096 | bytes 32768 | tf_op jit(solution)/shard_map/psum | solution.py:19
  185.7 27.0 %psum.88 = f32[1,16,256]{2,1,0:T(8,128)S(1)} all-reduce(f32[1,16,256]{2,1,0:T(8,128)S(1)} %psum.87), channel_id=1, replica_groups=mesh['gz'=2,'row'=4,'col_0'=8,'col_1'=4] {'col_0'}, use_global_device_ids=true, to_apply=%region_22.23 | all-reduce | flops 4096 | bytes 32768 | tf_op jit(solution)/shard_map/psum | solution.py:19
  212.8 14.5 %psum.89 = f32[1,16,256]{2,1,0:T(8,128)S(1)} all-reduce(f32[1,16,256]{2,1,0:T(8,128)S(1)} %psum.88), channel_id=1, replica_groups=mesh['gz'=2,'row'=4,'col_0'=8,'col_1'=4] {'col_1'}, use_global_device_ids=true, to_apply=%region_23.24 | all-reduce | flops 4096 | bytes 32768 | tf_op jit(solution)/shard_map/psum | solution.py:19
  227.8 8.8 %all_to_all.109 = f32[4,1,16,256]{3,2,1,0:T(8,128)S(1)} all-to-all(f32[4,1,16,256]{3,2,1,0:T(8,128)S(1)} %broadcast_in_dim.990), channel_id=1, replica_groups=mesh['gz'=2,'row'=4,'col_0'=8,'col_1'=4] {'col_1'}, dimensions={0} | all-to-all | bytes 131072 | tf_op jit(solution)/shard_map/all_to_all | solution.py:25
  236.6 1.1 broadcast_in_dim.991
  237.7 6.1 %all-to-all-start.6 = ((f32[64,1,16,256]{3,2,1,0:T(8,128)}), f32[64,1,16,256]{3,2,1,0:T(8,128)S(1)}, u32[]{:S(2)}, u32[]{:S(2)}) async-start(f32[64,1,16,256]{3,2,1,0:T(8,128)} %broadcast_in_dim.991), calls=%async_computation.6 | async-start | bytes 2097152 | tf_op jit(solution)/shard_map/all_to_all | solution.py:25
  244.6 29.5 %all-to-all-done.6 = f32[64,1,16,256]{3,2,1,0:T(8,128)S(1)} async-done(((f32[64,1,16,256]{3,2,1,0:T(8,128)}), f32[64,1,16,256]{3,2,1,0:T(8,128)S(1)}, u32[]{:S(2)}, u32[]{:S(2)}) %all-to-all-start.6) | async-done | bytes 1048608 | tf_op jit(solution)/shard_map/all_to_all | solution.py:25
  274.9 8.0 %all_to_all.110 = f32[4,1,16,256]{3,2,1,0:T(8,128)S(1)} all-to-all(f32[4,1,16,256]{3,2,1,0:T(8,128)S(1)} %broadcast_in_dim.1000), channel_id=1, replica_groups=mesh['gz'=2,'row'=4,'col_0'=8,'col_1'=4] {'col_1'}, dimensions={0} | all-to-all | bytes 131072 | tf_op jit(solution)/shard_map/all_to_all | solution.py:25
  282.9 1.1 broadcast_in_dim.1001
  284.0 4.7 all-to-all-start.8
  288.7 30.3 %all-to-all-done.8 = f32[64,1,16,256]{3,2,1,0:T(8,128)S(1)} async-done(((f32[64,1,16,256]{3,2,1,0:T(8,128)}), f32[64,1,16,256]{3,2,1,0:T(8,128)S(1)}, u32[]{:S(2)}, u32[]{:S(2)}) %all-to-all-start.8) | async-done | bytes 1048608 | tf_op jit(solution)/shard_map/all_to_all | solution.py:25
  319.5 14.8 %psum.90 = f32[1,16,256]{2,1,0:T(8,128)S(1)} all-reduce(f32[1,16,256]{2,1,0:T(8,128)S(1)} %select_bitcast_fusion), channel_id=1, replica_groups=mesh['gz'=2,'row'=4,'col_0'=8,'col_1'=4] {'row'}, use_global_device_ids=true, to_apply=%region_28.29 | all-reduce | flops 4096 | bytes 32768 | tf_op jit(solution)/shard_map/psum | solution.py:19
  334.3 28.9 %psum.91 = f32[1,16,256]{2,1,0:T(8,128)S(1)} all-reduce(f32[1,16,256]{2,1,0:T(8,128)S(1)} %psum.90), channel_id=1, replica_groups=mesh['gz'=2,'row'=4,'col_0'=8,'col_1'=4] {'col_0'}, use_global_device_ids=true, to_apply=%region_29.30 | all-reduce | flops 4096 | bytes 32768 | tf_op jit(solution)/shard_map/psum | solution.py:19
  363.1 14.4 %psum.92 = f32[1,16,256]{2,1,0:T(8,128)S(1)} all-reduce(f32[1,16,256]{2,1,0:T(8,128)S(1)} %psum.91), channel_id=1, replica_groups=mesh['gz'=2,'row'=4,'col_0'=8,'col_1'=4] {'col_1'}, use_global_device_ids=true, to_apply=%region_30.31 | all-reduce | flops 4096 | bytes 32768 | tf_op jit(solution)/shard_map/psum | solution.py:19
  378.1 14.8 %psum.93 = f32[2,16,256]{2,1,0:T(8,128)S(1)} all-reduce(f32[2,16,256]{2,1,0:T(8,128)S(1)} %broadcast_select_fusion.1), channel_id=1, replica_groups=mesh['gz'=2,'row'=4,'col_0'=8,'col_1'=4] {'row'}, use_global_device_ids=true, to_apply=%region_31.32 | all-reduce | flops 8192 | bytes 65536 | tf_op jit(solution)/shard_map/psum | solution.py:19
  392.9 27.1 %psum.94 = f32[2,16,256]{2,1,0:T(8,128)S(1)} all-reduce(f32[2,16,256]{2,1,0:T(8,128)S(1)} %psum.93), channel_id=1, replica_groups=mesh['gz'=2,'row'=4,'col_0'=8,'col_1'=4] {'col_0'}, use_global_device_ids=true, to_apply=%region_32.33 | all-reduce | flops 8192 | bytes 65536 | tf_op jit(solution)/shard_map/psum | solution.py:19
  420.0 16.1 %psum.95 = f32[2,16,256]{2,1,0:T(8,128)S(1)} all-reduce(f32[2,16,256]{2,1,0:T(8,128)S(1)} %psum.94), channel_id=1, replica_groups=mesh['gz'=2,'row'=4,'col_0'=8,'col_1'=4] {'col_1'}, use_global_device_ids=true, to_apply=%region_33.34 | all-reduce | flops 8192 | bytes 65536 | tf_op jit(solution)/shard_map/psum | solution.py:19
  437.2 6.5 %all-to-all-start.9 = ((bf16[32,1,128]{2,1,0:T(2,128)(2,1)}), bf16[32,1,128]{2,1,0:T(2,128)(2,1)S(1)}, u32[]{:S(2)}, u32[]{:S(2)}) async-start(bf16[32,1,128]{2,1,0:T(2,128)(2,1)} %all_to_all.89), calls=%async_computation.9 | async-start | bytes 32768 | tf_op jit(solution)/shard_map/all_to_all | solution.py:45
  443.7 7.9 %all-to-all-done.9 = bf16[32,1,128]{2,1,0:T(2,128)(2,1)S(1)} async-done(((bf16[32,1,128]{2,1,0:T(2,128)(2,1)}), bf16[32,1,128]{2,1,0:T(2,128)(2,1)S(1)}, u32[]{:S(2)}, u32[]{:S(2)}) %all-to-all-start.9) | async-done | bytes 8224 | tf_op jit(solution)/shard_map/all_to_all | solution.py:45
  452.3 5.7 all-to-all-start.10
  458.2 7.8 %all-to-all-done.10 = bf16[32,1,128]{2,1,0:T(2,128)(2,1)S(1)} async-done(((bf16[32,1,128]{2,1,0:T(2,128)(2,1)}), bf16[32,1,128]{2,1,0:T(2,128)(2,1)S(1)}, u32[]{:S(2)}, u32[]{:S(2)}) %all-to-all-start.10) | async-done | bytes 8224 | tf_op jit(solution)/shard_map/all_to_all | solution.py:25
  468.5 5.5 all-to-all-start.11
  474.0 8.0 %all-to-all-done.11 = bf16[32,2,128]{2,1,0:T(2,128)(2,1)S(1)} async-done(((bf16[32,2,128]{2,1,0:T(2,128)(2,1)}), bf16[32,2,128]{2,1,0:T(2,128)(2,1)S(1)}, u32[]{:S(2)}, u32[]{:S(2)}) %all-to-all-start.11) | async-done | bytes 16416 | tf_op jit(solution)/shard_map/all_to_all | solution.py:45
  483.4 5.5 all-to-all-start.12
  488.9 8.0 %all-to-all-done.12 = bf16[32,2,128]{2,1,0:T(2,128)(2,1)S(1)} async-done(((bf16[32,2,128]{2,1,0:T(2,128)(2,1)}), bf16[32,2,128]{2,1,0:T(2,128)(2,1)S(1)}, u32[]{:S(2)}, u32[]{:S(2)}) %all-to-all-start.12) | async-done | bytes 16416 | tf_op jit(solution)/shard_map/all_to_all | solution.py:25
  497.5 0.7 reduce.173
  498.9 5.5 all-to-all-start.13
  504.4 8.2 %all-to-all-done.13 = bf16[32,2,256]{2,1,0:T(2,128)(2,1)S(1)} async-done(((bf16[32,2,256]{2,1,0:T(2,128)(2,1)}), bf16[32,2,256]{2,1,0:T(2,128)(2,1)S(1)}, u32[]{:S(2)}, u32[]{:S(2)}) %all-to-all-start.13) | async-done | bytes 32800 | tf_op jit(solution)/shard_map/all_to_all | solution.py:45
  514.2 5.4 all-to-all-start.14
  519.6 8.2 %all-to-all-done.14 = bf16[32,2,256]{2,1,0:T(2,128)(2,1)S(1)} async-done(((bf16[32,2,256]{2,1,0:T(2,128)(2,1)}), bf16[32,2,256]{2,1,0:T(2,128)(2,1)S(1)}, u32[]{:S(2)}, u32[]{:S(2)}) %all-to-all-start.14) | async-done | bytes 32800 | tf_op jit(solution)/shard_map/all_to_all | solution.py:25
  528.7 0.9 reduce.175
  529.6 13.0 %all_to_all.111 = bf16[32,2,512]{2,1,0:T(2,128)(2,1)S(1)} all-to-all(bf16[32,2,512]{2,1,0:T(2,128)(2,1)S(1)} %reshape.3590), channel_id=1, replica_groups=mesh['gz'=2,'row'=4,'col_0'=8,'col_1'=4] {'col_0','col_1'}, dimensions={0} | all-to-all | bytes 131072 | tf_op jit(solution)/shard_map/all_to_all | solution.py:45
  542.9 0.9 reduce.176
  544.5 5.3 all-to-all-start.16
  549.8 8.4 %all-to-all-done.16 = bf16[32,2,512]{2,1,0:T(2,128)(2,1)S(1)} async-done(((bf16[32,2,512]{2,1,0:T(2,128)(2,1)}), bf16[32,2,512]{2,1,0:T(2,128)(2,1)S(1)}, u32[]{:S(2)}, u32[]{:S(2)}) %all-to-all-start.16) | async-done | bytes 65568 | tf_op jit(solution)/shard_map/all_to_all | solution.py:25
  559.4 1.3 reduce.177
  561.4 5.4 all-to-all-start.17
  566.8 8.9 %all-to-all-done.17 = bf16[32,2,1024]{2,1,0:T(2,128)(2,1)S(1)} async-done(((bf16[32,2,1024]{2,1,0:T(2,128)(2,1)}), bf16[32,2,1024]{2,1,0:T(2,128)(2,1)S(1)}, u32[]{:S(2)}, u32[]{:S(2)}) %all-to-all-start.17) | async-done | bytes 131104 | tf_op jit(solution)/shard_map/all_to_all | solution.py:45
  576.2 1.3 reduce.178
  578.2 5.5 all-to-all-start.18
  583.8 8.9 %all-to-all-done.18 = bf16[32,2,1024]{2,1,0:T(2,128)(2,1)S(1)} async-done(((bf16[32,2,1024]{2,1,0:T(2,128)(2,1)}), bf16[32,2,1024]{2,1,0:T(2,128)(2,1)S(1)}, u32[]{:S(2)}, u32[]{:S(2)}) %all-to-all-start.18) | async-done | bytes 131104 | tf_op jit(solution)/shard_map/all_to_all | solution.py:25
  (194 shorter events, 25.2 us)
Async XLA Ops:
  0.0 6.3 %copy-start.4 = (f32[1,4,16,256]{3,2,1,0:T(8,128)S(1)}, f32[1,4,16,256]{3,2,1,0:T(8,128)}, u32[]{:S(2)}) copy-start(f32[1,4,16,256]{3,2,1,0:T(8,128)} %param.130) | copy-start | bytes 196612
  0.0 8.7 %copy-start.1 = (bf16[1,4,2,256,256]{4,3,2,1,0:T(8,128)(2,1)S(1)}, bf16[1,4,2,256,256]{4,3,2,1,0:T(8,128)(2,1)}, u32[]{:S(2)}) copy-start(bf16[1,4,2,256,256]{4,3,2,1,0:T(8,128)(2,1)} %param.133) | copy-start | bytes 3145732
  16.0 23.6 %copy-start.2 = (bf16[1,4,256,256]{3,2,1,0:T(8,128)(2,1)S(1)}, bf16[1,4,256,256]{3,2,1,0:T(8,128)(2,1)}, u32[]{:S(2)}) copy-start(bf16[1,4,256,256]{3,2,1,0:T(8,128)(2,1)} %param.131) | copy-start | bytes 1572868
  16.8 22.7 %all-to-all-start = ((bf16[32,1,16,256]{3,2,1,0:T(8,128)(2,1)}), bf16[32,1,16,256]{3,2,1,0:T(8,128)(2,1)S(1)}, u32[]{:S(2)}, u32[]{:S(2)}) async-start(bf16[32,1,16,256]{3,2,1,0:T(8,128)(2,1)} %select_convert_fusion.4), calls=%async_computation | async-start | bytes 524288 | tf_op jit(solution)/shard_map/all_to_all | solution.py:45
  34.9 0.7 copy-start.5
  41.0 17.8 %all-to-all-start.1 = ((bf16[32,1,16,256]{3,2,1,0:T(8,128)(2,1)}), bf16[32,1,16,256]{3,2,1,0:T(8,128)(2,1)S(1)}, u32[]{:S(2)}, u32[]{:S(2)}) async-start(bf16[32,1,16,256]{3,2,1,0:T(8,128)(2,1)} %select_convert_fusion.3), calls=%async_computation.1 | async-start | bytes 524288 | tf_op jit(solution)/shard_map/all_to_all | solution.py:45
  60.3 15.7 %all-to-all-start.2 = ((bf16[32,1,16,256]{3,2,1,0:T(8,128)(2,1)}), bf16[32,1,16,256]{3,2,1,0:T(8,128)(2,1)S(1)}, u32[]{:S(2)}, u32[]{:S(2)}) async-start(bf16[32,1,16,256]{3,2,1,0:T(8,128)(2,1)} %select_convert_fusion.2), calls=%async_computation.2 | async-start | bytes 524288 | tf_op jit(solution)/shard_map/all_to_all | solution.py:45
  77.5 15.7 %all-to-all-start.3 = ((bf16[32,1,16,256]{3,2,1,0:T(8,128)(2,1)}), bf16[32,1,16,256]{3,2,1,0:T(8,128)(2,1)S(1)}, u32[]{:S(2)}, u32[]{:S(2)}) async-start(bf16[32,1,16,256]{3,2,1,0:T(8,128)(2,1)} %select_convert_fusion.1), calls=%async_computation.3 | async-start | bytes 524288 | tf_op jit(solution)/shard_map/all_to_all | solution.py:45
  94.6 15.5 %all-to-all-start.4 = ((bf16[32,1,16,256]{3,2,1,0:T(8,128)(2,1)}), bf16[32,1,16,256]{3,2,1,0:T(8,128)(2,1)S(1)}, u32[]{:S(2)}, u32[]{:S(2)}) async-start(bf16[32,1,16,256]{3,2,1,0:T(8,128)(2,1)} %select_convert_fusion), calls=%async_computation.4 | async-start | bytes 524288 | tf_op jit(solution)/shard_map/all_to_all | solution.py:45
  237.7 36.8 %copy-start.3 = (bf16[1,4,256,256]{3,2,1,0:T(8,128)(2,1)S(1)}, bf16[1,4,256,256]{3,2,1,0:T(8,128)(2,1)}, u32[]{:S(2)}) copy-start(bf16[1,4,256,256]{3,2,1,0:T(8,128)(2,1)} %param.132) | copy-start | bytes 1572868
  237.7 36.3 %all-to-all-start.6 = ((f32[64,1,16,256]{3,2,1,0:T(8,128)}), f32[64,1,16,256]{3,2,1,0:T(8,128)S(1)}, u32[]{:S(2)}, u32[]{:S(2)}) async-start(f32[64,1,16,256]{3,2,1,0:T(8,128)} %broadcast_in_dim.991), calls=%async_computation.6 | async-start | bytes 2097152 | tf_op jit(solution)/shard_map/all_to_all | solution.py:25
  243.8 30.5 %copy-start = (bf16[1,4,2,256,256]{4,3,2,1,0:T(8,128)(2,1)S(1)}, bf16[1,4,2,256,256]{4,3,2,1,0:T(8,128)(2,1)}, u32[]{:S(2)}) copy-start(bf16[1,4,2,256,256]{4,3,2,1,0:T(8,128)(2,1)} %param.134) | copy-start | bytes 3145732
  284.0 34.9 %all-to-all-start.8 = ((f32[64,1,16,256]{3,2,1,0:T(8,128)}), f32[64,1,16,256]{3,2,1,0:T(8,128)S(1)}, u32[]{:S(2)}, u32[]{:S(2)}) async-start(f32[64,1,16,256]{3,2,1,0:T(8,128)} %broadcast_in_dim.1001), calls=%async_computation.8 | async-start | bytes 2097152 | tf_op jit(solution)/shard_map/all_to_all | solution.py:25
  437.2 14.4 %all-to-all-start.9 = ((bf16[32,1,128]{2,1,0:T(2,128)(2,1)}), bf16[32,1,128]{2,1,0:T(2,128)(2,1)S(1)}, u32[]{:S(2)}, u32[]{:S(2)}) async-start(bf16[32,1,128]{2,1,0:T(2,128)(2,1)} %all_to_all.89), calls=%async_computation.9 | async-start | bytes 32768 | tf_op jit(solution)/shard_map/all_to_all | solution.py:45
  452.3 13.7 %all-to-all-start.10 = ((bf16[32,1,128]{2,1,0:T(2,128)(2,1)}), bf16[32,1,128]{2,1,0:T(2,128)(2,1)S(1)}, u32[]{:S(2)}, u32[]{:S(2)}) async-start(bf16[32,1,128]{2,1,0:T(2,128)(2,1)} %broadcast_in_dim.1006), calls=%async_computation.10 | async-start | bytes 32768 | tf_op jit(solution)/shard_map/all_to_all | solution.py:25
  468.5 13.5 %all-to-all-start.11 = ((bf16[32,2,128]{2,1,0:T(2,128)(2,1)}), bf16[32,2,128]{2,1,0:T(2,128)(2,1)S(1)}, u32[]{:S(2)}, u32[]{:S(2)}) async-start(bf16[32,2,128]{2,1,0:T(2,128)(2,1)} %reshape.3582), calls=%async_computation.11 | async-start | bytes 32768 | tf_op jit(solution)/shard_map/all_to_all | solution.py:45
  483.4 13.5 %all-to-all-start.12 = ((bf16[32,2,128]{2,1,0:T(2,128)(2,1)}), bf16[32,2,128]{2,1,0:T(2,128)(2,1)S(1)}, u32[]{:S(2)}, u32[]{:S(2)}) async-start(bf16[32,2,128]{2,1,0:T(2,128)(2,1)} %reshape.3584), calls=%async_computation.12 | async-start | bytes 32768 | tf_op jit(solution)/shard_map/all_to_all | solution.py:25
  498.9 13.8 %all-to-all-start.13 = ((bf16[32,2,256]{2,1,0:T(2,128)(2,1)}), bf16[32,2,256]{2,1,0:T(2,128)(2,1)S(1)}, u32[]{:S(2)}, u32[]{:S(2)}) async-start(bf16[32,2,256]{2,1,0:T(2,128)(2,1)} %reshape.3586), calls=%async_computation.13 | async-start | bytes 65536 | tf_op jit(solution)/shard_map/all_to_all | solution.py:45
  514.2 13.6 %all-to-all-start.14 = ((bf16[32,2,256]{2,1,0:T(2,128)(2,1)}), bf16[32,2,256]{2,1,0:T(2,128)(2,1)S(1)}, u32[]{:S(2)}, u32[]{:S(2)}) async-start(bf16[32,2,256]{2,1,0:T(2,128)(2,1)} %reshape.3588), calls=%async_computation.14 | async-start | bytes 65536 | tf_op jit(solution)/shard_map/all_to_all | solution.py:25
  544.5 13.8 %all-to-all-start.16 = ((bf16[32,2,512]{2,1,0:T(2,128)(2,1)}), bf16[32,2,512]{2,1,0:T(2,128)(2,1)S(1)}, u32[]{:S(2)}, u32[]{:S(2)}) async-start(bf16[32,2,512]{2,1,0:T(2,128)(2,1)} %reshape.3592), calls=%async_computation.16 | async-start | bytes 131072 | tf_op jit(solution)/shard_map/all_to_all | solution.py:25
  561.4 14.4 %all-to-all-start.17 = ((bf16[32,2,1024]{2,1,0:T(2,128)(2,1)}), bf16[32,2,1024]{2,1,0:T(2,128)(2,1)S(1)}, u32[]{:S(2)}, u32[]{:S(2)}) async-start(bf16[32,2,1024]{2,1,0:T(2,128)(2,1)} %reshape.3594), calls=%async_computation.17 | async-start | bytes 262144 | tf_op jit(solution)/shard_map/all_to_all | solution.py:45
  578.2 14.4 %all-to-all-start.18 = ((bf16[32,2,1024]{2,1,0:T(2,128)(2,1)}), bf16[32,2,1024]{2,1,0:T(2,128)(2,1)S(1)}, u32[]{:S(2)}, u32[]{:S(2)}) async-start(bf16[32,2,1024]{2,1,0:T(2,128)(2,1)} %reshape.3596), calls=%async_computation.18 | async-start | bytes 262144 | tf_op jit(solution)/shard_map/all_to_all | solution.py:25
where the time goes:
time: 598 us; the launch traced here: 595 us
  blocking collectives  262 us (44%)
  waiting for transfers between devices  168 us (28%)
  starting transfers between devices  96.5 us (16%)
  between operations  26 us (4%)
  other arithmetic  17.9 us (3%)
  local copies, waits for them, and re-layouts  12.6 us (2%)
  matrix products  12.5 us (2%)
    psum x12, blocking collectives, one_axis_at_a_time(): value = lax.psum(value, axis)  232 us
    all_to_all x7, waiting for transfers between devices, from_everyone(): return lax.all_to_all(copies, axis, split_axis=0, concat_axis=0, tiled=True)  101 us
    all_to_all x9, waiting for transfers between devices, summed_on_arrival(): lax.all_to_all(tiles, axis, split_axis=0, concat_axis=0, tiled=True)  67 us
    all_to_all x9, starting transfers between devices, summed_on_arrival(): lax.all_to_all(tiles, axis, split_axis=0, concat_axis=0, tiled=True)  58.4 us
    all_to_all x7, starting transfers between devices, from_everyone(): return lax.all_to_all(copies, axis, split_axis=0, concat_axis=0, tiled=True)  38.1 us
    all_to_all x2, blocking collectives, from_everyone(): return lax.all_to_all(copies, axis, split_axis=0, concat_axis=0, tiled=True)  16.8 us
    all_to_all x1, blocking collectives, summed_on_arrival(): lax.all_to_all(tiles, axis, split_axis=0, concat_axis=0, tiled=True)  13 us
  transfers between devices with their start and end apart: 16, of which 16 were waited for; matrix products, arithmetic and copies ran while one was open for 0% of the time, Pallas kernels for 0%

commit v1 on v0

v1 whole, which is shorter than its diff:
```python
import functools

import jax
import jax.numpy as jnp
from jax import lax
from jax.experimental import pallas as pl
from jax.experimental.pallas import tpu as pltpu
from jax.sharding import Mesh
from jax.sharding import PartitionSpec as P

W = 256
RHS = 16
LOCAL_COUNT = 3
UPPER = 8
LOW = 2
DEVICES = 256
AXES = ("gz", "row", "col")
BF16 = jnp.bfloat16
F32 = jnp.float32
META = 16
VMEM = pl.BlockSpec(memory_space=pltpu.VMEM)
SMEM = pl.BlockSpec(memory_space=pltpu.SMEM)
PARAMS = pltpu.CompilerParams(vmem_limit_bytes=32 * 1024 * 1024)


def in_column(t):
    return (t % 4) == (0 if t < DEVICES // 2 else 2)


def partner(t, level):
    other = t ^ (1 << (level - 1))
    return other ^ 2 if level == UPPER else other


def exchange(value, level):
    pairs = [
        (t, partner(t, level)) for t in range(DEVICES) if level <= LOW or in_column(t)
    ]
    return lax.ppermute(value, AXES, pairs)


def over_y(value):
    total = None
    for step in (1, 2, 3):
        pairs = [
            (t, t - t % 4 + (t % 4 + step) % 4) for t in range(DEVICES) if in_column(t)
        ]
        came = lax.ppermute(value, AXES, pairs)
        total = came if total is None else total + came
    return total


def times(vectors, blocks):
    return jnp.dot(vectors, blocks, preferred_element_type=F32)


def times_rows(vectors, blocks):
    return lax.dot_general(
        vectors, blocks, (((1,), (1,)), ((), ())), preferred_element_type=F32
    )


def column_pad(width):
    return lax.broadcasted_iota(jnp.int32, (W, 1), 0) < width


def row_pad(width):
    return lax.broadcasted_iota(jnp.int32, (1, W), 1) < width


def combine_kernel(widths, far, linv, uinv, lblk, ublk, low, up):
    pad = column_pad(widths[0, LOCAL_COUNT])
    distance = jnp.full((META, W), far[0, LOCAL_COUNT], jnp.int32).astype(F32).astype(BF16)
    lower = jnp.where(pad, linv[0, 0], 0)
    upper = jnp.where(pad, uinv[0, 0], 0)
    for block in range(2):
        low[block * W : (block + 1) * W] = times(lblk[0, 0, block], lower).T.astype(BF16)
        up[block * W : (block + 1) * W] = times(upper, ublk[0, 0, block]).T.astype(BF16)
    up[2 * W : 3 * W] = times(upper, lower).T.astype(BF16)
    low[2 * W :] = distance
    up[3 * W :] = distance


def combine(widths, far, linv, uinv, lblk, ublk):
    slot = pl.BlockSpec((1, 1, W, W), lambda i: (0, LOCAL_COUNT, 0, 0))
    pair = pl.BlockSpec((1, 1, 2, W, W), lambda i: (0, LOCAL_COUNT, 0, 0, 0))
    return pl.pallas_call(
        combine_kernel,
        grid=(1,),
        in_specs=[SMEM, SMEM, slot, slot, pair, pair],
        out_specs=[
            pl.BlockSpec((2 * W + META, W), lambda i: (0, 0)),
            pl.BlockSpec((3 * W + META, W), lambda i: (0, 0)),
        ],
        out_shape=[
            jax.ShapeDtypeStruct((2 * W + META, W), BF16),
            jax.ShapeDtypeStruct((3 * W + META, W), BF16),
        ],
        compiler_params=PARAMS,
    )(widths, far, linv, uinv, lblk, ublk)


def leaves_kernel(widths, far, level, rights, linv, lblk, solved, sums, halves):
    own = rights[0, LOCAL_COUNT]
    for v in range(1, UPPER + 1):
        sums[(v - 1) * RHS : v * RHS] = jnp.where(level[0] == v, own, 0.0)
    pending = jnp.zeros((RHS, W), F32)
    for slot in range(LOCAL_COUNT):
        residue = rights[0, slot]
        if slot == LOCAL_COUNT - 1:
            residue = residue - pending
        forward = jnp.where(
            row_pad(widths[0, slot]), times_rows(residue.astype(BF16), linv[0, slot]), 0.0
        )
        solved[slot] = forward
        half = forward.astype(BF16)
        near = times_rows(half, lblk[0, slot, 0])
        away = times_rows(half, lblk[0, slot, 1])
        if slot == LOCAL_COUNT - 1:
            sums[:RHS] = sums[:RHS] - near
            target = far[0, slot]
        else:
            pending = pending + near
            target = far[0, slot] - 1
        for v in range(1, UPPER + 1):
            rows = slice((v - 1) * RHS, v * RHS)
            sums[rows] = sums[rows] - jnp.where(target == v, away, 0.0)
    halves[...] = sums[...].astype(BF16)


def leaves(widths, far, level, rights, linv, lblk):
    return pl.pallas_call(
        leaves_kernel,
        grid=(1,),
        in_specs=[
            SMEM,
            SMEM,
            SMEM,
            pl.BlockSpec((1, 4, RHS, W), lambda i: (0, 0, 0, 0)),
            pl.BlockSpec((1, LOCAL_COUNT, W, W), lambda i: (0, 0, 0, 0)),
            pl.BlockSpec((1, LOCAL_COUNT, 2, W, W), lambda i: (0, 0, 0, 0, 0)),
        ],
        out_specs=[
            pl.BlockSpec((LOCAL_COUNT, RHS, W), lambda i: (0, 0, 0)),
            pl.BlockSpec((UPPER * RHS, W), lambda i: (0, 0)),
            pl.BlockSpec((UPPER * RHS, W), lambda i: (0, 0)),
        ],
        out_shape=[
            jax.ShapeDtypeStruct((LOCAL_COUNT, RHS, W), F32),
            jax.ShapeDtypeStruct((UPPER * RHS, W), F32),
            jax.ShapeDtypeStruct((UPPER * RHS, W), BF16),
        ],
        compiler_params=PARAMS,
    )(widths, far, level, rights, linv, lblk)


def climb_kernel(count, sums, came, low, residue, rest, halves):
    total = sums[...] + came[...].astype(F32)
    half = total[:RHS].astype(BF16)
    residue[...] = half
    near = times(half, low[:W])
    away = times(half, low[W : 2 * W])
    distance = low[2 * W : 2 * W + 1].astype(F32)
    for step in range(1, count):
        value = total[step * RHS : (step + 1) * RHS]
        if step == 1:
            value = value - near
        value = value - jnp.where(distance == float(step), away, 0.0)
        rest[(step - 1) * RHS : step * RHS] = value
        halves[(step - 1) * RHS : step * RHS] = value.astype(BF16)


def climb(sums, came, low):
    count = sums.shape[0] // RHS
    rows = (count - 1) * RHS
    return pl.pallas_call(
        functools.partial(climb_kernel, count),
        in_specs=[VMEM] * 3,
        out_specs=[VMEM] * 3,
        out_shape=[
            jax.ShapeDtypeStruct((RHS, W), BF16),
            jax.ShapeDtypeStruct((rows, W), F32),
            jax.ShapeDtypeStruct((rows, W), BF16),
        ],
        compiler_params=PARAMS,
    )(sums, came, low)


def separator(residue, up, above):
    value = times(residue, up[2 * W : 3 * W])
    if not above:
        return value
    distance = up[3 * W : 3 * W + 1].astype(F32)
    known = jnp.zeros((RHS, W), F32)
    for step, part in enumerate(above, 1):
        known = known + jnp.where(distance == float(step), part.astype(F32), 0.0)
    return value - times(above[0], up[:W]) - times(known.astype(BF16), up[W : 2 * W])


def top_kernel(*refs):
    amount = UPPER - LOW
    residues, ups, out = (refs[:amount], refs[amount : 2 * amount], refs[2 * amount])
    above = []
    for v in range(UPPER, LOW, -1):
        value = separator(residues[v - LOW - 1][...], ups[v - LOW - 1], above).astype(BF16)
        out[(v - LOW - 1) * RHS : (v - LOW) * RHS] = value
        above = [value] + above


def top(residues, ups):
    return pl.pallas_call(
        top_kernel,
        in_specs=[VMEM] * (2 * (UPPER - LOW)),
        out_specs=VMEM,
        out_shape=jax.ShapeDtypeStruct(((UPPER - LOW) * RHS, W), BF16),
        compiler_params=PARAMS,
    )(*residues, *ups)


def descend_kernel(widths, far, level, solved, known, r1, r2, u1, u2, uinv, ublk, out):
    above = [known[k * RHS : (k + 1) * RHS] for k in range(UPPER - LOW)]
    own = jnp.zeros((RHS, W), F32)
    for k, part in enumerate(above):
        own = jnp.where(level[0] == k + LOW + 1, part.astype(F32), own)
    for v, residue, up in ((2, r2, u2), (1, r1, u1)):
        value = separator(residue[...], up, above)
        own = jnp.where(level[0] == v, value, own)
        above = [value.astype(BF16)] + above
    out[0, LOCAL_COUNT] = own
    for slot in (2, 1, 0):
        distant = jnp.zeros((RHS, W), F32)
        for step, part in enumerate(above, 1):
            distant = distant + jnp.where(far[0, slot] == step, part.astype(F32), 0.0)
        residue = (
            solved[slot]
            - times_rows(above[0], ublk[0, slot, 0])
            - times_rows(distant.astype(BF16), ublk[0, slot, 1])
        )
        value = jnp.where(
            row_pad(widths[0, slot]), times_rows(residue.astype(BF16), uinv[0, slot]), 0.0
        )
        out[0, slot] = value
        if slot == 2:
            above = [value.astype(BF16)] + above


def descend(widths, far, level, solved, known, r1, r2, u1, u2, uinv, ublk):
    def whole(array):
        return pl.BlockSpec(array.shape, lambda i: (0,) * array.ndim)

    return pl.pallas_call(
        descend_kernel,
        grid=(1,),
        in_specs=[
            SMEM,
            SMEM,
            SMEM,
            whole(solved),
            whole(known),
            whole(r1),
            whole(r2),
            whole(u1),
            whole(u2),
            pl.BlockSpec((1, LOCAL_COUNT, W, W), lambda i: (0, 0, 0, 0)),
            pl.BlockSpec((1, LOCAL_COUNT, 2, W, W), lambda i: (0, 0, 0, 0, 0)),
        ],
        out_specs=pl.BlockSpec((1, 4, RHS, W), lambda i: (0, 0, 0, 0)),
        out_shape=jax.ShapeDtypeStruct((1, 4, RHS, W), F32),
        compiler_params=PARAMS,
    )(widths, far, level, solved, known, r1, r2, u1, u2, uinv, ublk)


def local(rights, linv, uinv, lblk, ublk, widths, far, owner_level):
    device = (
        lax.axis_index("gz") * lax.axis_size("row") + lax.axis_index("row")
    ) * lax.axis_size("col") + lax.axis_index("col")
    everyone = jnp.arange(DEVICES, dtype=jnp.int32)
    level = jnp.sum(jnp.where(everyone == device, owner_level, 0)).reshape(1)
    heights = jnp.arange(1, UPPER + 1, dtype=jnp.int32)[:, None]
    same_half = (everyone[None, :] >> (heights - 1)) == (device >> (heights - 1))
    here = jnp.any(same_half & (owner_level[None, :] == heights), axis=1)
    low, up = combine(widths, far, linv, uinv, lblk, ublk)
    solved, sums, halves = leaves(widths, far, level, rights, linv, lblk)
    residues = []
    ups = []
    for v in range(1, UPPER + 1):
        mine = here[v - 1]
        came = exchange(halves, v)
        if v < UPPER:
            low_came = exchange(low, v)
            low_here = jnp.where(mine, low, low_came)
            low = jnp.where(mine, low_came, low)
        up_came = exchange(up, v)
        ups.append(jnp.where(mine, up, up_came))
        up = jnp.where(mine, up_came, up)
        if v < UPPER:
            residue, sums, halves = climb(sums, came, low_here)
        else:
            residue = (sums + came.astype(F32)).astype(BF16)
        residues.append(residue)
    known = top(residues[LOW:], ups[LOW:])
    shared = over_y(known)
    y = device % 4
    column = jnp.where(device < DEVICES // 2, y == 0, y == 2)
    known = jnp.where(column, known, shared)
    return descend(
        widths, far, level, solved, known, residues[0], residues[1], ups[0], ups[1], uinv, ublk
    )


def solution(mesh):
    split = P(AXES)
    in_specs = (split,) * 7 + (P(),)
    return jax.shard_map(local, mesh=mesh, in_specs=in_specs, out_specs=split, check_vma=False)
```

time: 598 us -> 162 us (0.27)
  the two profiles are of different devices: /device:TPU:24 before, /device:TPU:1 now
where the time goes in v1:
time: 162 us; the launch traced here: 161 us
  waiting for transfers between devices  75.9 us (47%)
  starting transfers between devices  58.5 us (36%)
  other arithmetic  11 us (7%)
  local copies, waits for them, and re-layouts  7.89 us (5%)
  Pallas kernels  7.35 us (5%)
    ppermute x23, starting transfers between devices, exchange(): return lax.ppermute(value, AXES, pairs)  55.9 us
    ppermute x3, waiting for transfers between devices, over_y(): came = lax.ppermute(value, AXES, pairs)  53.5 us
    ppermute x23, waiting for transfers between devices, exchange(): return lax.ppermute(value, AXES, pairs)  22.4 us
    unnamed x28, local copies, waits for them, and re-layouts  7.2 us
    select_n x6, other arithmetic, local(): low = jnp.where(mine, low_came, low)  4.01 us
    select_n x5, other arithmetic, local(): up = jnp.where(mine, up_came, up)  3.45 us
  transfers between devices with their start and end apart: 26, of which 6 were waited for; matrix products, arithmetic and copies ran while one was open for 7% of the time, Pallas kernels for 2%

profile of v1, /device:TPU:1, one launch (start us, length us, event | category | flops | bytes accessed | tf_op | source)
XLA Modules:
  0.0 161.2 jit_solution(782428682821412251)
XLA Ops:
  0.0 1.2 copy-done
  1.2 1.2 copy-done.2
  2.5 1.0 copy-done.4
  3.5 1.0 copy-done.6
  4.5 0.7 copy-done.9
  5.2 0.7 copy-done.11
  5.8 1.0 shard_map.83
  6.8 2.2 %collective-permute-start.15 = (bf16[784,256]{1,0:T(8,128)(2,1)S(1)}, bf16[784,256]{1,0:T(8,128)(2,1)S(1)}, u32[]{:S(2)}, u32[]{:S(2)}) collective-permute-start(bf16[784,256]{1,0:T(8,128)(2,1)S(1)} %get-tuple-element.54), channel_id=1, source_target_pairs={{0,1},{1,0},{2,3},{3,2},{4,5},{5,4},{6,7},{7,6},{8,9},{9,8},{10,11... | collective-permute-start | bytes 1204232 | tf_op jit(solution)/shard_map/ppermute | solution.py:39
  9.2 0.7 copy-done.13
  9.8 0.2 fusion.1
  10.0 0.7 fusion.3
  10.7 6.1 %collective-permute-done.15 = bf16[784,256]{1,0:T(8,128)(2,1)S(1)} collective-permute-done((bf16[784,256]{1,0:T(8,128)(2,1)S(1)}, bf16[784,256]{1,0:T(8,128)(2,1)S(1)}, u32[]{:S(2)}, u32[]{:S(2)}) %collective-permute-start.15) | collective-permute-done | bytes 401440 | tf_op jit(solution)/shard_map/ppermute | solution.py:39
  16.8 0.6 broadcast_select_fusion.9
  17.4 4.1 %collective-permute-start.16 = (bf16[784,256]{1,0:T(8,128)(2,1)S(1)}, bf16[784,256]{1,0:T(8,128)(2,1)S(1)}, u32[]{:S(2)}, u32[]{:S(2)}) collective-permute-start(bf16[784,256]{1,0:T(8,128)(2,1)S(1)} %get-tuple-element.60), channel_id=1, source_target_pairs={{0,2},{1,3},{2,0},{3,1},{4,6},{5,7},{6,4},{7,5},{8,10},{9,11},{10,... | collective-permute-start | bytes 1204232 | tf_op jit(solution)/shard_map/ppermute | solution.py:39
  21.5 1.1 collective-permute-done.1
  22.6 0.6 broadcast_select_fusion.26
  23.2 4.1 %collective-permute-start.3 = (bf16[528,256]{1,0:T(8,128)(2,1)S(1)}, bf16[528,256]{1,0:T(8,128)(2,1)S(1)}, u32[]{:S(2)}, u32[]{:S(2)}) collective-permute-start(bf16[528,256]{1,0:T(8,128)(2,1)S(1)} %get-tuple-element.81), channel_id=1, source_target_pairs={{0,2},{1,3},{2,0},{3,1},{4,6},{5,7},{6,4},{7,5},{8,10},{9,11},{10,... | collective-permute-start | bytes 811016 | tf_op jit(solution)/shard_map/ppermute | solution.py:39
  27.3 7.4 %collective-permute-done.16 = bf16[784,256]{1,0:T(8,128)(2,1)S(1)} collective-permute-done((bf16[784,256]{1,0:T(8,128)(2,1)S(1)}, bf16[784,256]{1,0:T(8,128)(2,1)S(1)}, u32[]{:S(2)}, u32[]{:S(2)}) %collective-permute-start.16) | collective-permute-done | bytes 401440 | tf_op jit(solution)/shard_map/ppermute | solution.py:39
  34.8 0.7 broadcast_select_fusion.11
  35.5 0.7 collective-permute-start.17
  36.2 4.3 %collective-permute-done.3 = bf16[528,256]{1,0:T(8,128)(2,1)S(1)} collective-permute-done((bf16[528,256]{1,0:T(8,128)(2,1)S(1)}, bf16[528,256]{1,0:T(8,128)(2,1)S(1)}, u32[]{:S(2)}, u32[]{:S(2)}) %collective-permute-start.3) | collective-permute-done | bytes 270368 | tf_op jit(solution)/shard_map/ppermute | solution.py:39
  40.6 0.8 broadcast_select_fusion.24
  41.3 0.7 collective-permute-start.5
  42.0 0.7 broadcast_select_fusion.13
  42.8 0.7 collective-permute-start.18
  43.5 0.7 broadcast_select_fusion.22
  44.2 0.7 collective-permute-start.7
  44.9 0.6 broadcast_select_fusion.7
  45.5 0.7 collective-permute-start.19
  46.2 0.6 broadcast_select_fusion.20
  46.9 0.8 collective-permute-start.9
  47.7 0.7 broadcast_select_fusion.5
  48.4 0.7 collective-permute-start.20
  49.1 0.6 fusion.2
  49.8 0.6 copy-done.10
  50.4 1.8 %shard_map.82 = (f32[3,16,256]{2,1,0:T(8,128)S(1)}, f32[128,256]{1,0:T(8,128)S(1)}, bf16[128,256]{1,0:T(8,128)(2,1)S(1)}) custom-call(s32[1,4]{1,0:T(1,128)S(1)} %copy-done.10, s32[1,4]{1,0:T(1,128)S(1)} %copy-done.12, s32[1]{0:T(128)} %bitcast.level, f32[1,4,16,256]{3,2,1,0:T(8,128)S(1)} %copy-done.8, bf16[1,4,256,256]{3,2,1,0:T(8,128)(2,1)S(1)} %copy-done.5, ...), custom_call_target="tpu_custom_call" | custom-call | tf_op jit(solution)/shard_map/pallas_call | solution.py:132
  52.3 3.4 %collective-permute-done.came = bf16[128,256]{1,0:T(8,128)(2,1)S(1)} collective-permute-done((bf16[128,256]{1,0:T(8,128)(2,1)S(1)}, bf16[128,256]{1,0:T(8,128)(2,1)S(1)}, u32[]{:S(2)}, u32[]{:S(2)}) %collective-permute-start) | collective-permute-done | bytes 65568 | tf_op jit(solution)/shard_map/ppermute | solution.py:39
  55.7 0.2 shard_map.84
  55.9 33.7 %collective-permute-start.2 = (bf16[112,256]{1,0:T(8,128)(2,1)S(1)}, bf16[112,256]{1,0:T(8,128)(2,1)S(1)}, u32[]{:S(2)}, u32[]{:S(2)}) collective-permute-start(bf16[112,256]{1,0:T(8,128)(2,1)S(1)} %get-tuple-element.36), channel_id=1, source_target_pairs={{0,2},{1,3},{2,0},{3,1},{4,6},{5,7},{6,4},{7,5},{8,10},{9,11},{10,... | collective-permute-start | bytes 172040 | tf_op jit(solution)/shard_map/ppermute | solution.py:39
  89.6 0.6 broadcast_select_fusion.18
  90.2 0.7 collective-permute-start.11
  90.9 0.7 broadcast_select_fusion.3
  91.6 0.7 collective-permute-start.21
  92.3 0.2 shard_map.85
  92.5 0.7 collective-permute-start.4
  93.2 0.2 shard_map.86
  93.3 0.7 collective-permute-start.6
  94.0 0.2 shard_map.87
  94.2 0.7 collective-permute-start.8
  95.0 0.7 collective-permute-start.10
  95.7 0.7 broadcast_select_fusion.16
  96.4 0.7 collective-permute-start.13
  97.3 0.7 collective-permute-start.12
  97.9 0.7 broadcast_select_fusion.1
  98.6 0.7 collective-permute-start.22
  99.3 0.7 broadcast_select_fusion.15.low
  100.2 0.7 collective-permute-start.14
  100.9 0.7 broadcast_select_fusion.refs_11_
  101.6 0.7 shard_map.91
  102.3 0.7 collective-permute-start.25
  103.0 1.3 collective-permute-start.24
  104.3 0.7 collective-permute-start.23
  105.0 53.4 %collective-permute-done.24 = bf16[96,256]{1,0:T(8,128)(2,1)S(1)} collective-permute-done((bf16[96,256]{1,0:T(8,128)(2,1)S(1)}, bf16[96,256]{1,0:T(8,128)(2,1)S(1)}, u32[]{:S(2)}, u32[]{:S(2)}) %collective-permute-start.24) | collective-permute-done | bytes 49184 | tf_op jit(solution)/shard_map/ppermute | solution.py:48
  158.5 2.7 %shard_map.92 = f32[1,4,16,256]{3,2,1,0:T(8,128)} custom-call(s32[1,4]{1,0:T(1,128)S(1)} %copy-done.10, s32[1,4]{1,0:T(1,128)S(1)} %copy-done.12, s32[1]{0:T(128)} %bitcast.level, f32[3,16,256]{2,1,0:T(8,128)S(1)} %get-tuple-element.31.solved, bf16[96,256]{1,0:T(8,128)(2,1)S(1)} %add_select_fusion.known, bf16[16,256]{1,0:T(8,128)(2,1)S(1)} %get-tuple-element.55.r1, ...), custom_call_target="tpu_custom_call" | custom-call | tf_op jit(solution)/shard_map/pallas_call | solution.py:251
  (48 shorter events, 0.8 us)
Async XLA Ops:
  0.0 1.2 copy-start
  1.2 1.2 copy-start.2
  2.5 1.0 copy-start.4
  3.5 1.0 copy-start.6
  4.5 0.7 copy-start.9
  5.2 0.7 copy-start.11
  6.8 10.0 %collective-permute-start.15 = (bf16[784,256]{1,0:T(8,128)(2,1)S(1)}, bf16[784,256]{1,0:T(8,128)(2,1)S(1)}, u32[]{:S(2)}, u32[]{:S(2)}) collective-permute-start(bf16[784,256]{1,0:T(8,128)(2,1)S(1)} %get-tuple-element.54), channel_id=1, source_target_pairs={{0,1},{1,0},{2,3},{3,2},{4,5},{5,4},{6,7},{7,6},{8,9},{9,8},{10,11... | collective-permute-start | bytes 1204232 | tf_op jit(solution)/shard_map/ppermute | solution.py:39
  9.1 13.6 %collective-permute-start.1 = (bf16[528,256]{1,0:T(8,128)(2,1)S(1)}, bf16[528,256]{1,0:T(8,128)(2,1)S(1)}, u32[]{:S(2)}, u32[]{:S(2)}) collective-permute-start(bf16[528,256]{1,0:T(8,128)(2,1)S(1)} %get-tuple-element.34), channel_id=1, source_target_pairs={{0,1},{1,0},{2,3},{3,2},{4,5},{5,4},{6,7},{7,6},{8,9},{9,8},{10,11... | collective-permute-start | bytes 811016 | tf_op jit(solution)/shard_map/ppermute | solution.py:39
  9.2 0.7 copy-start.13
  17.4 17.3 %collective-permute-start.16 = (bf16[784,256]{1,0:T(8,128)(2,1)S(1)}, bf16[784,256]{1,0:T(8,128)(2,1)S(1)}, u32[]{:S(2)}, u32[]{:S(2)}) collective-permute-start(bf16[784,256]{1,0:T(8,128)(2,1)S(1)} %get-tuple-element.60), channel_id=1, source_target_pairs={{0,2},{1,3},{2,0},{3,1},{4,6},{5,7},{6,4},{7,5},{8,10},{9,11},{10,... | collective-permute-start | bytes 1204232 | tf_op jit(solution)/shard_map/ppermute | solution.py:39
  23.2 17.3 %collective-permute-start.3 = (bf16[528,256]{1,0:T(8,128)(2,1)S(1)}, bf16[528,256]{1,0:T(8,128)(2,1)S(1)}, u32[]{:S(2)}, u32[]{:S(2)}) collective-permute-start(bf16[528,256]{1,0:T(8,128)(2,1)S(1)} %get-tuple-element.81), channel_id=1, source_target_pairs={{0,2},{1,3},{2,0},{3,1},{4,6},{5,7},{6,4},{7,5},{8,10},{9,11},{10,... | collective-permute-start | bytes 811016 | tf_op jit(solution)/shard_map/ppermute | solution.py:39
  35.5 6.5 %collective-permute-start.17 = (bf16[784,256]{1,0:T(8,128)(2,1)S(1)}, bf16[784,256]{1,0:T(8,128)(2,1)S(1)}, u32[]{:S(2)}, u32[]{:S(2)}) collective-permute-start(bf16[784,256]{1,0:T(8,128)(2,1)S(1)} %get-tuple-element.58), channel_id=1, source_target_pairs={{0,4},{4,0},{8,12},{12,8},{16,20},{20,16},{24,28},{28,24},{32,36},... | collective-permute-start | bytes 1204232 | tf_op jit(solution)/shard_map/ppermute | solution.py:39
  41.3 2.1 %collective-permute-start.5 = (bf16[528,256]{1,0:T(8,128)(2,1)S(1)}, bf16[528,256]{1,0:T(8,128)(2,1)S(1)}, u32[]{:S(2)}, u32[]{:S(2)}) collective-permute-start(bf16[528,256]{1,0:T(8,128)(2,1)S(1)} %get-tuple-element.79), channel_id=1, source_target_pairs={{0,4},{4,0},{8,12},{12,8},{16,20},{20,16},{24,28},{28,24},{32,36},... | collective-permute-start | bytes 811016 | tf_op jit(solution)/shard_map/ppermute | solution.py:39
  42.8 2.1 %collective-permute-start.18 = (bf16[784,256]{1,0:T(8,128)(2,1)S(1)}, bf16[784,256]{1,0:T(8,128)(2,1)S(1)}, u32[]{:S(2)}, u32[]{:S(2)}) collective-permute-start(bf16[784,256]{1,0:T(8,128)(2,1)S(1)} %get-tuple-element.69), channel_id=1, source_target_pairs={{0,8},{4,12},{8,0},{12,4},{16,24},{20,28},{24,16},{28,20},{32,40},... | collective-permute-start | bytes 1204232 | tf_op jit(solution)/shard_map/ppermute | solution.py:39
  44.2 2.0 %collective-permute-start.7 = (bf16[528,256]{1,0:T(8,128)(2,1)S(1)}, bf16[528,256]{1,0:T(8,128)(2,1)S(1)}, u32[]{:S(2)}, u32[]{:S(2)}) collective-permute-start(bf16[528,256]{1,0:T(8,128)(2,1)S(1)} %get-tuple-element.77), channel_id=1, source_target_pairs={{0,8},{4,12},{8,0},{12,4},{16,24},{20,28},{24,16},{28,20},{32,40},... | collective-permute-start | bytes 811016 | tf_op jit(solution)/shard_map/ppermute | solution.py:39
  45.5 2.2 %collective-permute-start.19 = (bf16[784,256]{1,0:T(8,128)(2,1)S(1)}, bf16[784,256]{1,0:T(8,128)(2,1)S(1)}, u32[]{:S(2)}, u32[]{:S(2)}) collective-permute-start(bf16[784,256]{1,0:T(8,128)(2,1)S(1)} %get-tuple-element.67), channel_id=1, source_target_pairs={{0,16},{4,20},{8,24},{12,28},{16,0},{20,4},{24,8},{28,12},{32,48},... | collective-permute-start | bytes 1204232 | tf_op jit(solution)/shard_map/ppermute | solution.py:39
  46.2 3.5 %copy-start.8 = (f32[1,4,16,256]{3,2,1,0:T(8,128)S(1)}, f32[1,4,16,256]{3,2,1,0:T(8,128)}, u32[]{:S(2)}) copy-start(f32[1,4,16,256]{3,2,1,0:T(8,128)} %rights.1) | copy-start | bytes 196612
  46.9 2.9 %copy-start.1 = (bf16[1,4,2,256,256]{4,3,2,1,0:T(8,128)(2,1)S(1)}, bf16[1,4,2,256,256]{4,3,2,1,0:T(8,128)(2,1)}, u32[]{:S(2)}) copy-start(bf16[1,4,2,256,256]{4,3,2,1,0:T(8,128)(2,1)} %lblk.3) | copy-start | bytes 3145732
  46.9 42.7 %collective-permute-start.9 = (bf16[528,256]{1,0:T(8,128)(2,1)S(1)}, bf16[528,256]{1,0:T(8,128)(2,1)S(1)}, u32[]{:S(2)}, u32[]{:S(2)}) collective-permute-start(bf16[528,256]{1,0:T(8,128)(2,1)S(1)} %get-tuple-element.75), channel_id=1, source_target_pairs={{0,16},{4,20},{8,24},{12,28},{16,0},{20,4},{24,8},{28,12},{32,48},... | collective-permute-start | bytes 811016 | tf_op jit(solution)/shard_map/ppermute | solution.py:39
  47.7 2.0 %copy-start.5 = (bf16[1,4,256,256]{3,2,1,0:T(8,128)(2,1)S(1)}, bf16[1,4,256,256]{3,2,1,0:T(8,128)(2,1)}, u32[]{:S(2)}) copy-start(bf16[1,4,256,256]{3,2,1,0:T(8,128)(2,1)} %linv.3) | copy-start | bytes 1572868
  48.4 42.5 %collective-permute-start.20 = (bf16[784,256]{1,0:T(8,128)(2,1)S(1)}, bf16[784,256]{1,0:T(8,128)(2,1)S(1)}, u32[]{:S(2)}, u32[]{:S(2)}) collective-permute-start(bf16[784,256]{1,0:T(8,128)(2,1)S(1)} %get-tuple-element.65), channel_id=1, source_target_pairs={{0,32},{4,36},{8,40},{12,44},{16,48},{20,52},{24,56},{28,60},{32,0... | collective-permute-start | bytes 1204232 | tf_op jit(solution)/shard_map/ppermute | solution.py:39
  49.7 0.7 copy-start.10
  49.7 0.7 copy-start.12
  52.2 3.5 %collective-permute-start = (bf16[128,256]{1,0:T(8,128)(2,1)S(1)}, bf16[128,256]{1,0:T(8,128)(2,1)S(1)}, u32[]{:S(2)}, u32[]{:S(2)}) collective-permute-start(bf16[128,256]{1,0:T(8,128)(2,1)S(1)} %get-tuple-element.33), channel_id=1, source_target_pairs={{0,1},{1,0},{2,3},{3,2},{4,5},{5,4},{6,7},{7,6},{8,9},{9,8},{10,11... | collective-permute-start | bytes 196616 | tf_op jit(solution)/shard_map/ppermute | solution.py:39
  55.9 36.5 %collective-permute-start.2 = (bf16[112,256]{1,0:T(8,128)(2,1)S(1)}, bf16[112,256]{1,0:T(8,128)(2,1)S(1)}, u32[]{:S(2)}, u32[]{:S(2)}) collective-permute-start(bf16[112,256]{1,0:T(8,128)(2,1)S(1)} %get-tuple-element.36), channel_id=1, source_target_pairs={{0,2},{1,3},{2,0},{3,1},{4,6},{5,7},{6,4},{7,5},{8,10},{9,11},{10,... | collective-permute-start | bytes 172040 | tf_op jit(solution)/shard_map/ppermute | solution.py:39
  90.2 5.5 %collective-permute-start.11 = (bf16[528,256]{1,0:T(8,128)(2,1)S(1)}, bf16[528,256]{1,0:T(8,128)(2,1)S(1)}, u32[]{:S(2)}, u32[]{:S(2)}) collective-permute-start(bf16[528,256]{1,0:T(8,128)(2,1)S(1)} %get-tuple-element.73), channel_id=1, source_target_pairs={{0,32},{4,36},{8,40},{12,44},{16,48},{20,52},{24,56},{28,60},{32,0... | collective-permute-start | bytes 811016 | tf_op jit(solution)/shard_map/ppermute | solution.py:39
  91.6 6.3 %collective-permute-start.21 = (bf16[784,256]{1,0:T(8,128)(2,1)S(1)}, bf16[784,256]{1,0:T(8,128)(2,1)S(1)}, u32[]{:S(2)}, u32[]{:S(2)}) collective-permute-start(bf16[784,256]{1,0:T(8,128)(2,1)S(1)} %get-tuple-element.63), channel_id=1, source_target_pairs={{0,64},{4,68},{8,72},{12,76},{16,80},{20,84},{24,88},{28,92},{32,9... | collective-permute-start | bytes 1204232 | tf_op jit(solution)/shard_map/ppermute | solution.py:39
  92.5 0.7 collective-permute-start.4
  93.3 0.7 collective-permute-start.6
  94.2 0.7 collective-permute-start.8
  95.0 2.1 %collective-permute-start.10 = (bf16[48,256]{1,0:T(8,128)(2,1)S(1)}, bf16[48,256]{1,0:T(8,128)(2,1)S(1)}, u32[]{:S(2)}, u32[]{:S(2)}) collective-permute-start(bf16[48,256]{1,0:T(8,128)(2,1)S(1)} %get-tuple-element.47), channel_id=1, source_target_pairs={{0,32},{4,36},{8,40},{12,44},{16,48},{20,52},{24,56},{28,60},{32,0... | collective-permute-start | bytes 73736 | tf_op jit(solution)/shard_map/ppermute | solution.py:39
  96.4 2.9 %collective-permute-start.13 = (bf16[528,256]{1,0:T(8,128)(2,1)S(1)}, bf16[528,256]{1,0:T(8,128)(2,1)S(1)}, u32[]{:S(2)}, u32[]{:S(2)}) collective-permute-start(bf16[528,256]{1,0:T(8,128)(2,1)S(1)} %get-tuple-element.71), channel_id=1, source_target_pairs={{0,64},{4,68},{8,72},{12,76},{16,80},{20,84},{24,88},{28,92},{32,9... | collective-permute-start | bytes 811016 | tf_op jit(solution)/shard_map/ppermute | solution.py:39
  97.3 2.8 %collective-permute-start.12 = (bf16[32,256]{1,0:T(8,128)(2,1)S(1)}, bf16[32,256]{1,0:T(8,128)(2,1)S(1)}, u32[]{:S(2)}, u32[]{:S(2)}) collective-permute-start(bf16[32,256]{1,0:T(8,128)(2,1)S(1)} %get-tuple-element.50), channel_id=1, source_target_pairs={{0,64},{4,68},{8,72},{12,76},{16,80},{20,84},{24,88},{28,92},{32,9... | collective-permute-start | bytes 49160 | tf_op jit(solution)/shard_map/ppermute | solution.py:39
  98.6 2.2 %collective-permute-start.22 = (bf16[784,256]{1,0:T(8,128)(2,1)S(1)}, bf16[784,256]{1,0:T(8,128)(2,1)S(1)}, u32[]{:S(2)}, u32[]{:S(2)}) collective-permute-start(bf16[784,256]{1,0:T(8,128)(2,1)S(1)} %get-tuple-element.61), channel_id=1, source_target_pairs={{0,130},{4,134},{8,138},{12,142},{16,146},{20,150},{24,154},{28,15... | collective-permute-start | bytes 1204232 | tf_op jit(solution)/shard_map/ppermute | solution.py:39
  100.2 0.7 collective-permute-start.14
  101.6 56.9 %copy-start.3 = (bf16[1,4,2,256,256]{4,3,2,1,0:T(8,128)(2,1)S(1)}, bf16[1,4,2,256,256]{4,3,2,1,0:T(8,128)(2,1)}, u32[]{:S(2)}) copy-start(bf16[1,4,2,256,256]{4,3,2,1,0:T(8,128)(2,1)} %ublk.3) | copy-start | bytes 3145732
  101.6 56.9 %copy-start.7 = (bf16[1,4,256,256]{3,2,1,0:T(8,128)(2,1)S(1)}, bf16[1,4,256,256]{3,2,1,0:T(8,128)(2,1)}, u32[]{:S(2)}) copy-start(bf16[1,4,256,256]{3,2,1,0:T(8,128)(2,1)} %uinv.3) | copy-start | bytes 1572868
  102.3 2.7 %collective-permute-start.25 = (bf16[96,256]{1,0:T(8,128)(2,1)S(1)}, bf16[96,256]{1,0:T(8,128)(2,1)S(1)}, u32[]{:S(2)}, u32[]{:S(2)}) collective-permute-start(bf16[96,256]{1,0:T(8,128)(2,1)S(1)} %shard_map.91), channel_id=1, source_target_pairs={{0,3},{4,7},{8,11},{12,15},{16,19},{20,23},{24,27},{28,31},{32,35}... | collective-permute-start | bytes 147464 | tf_op jit(solution)/shard_map/ppermute | solution.py:48
  103.0 55.4 %collective-permute-start.24 = (bf16[96,256]{1,0:T(8,128)(2,1)S(1)}, bf16[96,256]{1,0:T(8,128)(2,1)S(1)}, u32[]{:S(2)}, u32[]{:S(2)}) collective-permute-start(bf16[96,256]{1,0:T(8,128)(2,1)S(1)} %shard_map.91), channel_id=1, source_target_pairs={{0,2},{4,6},{8,10},{12,14},{16,18},{20,22},{24,26},{28,30},{32,34}... | collective-permute-start | bytes 147464 | tf_op jit(solution)/shard_map/ppermute | solution.py:48
  104.3 54.2 %collective-permute-start.23 = (bf16[96,256]{1,0:T(8,128)(2,1)S(1)}, bf16[96,256]{1,0:T(8,128)(2,1)S(1)}, u32[]{:S(2)}, u32[]{:S(2)}) collective-permute-start(bf16[96,256]{1,0:T(8,128)(2,1)S(1)} %shard_map.91), channel_id=1, source_target_pairs={{0,1},{4,5},{8,9},{12,13},{16,17},{20,21},{24,25},{28,29},{32,33},... | collective-permute-start | bytes 147464 | tf_op jit(solution)/shard_map/ppermute | solution.py:48

commit v2 on v1

v2 whole, which is shorter than its diff:
```python
import functools

import jax
import jax.numpy as jnp
from jax import lax
from jax.experimental import pallas as pl
from jax.experimental.pallas import tpu as pltpu
from jax.sharding import PartitionSpec as P

W = 256
RHS = 16
LOCAL_COUNT = 3
UPPER = 8
LOW = 2
DEVICES = 256
AXES = ("gz", "row", "col")
BF16 = jnp.bfloat16
F32 = jnp.float32
FAR_A = 2 * W
SUMS = 2 * W + RHS
FAR_B = 3 * W
ROWS = 3 * W + RHS
OTHER_PAIR = UPPER
ROLE_A = UPPER + 1
FLAGS = UPPER + 2
VMEM = pl.BlockSpec(memory_space=pltpu.VMEM)
HBM = pl.BlockSpec(memory_space=pltpu.HBM)
PARAMS = pltpu.CompilerParams(vmem_limit_bytes=24 * 1024 * 1024)


def seat(t):
    return (t % 4 - (0 if t < DEVICES // 2 else 2)) % 4


def at_seat(t, place):
    return t - t % 4 + (place + (0 if t < DEVICES // 2 else 2)) % 4


def send(value, pairs):
    return lax.ppermute(value, AXES, pairs)


def seats(moves):
    firsts = [t for t in range(DEVICES) if t % 4 == 0]
    return [(at_seat(t, a), at_seat(t, b)) for t in firsts for a, b in moves]


def across(level):
    return [(t, t ^ (1 << (level - 1))) for t in range(DEVICES) if seat(t) < 2]


def layers(a, b):
    firsts = [t for t in range(DEVICES) if t % 4 == 0]
    return [(at_seat(t, a), at_seat(t ^ (DEVICES // 2), b)) for t in firsts]


def times(vectors, blocks):
    return jnp.dot(vectors, blocks, preferred_element_type=F32)


def times_rows(vectors, blocks):
    return lax.dot_general(
        vectors, blocks, (((1,), (1,)), ((), ())), preferred_element_type=F32
    )


def row_pad(width):
    return lax.broadcasted_iota(jnp.int32, (1, W), 1) < width


def part(rows, index):
    return rows[index * RHS : (index + 1) * RHS]


def begin_kernel(
    rights_in,
    linv_in,
    uinv_in,
    lblk_in,
    ublk_in,
    widths_in,
    far_in,
    owner,
    first,
    second,
    solved,
    sums,
    flags,
    level,
    rights,
    linv,
    uinv,
    lblk,
    ublk,
    widths,
    far,
    sems,
):
    own = pl.ds(LOCAL_COUNT, 1)
    rest = pl.ds(0, LOCAL_COUNT)
    small = [
        pltpu.make_async_copy(widths_in, widths, sems.at[0]),
        pltpu.make_async_copy(far_in, far, sems.at[1]),
    ]
    mine = [
        pltpu.make_async_copy(linv_in.at[0, own], linv.at[own], sems.at[2]),
        pltpu.make_async_copy(lblk_in.at[0, own], lblk.at[own], sems.at[3]),
        pltpu.make_async_copy(uinv_in.at[0, own], uinv, sems.at[4]),
        pltpu.make_async_copy(ublk_in.at[0, own], ublk, sems.at[5]),
    ]
    leaf = [
        pltpu.make_async_copy(rights_in.at[0], rights, sems.at[6]),
        pltpu.make_async_copy(linv_in.at[0, rest], linv.at[rest], sems.at[7]),
        pltpu.make_async_copy(lblk_in.at[0, rest], lblk.at[rest], sems.at[8]),
    ]
    for copy in small + mine + leaf:
        copy.start()
    gz = lax.axis_index("gz")
    col = lax.axis_index("col")
    me = gz * (DEVICES // 2) + lax.axis_index("row") * (DEVICES // 8) + col
    y = col % 4
    place = (y + 2 * gz) % 4
    everyone = lax.broadcasted_iota(jnp.int32, (1, DEVICES), 1)
    owners = owner[...]

    def spread(value):
        return jnp.broadcast_to(value, (RHS, W))

    def found(chosen):
        return spread(jnp.max(jnp.where(chosen, 1.0, 0.0), axis=1, keepdims=True))

    for v in range(1, UPPER + 1):
        half = lax.shift_right_logical(everyone, v - 1) == lax.shift_right_logical(me, v - 1)
        flags[(v - 1) * RHS : v * RHS] = found(half & (owners == v)).astype(BF16)
    flags[OTHER_PAIR * RHS : (OTHER_PAIR + 1) * RHS] = found(
        (everyone == (me ^ 2)) & (owners == 1)
    ).astype(BF16)
    flags[ROLE_A * RHS : (ROLE_A + 1) * RHS] = jnp.full(
        (RHS, W), jnp.where(place == 0, 1.0, 0.0), F32
    ).astype(BF16)
    my_level = spread(
        jnp.sum(jnp.where(everyone == me, owners, 0).astype(F32), axis=1, keepdims=True)
    )
    level[...] = my_level
    for copy in small + mine:
        copy.wait()
    pad = lax.broadcasted_iota(jnp.int32, (W, 1), 0) < widths[0, LOCAL_COUNT]
    distance = jnp.full((RHS, W), far[0, LOCAL_COUNT], jnp.int32).astype(F32).astype(BF16)
    lower = jnp.where(pad, linv[LOCAL_COUNT].astype(F32), 0.0).astype(BF16)
    upper = jnp.where(pad, uinv[0].astype(F32), 0.0).astype(BF16)
    low_blocks = [times(lblk[LOCAL_COUNT, b], lower).T.astype(BF16) for b in range(2)]
    up_blocks = [times(upper, ublk[0, b]).T.astype(BF16) for b in range(2)]
    up_blocks.append(times(upper, lower).T.astype(BF16))
    for copy in leaf:
        copy.wait()
    for v in range(1, UPPER + 1):
        sums[(v - 1) * RHS : v * RHS] = jnp.where(my_level == v, rights[LOCAL_COUNT], 0.0)
    pending = jnp.zeros((RHS, W), F32)
    for slot in range(LOCAL_COUNT):
        residue = rights[slot]
        if slot == LOCAL_COUNT - 1:
            residue = residue - pending
        forward = jnp.where(
            row_pad(widths[0, slot]), times_rows(residue.astype(BF16), linv[slot]), 0.0
        )
        solved[slot] = forward
        half = forward.astype(BF16)
        near = times_rows(half, lblk[slot, 0])
        away = times_rows(half, lblk[slot, 1])
        if slot == LOCAL_COUNT - 1:
            sums[:RHS] = sums[:RHS] - near
            target = far[0, slot]
        else:
            pending = pending + near
            target = far[0, slot] - 1
        for v in range(1, UPPER + 1):
            rows = slice((v - 1) * RHS, v * RHS)
            sums[rows] = sums[rows] - jnp.where(target == v, away, 0.0)
    halves = sums[...].astype(BF16)

    def write(low, up):
        for b in range(2):
            low[b * W : (b + 1) * W] = low_blocks[b]
        low[FAR_A : FAR_A + RHS] = distance
        low[SUMS : SUMS + UPPER * RHS] = halves
        low[SUMS + UPPER * RHS :] = jnp.zeros((ROWS - SUMS - UPPER * RHS, W), BF16)
        for b in range(3):
            up[b * W : (b + 1) * W] = up_blocks[b]
        up[FAR_B:] = distance

    @pl.when(place % 2 == 0)
    def _():
        write(first, second)

    @pl.when(place % 2 == 1)
    def _():
        write(second, first)


def begin(rights, linv, uinv, lblk, ublk, widths, far, owner):
    return pl.pallas_call(
        begin_kernel,
        in_specs=[HBM] * 7 + [VMEM],
        out_specs=[VMEM] * 6,
        out_shape=[
            jax.ShapeDtypeStruct((ROWS, W), BF16),
            jax.ShapeDtypeStruct((ROWS, W), BF16),
            jax.ShapeDtypeStruct((LOCAL_COUNT, RHS, W), F32),
            jax.ShapeDtypeStruct((UPPER * RHS, W), F32),
            jax.ShapeDtypeStruct((FLAGS * RHS, W), BF16),
            jax.ShapeDtypeStruct((RHS, W), F32),
        ],
        scratch_shapes=[
            pltpu.VMEM((4, RHS, W), F32),
            pltpu.VMEM((4, W, W), BF16),
            pltpu.VMEM((1, W, W), BF16),
            pltpu.VMEM((4, 2, W, W), BF16),
            pltpu.VMEM((1, 2, W, W), BF16),
            pltpu.SMEM((1, 4), jnp.int32),
            pltpu.SMEM((1, 4), jnp.int32),
            pltpu.SemaphoreType.DMA((9,)),
        ],
        compiler_params=PARAMS,
    )(rights, linv, uinv, lblk, ublk, widths, far, owner)


def flag(flags, index):
    return part(flags, index).astype(F32) > 0.5


def choose(test, one, other):
    return jnp.where(test, one.astype(F32), other.astype(F32)).astype(BF16)


def choose_rows(test, one, other, chosen, left):
    wide = jnp.concatenate([test] * 16, axis=0)
    for start in range(0, ROWS, W):
        rows = slice(start, min(start + W, ROWS))
        amount = rows.stop - rows.start
        a, b = (one[rows], other[rows])
        chosen[rows] = choose(wide[:amount], a, b)
        left[rows] = choose(wide[:amount], b, a)


def eliminate(total, low):
    half = total[:RHS].astype(BF16)
    near = times(half, low[:W])
    away = times(half, low[W : 2 * W])
    distance = low[FAR_A : FAR_A + RHS].astype(F32)
    rest = []
    for step in range(1, total.shape[0] // RHS):
        value = part(total, step)
        if step == 1:
            value = value - near
        rest.append(value - jnp.where(distance == float(step), away, 0.0))
    return half, jnp.concatenate(rest, axis=0)


def pass_on(flags, rest, left):
    rows = rest.shape[0]
    wide = jnp.concatenate([flag(flags, ROLE_A)] * (rows // RHS), axis=0)
    left[SUMS : SUMS + rows] = choose(wide, rest.astype(BF16), left[SUMS : SUMS + rows])


def climb_low_kernel(own, r1, r2, r3, sums, flags, k1, k1q, k2, left, residues, rest, lp, lq):
    choose_rows(flag(flags, 0), own, r1, k1, lp)
    choose_rows(flag(flags, OTHER_PAIR), r2, r3, k1q, lq)
    choose_rows(flag(flags, 1), lp, lq, k2, left)
    rows = slice(SUMS, SUMS + UPPER * RHS)
    near = sums[...] + r1[rows].astype(F32)
    other = r2[rows].astype(F32) + r3[rows].astype(F32)
    half, near = eliminate(near, k1)
    residues[:RHS] = half
    half, other = eliminate(other, k1q)
    residues[RHS : 2 * RHS] = half
    half, value = eliminate(near + other, k2)
    residues[2 * RHS :] = half
    rest[...] = value
    pass_on(flags, value, left)


def climb_low(own, r1, r2, r3, sums, flags):
    message = jax.ShapeDtypeStruct((ROWS, W), BF16)
    return pl.pallas_call(
        climb_low_kernel,
        in_specs=[VMEM] * 6,
        out_specs=[VMEM] * 6,
        out_shape=[
            message,
            message,
            message,
            message,
            jax.ShapeDtypeStruct((3 * RHS, W), BF16),
            jax.ShapeDtypeStruct(((UPPER - LOW) * RHS, W), F32),
        ],
        scratch_shapes=[pltpu.VMEM((ROWS, W), BF16)] * 2,
        compiler_params=PARAMS,
    )(own, r1, r2, r3, sums, flags)


def climb_kernel(height, own, came, sums, flags, chosen, left, residue, rest):
    choose_rows(flag(flags, height - 1), own, came, chosen, left)
    total = sums[...] + came[SUMS : SUMS + sums.shape[0]].astype(F32)
    half, value = eliminate(total, chosen)
    residue[...] = half
    rest[...] = value
    pass_on(flags, value, left)


def climb(height, own, came, sums, flags):
    message = jax.ShapeDtypeStruct((ROWS, W), BF16)
    return pl.pallas_call(
        functools.partial(climb_kernel, height),
        in_specs=[VMEM] * 4,
        out_specs=[VMEM] * 4,
        out_shape=[
            message,
            message,
            jax.ShapeDtypeStruct((RHS, W), BF16),
            jax.ShapeDtypeStruct((sums.shape[0] - RHS, W), F32),
        ],
        compiler_params=PARAMS,
    )(own, came, sums, flags)


def separator(residue, up, above):
    distance = up[FAR_B : FAR_B + RHS].astype(F32)
    known = jnp.zeros((RHS, W), F32)
    for step, value in enumerate(above, 1):
        known = known + jnp.where(distance == float(step), value.astype(F32), 0.0)
    return (
        times(residue, up[2 * W : 3 * W])
        - times(above[0], up[:W])
        - times(known.astype(BF16), up[W : 2 * W])
    ).astype(BF16)


def top_kernel(vectors, root, mine, came, flags, *refs):
    ups, (near_out, other_out) = (refs[:-2], refs[-2:])
    wide = jnp.concatenate([flag(flags, UPPER - 1)] * 16, axis=0)
    last = choose(wide, mine[2 * W : 3 * W], came[...])
    residue = part(vectors, UPPER).astype(F32) + root[...].astype(F32)
    above = [times(residue.astype(BF16), last).astype(BF16)]
    for v in range(UPPER - 1, LOW - 1, -1):
        above = [separator(part(vectors, v), ups[v], above)] + above
    for k, out in ((0, near_out), (1, other_out)):
        out[:RHS] = separator(part(vectors, k), ups[k], above)
        for step, value in enumerate(above, 1):
            out[step * RHS : (step + 1) * RHS] = value


def top(vectors, root, mine, came, flags, ups):
    known = jax.ShapeDtypeStruct((UPPER * RHS, W), BF16)
    return pl.pallas_call(
        top_kernel,
        in_specs=[VMEM] * (5 + len(ups)),
        out_specs=[VMEM] * 2,
        out_shape=[known, known],
        compiler_params=PARAMS,
    )(vectors, root, mine, came, flags, *ups)


def descend_kernel(
    uinv_in,
    ublk_in,
    widths_in,
    far_in,
    level,
    solved,
    own,
    a,
    b,
    c,
    out,
    uinv,
    ublk,
    widths,
    far,
    known,
    sems,
):
    rest = pl.ds(0, LOCAL_COUNT)
    copies = [
        pltpu.make_async_copy(widths_in, widths, sems.at[0]),
        pltpu.make_async_copy(far_in, far, sems.at[1]),
        pltpu.make_async_copy(uinv_in.at[0, rest], uinv, sems.at[2]),
        pltpu.make_async_copy(ublk_in.at[0, rest], ublk, sems.at[3]),
    ]
    for copy in copies:
        copy.start()
    place = (lax.axis_index("col") % 4 + 2 * lax.axis_index("gz")) % 4
    for seated, ref in ((0, a), (1, own), (2, b), (3, c)):

        @pl.when(place == seated)
        def _():
            known[...] = ref[...]

    above = [part(known, k) for k in range(UPPER)]
    own_value = jnp.zeros((RHS, W), F32)
    for k, value in enumerate(above):
        own_value = jnp.where(level[...] == k + 1, value.astype(F32), own_value)
    out[0, LOCAL_COUNT] = own_value
    for copy in copies:
        copy.wait()
    for slot in (2, 1, 0):
        distant = jnp.zeros((RHS, W), F32)
        for step, value in enumerate(above, 1):
            distant = distant + jnp.where(far[0, slot] == step, value.astype(F32), 0.0)
        residue = (
            solved[slot]
            - times_rows(above[0], ublk[slot, 0])
            - times_rows(distant.astype(BF16), ublk[slot, 1])
        )
        value = jnp.where(
            row_pad(widths[0, slot]), times_rows(residue.astype(BF16), uinv[slot]), 0.0
        )
        out[0, slot] = value
        if slot == 2:
            above = [value.astype(BF16)] + above


def descend(uinv, ublk, widths, far, level, solved, own, a, b, c):
    return pl.pallas_call(
        descend_kernel,
        in_specs=[HBM] * 4 + [VMEM] * 6,
        out_specs=VMEM,
        out_shape=jax.ShapeDtypeStruct((1, 4, RHS, W), F32),
        scratch_shapes=[
            pltpu.VMEM((LOCAL_COUNT, W, W), BF16),
            pltpu.VMEM((LOCAL_COUNT, 2, W, W), BF16),
            pltpu.SMEM((1, 4), jnp.int32),
            pltpu.SMEM((1, 4), jnp.int32),
            pltpu.VMEM((UPPER * RHS, W), BF16),
            pltpu.SemaphoreType.DMA((4,)),
        ],
        compiler_params=PARAMS,
    )(uinv, ublk, widths, far, level, solved, own, a, b, c)


def local(rights, linv, uinv, lblk, ublk, widths, far, owner_level):
    first, second, solved, sums, flags, level = begin(
        rights, linv, uinv, lblk, ublk, widths, far, owner_level.reshape(1, DEVICES)
    )
    r1 = send(second, seats(((1, 0), (0, 1))))
    r2 = send(first, seats(((2, 0), (3, 1))))
    r3 = send(second, seats(((3, 0), (2, 1))))
    near, other, above, message, residues, sums = climb_low(first, r1, r2, r3, sums, flags)
    ups = [near, other, above]
    vectors = [residues]
    for height in range(LOW + 1, UPPER):
        came = send(message, across(height))
        chosen, message, residue, sums = climb(height, message, came, sums, flags)
        ups.append(chosen)
        vectors.append(residue)
    root = sums.astype(BF16)
    root_came = send(root, layers(0, 1))
    vectors = send(jnp.concatenate(vectors + [root], axis=0), seats(((0, 1),)))
    last_came = send(message[2 * W : 3 * W], layers(1, 1))
    known, known_other = top(vectors, root_came, message, last_came, flags, ups)
    a = send(known, seats(((1, 0),)))
    b = send(known_other, seats(((1, 2),)))
    c = send(known_other, seats(((1, 3),)))
    return descend(uinv, ublk, widths, far, level, solved, known, a, b, c)


def solution(mesh):
    split = P(AXES)
    in_specs = (split,) * 7 + (P(),)
    return jax.shard_map(local, mesh=mesh, in_specs=in_specs, out_specs=split, check_vma=False)
```

time: 162 us -> 115 us (0.71)
  the two profiles are of different devices: /device:TPU:1 before, /device:TPU:24 now
where the time goes in v2:
time: 115 us
  waiting for transfers between devices  83.8 us (73%)
  starting transfers between devices  16.6 us (14%)
  Pallas kernels  7.09 us (6%)
  local copies, waits for them, and re-layouts  6.76 us (6%)
    ppermute x14, waiting for transfers between devices, send(): return lax.ppermute(value, AXES, pairs)  83.8 us
    ppermute x14, starting transfers between devices, send(): return lax.ppermute(value, AXES, pairs)  16.6 us
    unnamed x26, local copies, waits for them, and re-layouts  6.75 us
  transfers between devices with their start and end apart: 14, of which 3 were waited for; matrix products, arithmetic and copies ran while one was open for 0% of the time, Pallas kernels for 0%

profile of v2, /device:TPU:24, one launch (start us, length us, event | category | flops | bytes accessed | tf_op | source)
XLA Modules:
  0.0 114.6 jit_solution(808954749160121992)
XLA Ops:
  0.0 0.0 copy-start.7
  0.0 0.0 copy-start.8
  0.0 0.7 copy-done.7
  0.7 0.0 copy-done.8
  0.7 0.0 copy-start
  0.7 1.2 %copy-done = bf16[1,4,2,256,256]{4,3,2,1,0:T(8,128)(2,1)S(1)} copy-done((bf16[1,4,2,256,256]{4,3,2,1,0:T(8,128)(2,1)S(1)}, bf16[1,4,2,256,256]{4,3,2,1,0:T(8,128)(2,1)}, u32[]{:S(2)}) %copy-start) | copy-done | bytes 1048600
  1.9 0.0 copy-start.2
  1.9 1.0 copy-done.2
  2.9 0.0 copy-start.4
  2.9 1.2 %copy-done.4 = bf16[1,4,2,256,256]{4,3,2,1,0:T(8,128)(2,1)S(1)} copy-done((bf16[1,4,2,256,256]{4,3,2,1,0:T(8,128)(2,1)S(1)}, bf16[1,4,2,256,256]{4,3,2,1,0:T(8,128)(2,1)}, u32[]{:S(2)}) %copy-start.4) | copy-done | bytes 1048600
  4.2 0.0 copy-start.5
  4.2 1.0 copy-done.5
  5.2 0.0 copy-start.6
  5.2 0.8 copy-done.6
  6.0 0.0 copy-start.9
  6.0 0.7 copy-done.9
  6.7 2.1 %shard_map.82 = (bf16[784,256]{1,0:T(8,128)(2,1)S(1)}, bf16[784,256]{1,0:T(8,128)(2,1)S(1)}, f32[3,16,256]{2,1,0:T(8,128)S(1)}, f32[128,256]{1,0:T(8,128)S(1)}, ...) custom-call(f32[1,4,16,256]{3,2,1,0:T(8,128)S(1)} %copy-done.6, bf16[1,4,256,256]{3,2,1,0:T(8,128)(2,1)S(1)} %copy-done.5, ...), custom_call_target="tpu_custom_call" | custom-call | tf_op jit(solution)/shard_map/pallas_call | solution.py:201
  8.8 0.7 collective-permute-start
  9.5 6.6 %collective-permute-start.1 = (bf16[784,256]{1,0:T(8,128)(2,1)S(1)}, bf16[784,256]{1,0:T(8,128)(2,1)S(1)}, u32[]{:S(2)}, u32[]{:S(2)}) collective-permute-start(bf16[784,256]{1,0:T(8,128)(2,1)S(1)} %get-tuple-element.41.own), channel_id=1, source_target_pairs={{2,0},{3,1},{6,4},{7,5},{10,8},{11,9},{14,12},{15,13},{18,16},{19,... | collective-permute-start | bytes 1204232 | tf_op jit(solution)/shard_map/ppermute | solution.py:40
  16.1 1.3 %collective-permute-start.2 = (bf16[784,256]{1,0:T(8,128)(2,1)S(1)}, bf16[784,256]{1,0:T(8,128)(2,1)S(1)}, u32[]{:S(2)}, u32[]{:S(2)}) collective-permute-start(bf16[784,256]{1,0:T(8,128)(2,1)S(1)} %get-tuple-element.42), channel_id=1, source_target_pairs={{3,0},{2,1},{7,4},{6,5},{11,8},{10,9},{15,12},{14,13},{19,16},{18,... | collective-permute-start | bytes 1204232 | tf_op jit(solution)/shard_map/ppermute | solution.py:40
  17.4 0.0 collective-permute-done.r1
  17.4 4.1 %collective-permute-done.1.r2 = bf16[784,256]{1,0:T(8,128)(2,1)S(1)} collective-permute-done((bf16[784,256]{1,0:T(8,128)(2,1)S(1)}, bf16[784,256]{1,0:T(8,128)(2,1)S(1)}, u32[]{:S(2)}, u32[]{:S(2)}) %collective-permute-start.1) | collective-permute-done | bytes 401440 | tf_op jit(solution)/shard_map/ppermute | solution.py:40
  21.5 3.5 %collective-permute-done.2.r3 = bf16[784,256]{1,0:T(8,128)(2,1)S(1)} collective-permute-done((bf16[784,256]{1,0:T(8,128)(2,1)S(1)}, bf16[784,256]{1,0:T(8,128)(2,1)S(1)}, u32[]{:S(2)}, u32[]{:S(2)}) %collective-permute-start.2) | collective-permute-done | bytes 401440 | tf_op jit(solution)/shard_map/ppermute | solution.py:40
  25.0 0.6 shard_map.83
  25.6 0.7 collective-permute-start.3
  26.3 0.0 collective-permute-done.3.came
  26.3 0.3 shard_map.84
  26.6 0.7 collective-permute-start.4
  27.3 0.0 collective-permute-done.4.came
  27.3 0.3 shard_map.85
  27.6 0.7 collective-permute-start.5
  28.3 0.0 collective-permute-done.5.came
  28.3 0.3 shard_map.86
  28.6 0.7 collective-permute-start.6
  29.3 0.0 collective-permute-done.6.came
  29.3 0.3 shard_map.87
  29.6 0.7 collective-permute-start.7
  30.3 0.0 collective-permute-done.7.came
  30.3 0.3 shard_map.88
  30.6 0.7 collective-permute-start.10
  31.3 0.7 collective-permute-start.8
  32.0 0.7 collective-permute-start.9
  32.6 0.0 collective-permute-done.9.root
  32.7 0.0 collective-permute-done.8.vectors
  32.7 0.0 collective-permute-done.10.came
  32.7 0.0 copy-start.1
  32.7 0.0 copy-start.3
  32.7 1.1 shard_map.89
  33.8 0.7 collective-permute-start.11
  34.4 0.7 collective-permute-start.12
  35.1 1.3 %collective-permute-start.13 = (bf16[128,256]{1,0:T(8,128)(2,1)S(1)}, bf16[128,256]{1,0:T(8,128)(2,1)S(1)}, u32[]{:S(2)}, u32[]{:S(2)}) collective-permute-start(bf16[128,256]{1,0:T(8,128)(2,1)S(1)} %get-tuple-element.72), channel_id=1, source_target_pairs={{1,3},{5,7},{9,11},{13,15},{17,19},{21,23},{25,27},{29,31},{33,35}... | collective-permute-start | bytes 196616 | tf_op jit(solution)/shard_map/ppermute | solution.py:40
  36.4 0.0 collective-permute-done.11.a
  36.4 0.0 collective-permute-done.12.b
  36.4 76.2 %collective-permute-done.13.c = bf16[128,256]{1,0:T(8,128)(2,1)S(1)} collective-permute-done((bf16[128,256]{1,0:T(8,128)(2,1)S(1)}, bf16[128,256]{1,0:T(8,128)(2,1)S(1)}, u32[]{:S(2)}, u32[]{:S(2)}) %collective-permute-start.13) | collective-permute-done | bytes 65568 | tf_op jit(solution)/shard_map/ppermute | solution.py:40
  112.7 0.0 copy-done.1
  112.7 0.0 copy-done.3
  112.7 1.9 %shard_map.90 = f32[1,4,16,256]{3,2,1,0:T(8,128)} custom-call(bf16[1,4,256,256]{3,2,1,0:T(8,128)(2,1)S(1)} %copy-done.3, bf16[1,4,2,256,256]{4,3,2,1,0:T(8,128)(2,1)S(1)} %copy-done.1, s32[1,4]{1,0:T(1,128)S(1)} %copy-done.7, s32[1,4]{1,0:T(1,128)S(1)} %copy-done.8, f32[16,256]{1,0:T(8,128)S(1)} %get-tuple-element.39.level, ...), custom_call_target="tpu_custom_call" | custom-call | tf_op jit(solution)/shard_map/pallas_call | solution.py:423
  (8 shorter events, 0.0 us)
Async XLA Ops:
  0.0 0.7 copy-start.7
  0.0 0.7 copy-start.8
  0.7 1.2 %copy-start = (bf16[1,4,2,256,256]{4,3,2,1,0:T(8,128)(2,1)S(1)}, bf16[1,4,2,256,256]{4,3,2,1,0:T(8,128)(2,1)}, u32[]{:S(2)}) copy-start(bf16[1,4,2,256,256]{4,3,2,1,0:T(8,128)(2,1)} %ublk_in.3) | copy-start | bytes 3145732
  1.9 1.0 copy-start.2
  2.9 1.2 %copy-start.4 = (bf16[1,4,2,256,256]{4,3,2,1,0:T(8,128)(2,1)S(1)}, bf16[1,4,2,256,256]{4,3,2,1,0:T(8,128)(2,1)}, u32[]{:S(2)}) copy-start(bf16[1,4,2,256,256]{4,3,2,1,0:T(8,128)(2,1)} %lblk_in.1) | copy-start | bytes 3145732
  4.2 1.0 copy-start.5
  5.2 0.8 copy-start.6
  6.0 0.7 copy-start.9
  8.8 8.6 %collective-permute-start = (bf16[784,256]{1,0:T(8,128)(2,1)S(1)}, bf16[784,256]{1,0:T(8,128)(2,1)S(1)}, u32[]{:S(2)}, u32[]{:S(2)}) collective-permute-start(bf16[784,256]{1,0:T(8,128)(2,1)S(1)} %get-tuple-element.42), channel_id=1, source_target_pairs={{1,0},{0,1},{5,4},{4,5},{9,8},{8,9},{13,12},{12,13},{17,16},{16,17... | collective-permute-start | bytes 1204232 | tf_op jit(solution)/shard_map/ppermute | solution.py:40
  9.5 12.0 %collective-permute-start.1 = (bf16[784,256]{1,0:T(8,128)(2,1)S(1)}, bf16[784,256]{1,0:T(8,128)(2,1)S(1)}, u32[]{:S(2)}, u32[]{:S(2)}) collective-permute-start(bf16[784,256]{1,0:T(8,128)(2,1)S(1)} %get-tuple-element.41.own), channel_id=1, source_target_pairs={{2,0},{3,1},{6,4},{7,5},{10,8},{11,9},{14,12},{15,13},{18,16},{19,... | collective-permute-start | bytes 1204232 | tf_op jit(solution)/shard_map/ppermute | solution.py:40
  16.1 8.9 %collective-permute-start.2 = (bf16[784,256]{1,0:T(8,128)(2,1)S(1)}, bf16[784,256]{1,0:T(8,128)(2,1)S(1)}, u32[]{:S(2)}, u32[]{:S(2)}) collective-permute-start(bf16[784,256]{1,0:T(8,128)(2,1)S(1)} %get-tuple-element.42), channel_id=1, source_target_pairs={{3,0},{2,1},{7,4},{6,5},{11,8},{10,9},{15,12},{14,13},{19,16},{18,... | collective-permute-start | bytes 1204232 | tf_op jit(solution)/shard_map/ppermute | solution.py:40
  25.6 0.7 collective-permute-start.3
  26.6 0.7 collective-permute-start.4
  27.6 0.7 collective-permute-start.5
  28.6 0.7 collective-permute-start.6
  29.6 0.7 collective-permute-start.7
  30.6 2.1 %collective-permute-start.10 = (bf16[256,256]{1,0:T(8,128)(2,1)S(1)}, bf16[256,256]{1,0:T(8,128)(2,1)S(1)}, u32[]{:S(2)}, u32[]{:S(2)}) collective-permute-start(bf16[256,256]{1,0:T(8,128)(2,1)S(1)} %slice.3), channel_id=1, source_target_pairs={{1,131},{5,135},{9,139},{13,143},{17,147},{21,151},{25,155},{29,15... | collective-permute-start | bytes 393224 | tf_op jit(solution)/shard_map/ppermute | solution.py:40
  31.3 1.4 %collective-permute-start.8 = (bf16[144,256]{1,0:T(8,128)(2,1)S(1)}, bf16[144,256]{1,0:T(8,128)(2,1)S(1)}, u32[]{:S(2)}, u32[]{:S(2)}) collective-permute-start(bf16[144,256]{1,0:T(8,128)(2,1)S(1)} %get-tuple-element.73), channel_id=1, source_target_pairs={{0,1},{4,5},{8,9},{12,13},{16,17},{20,21},{24,25},{28,29},{32,33},... | collective-permute-start | bytes 221192 | tf_op jit(solution)/shard_map/ppermute | solution.py:40
  32.0 0.7 collective-permute-start.9
  32.7 80.0 %copy-start.1 = (bf16[1,4,2,256,256]{4,3,2,1,0:T(8,128)(2,1)S(1)}, bf16[1,4,2,256,256]{4,3,2,1,0:T(8,128)(2,1)}, u32[]{:S(2)}) copy-start(bf16[1,4,2,256,256]{4,3,2,1,0:T(8,128)(2,1)} %ublk_in.3) | copy-start | bytes 3145732
  32.7 80.0 %copy-start.3 = (bf16[1,4,256,256]{3,2,1,0:T(8,128)(2,1)S(1)}, bf16[1,4,256,256]{3,2,1,0:T(8,128)(2,1)}, u32[]{:S(2)}) copy-start(bf16[1,4,256,256]{3,2,1,0:T(8,128)(2,1)} %uinv_in.3) | copy-start | bytes 1572868
  33.8 2.7 %collective-permute-start.11 = (bf16[128,256]{1,0:T(8,128)(2,1)S(1)}, bf16[128,256]{1,0:T(8,128)(2,1)S(1)}, u32[]{:S(2)}, u32[]{:S(2)}) collective-permute-start(bf16[128,256]{1,0:T(8,128)(2,1)S(1)} %get-tuple-element.71.own), channel_id=1, source_target_pairs={{1,0},{5,4},{9,8},{13,12},{17,16},{21,20},{25,24},{29,28},{33,32},... | collective-permute-start | bytes 196616 | tf_op jit(solution)/shard_map/ppermute | solution.py:40
  34.4 2.0 %collective-permute-start.12 = (bf16[128,256]{1,0:T(8,128)(2,1)S(1)}, bf16[128,256]{1,0:T(8,128)(2,1)S(1)}, u32[]{:S(2)}, u32[]{:S(2)}) collective-permute-start(bf16[128,256]{1,0:T(8,128)(2,1)S(1)} %get-tuple-element.72), channel_id=1, source_target_pairs={{1,2},{5,6},{9,10},{13,14},{17,18},{21,22},{25,26},{29,30},{33,34}... | collective-permute-start | bytes 196616 | tf_op jit(solution)/shard_map/ppermute | solution.py:40
  35.1 77.5 %collective-permute-start.13 = (bf16[128,256]{1,0:T(8,128)(2,1)S(1)}, bf16[128,256]{1,0:T(8,128)(2,1)S(1)}, u32[]{:S(2)}, u32[]{:S(2)}) collective-permute-start(bf16[128,256]{1,0:T(8,128)(2,1)S(1)} %get-tuple-element.72), channel_id=1, source_target_pairs={{1,3},{5,7},{9,11},{13,15},{17,19},{21,23},{25,27},{29,31},{33,35}... | collective-permute-start | bytes 196616 | tf_op jit(solution)/shard_map/ppermute | solution.py:40

commit v3 on v2

--- a/solution.py
+++ b/solution.py
@@ -20,12 +20,15 @@
 SUMS = 2 * W + RHS
 FAR_B = 3 * W
 ROWS = 3 * W + RHS
-OTHER_PAIR = UPPER
-ROLE_A = UPPER + 1
-FLAGS = UPPER + 2
+GATHERS = (1, 3, 6)
+OTHER_PAIR = {low: UPPER + k for k, low in enumerate(GATHERS)}
+ROLE_A = UPPER + len(GATHERS)
+FLAGS = ROLE_A + 1
+LEADERS = (1, 6)
 VMEM = pl.BlockSpec(memory_space=pltpu.VMEM)
 HBM = pl.BlockSpec(memory_space=pltpu.HBM)
 PARAMS = pltpu.CompilerParams(vmem_limit_bytes=24 * 1024 * 1024)
+BEGIN_PARAMS = pltpu.CompilerParams(vmem_limit_bytes=60 * 1024 * 1024)
 
 
 def seat(t):
@@ -45,12 +48,24 @@
     return [(at_seat(t, a), at_seat(t, b)) for t in firsts for a, b in moves]
 
 
-def across(level):
-    return [(t, t ^ (1 << (level - 1))) for t in range(DEVICES) if seat(t) < 2]
+def leads(t):
+    return seat(t) < 2 and t // 4 % 8 in LEADERS
+
+
+def to_leaders(distance):
+    return [(t ^ (4 * distance), t) for t in range(DEVICES) if leads(t)]
+
+
+def from_leaders(distance):
+    return [(t, t ^ (4 * distance)) for t in range(DEVICES) if leads(t) and seat(t) == 1]
+
+
+def across(mask):
+    return [(t, t ^ mask) for t in range(DEVICES) if leads(t)]
 
 
 def layers(a, b):
-    firsts = [t for t in range(DEVICES) if t % 4 == 0]
+    firsts = [t for t in range(DEVICES) if t % 4 == 0 and t // 4 % 8 in LEADERS]
     return [(at_seat(t, a), at_seat(t ^ (DEVICES // 2), b)) for t in firsts]
 
 
@@ -132,9 +147,13 @@
     for v in range(1, UPPER + 1):
         half = lax.shift_right_logical(everyone, v - 1) == lax.shift_right_logical(me, v - 1)
         flags[(v - 1) * RHS : v * RHS] = found(half & (owners == v)).astype(BF16)
-    flags[OTHER_PAIR * RHS : (OTHER_PAIR + 1) * RHS] = found(
-        (everyone == (me ^ 2)) & (owners == 1)
-    ).astype(BF16)
+    for v in GATHERS:
+        half = lax.shift_right_logical(everyone, v - 1) == (
+            lax.shift_right_logical(me, v - 1) ^ 2
+        )
+        flags[OTHER_PAIR[v] * RHS : (OTHER_PAIR[v] + 1) * RHS] = found(
+            half & (owners == v)
+        ).astype(BF16)
     flags[ROLE_A * RHS : (ROLE_A + 1) * RHS] = jnp.full(
         (RHS, W), jnp.where(place == 0, 1.0, 0.0), F32
     ).astype(BF16)
@@ -220,7 +239,7 @@
             pltpu.SMEM((1, 4), jnp.int32),
             pltpu.SemaphoreType.DMA((9,)),
         ],
-        compiler_params=PARAMS,
+        compiler_params=BEGIN_PARAMS,
     )(rights, linv, uinv, lblk, ublk, widths, far, owner)
 
 
@@ -262,11 +281,13 @@
     left[SUMS : SUMS + rows] = choose(wide, rest.astype(BF16), left[SUMS : SUMS + rows])
 
 
-def climb_low_kernel(own, r1, r2, r3, sums, flags, k1, k1q, k2, left, residues, rest, lp, lq):
-    choose_rows(flag(flags, 0), own, r1, k1, lp)
-    choose_rows(flag(flags, OTHER_PAIR), r2, r3, k1q, lq)
-    choose_rows(flag(flags, 1), lp, lq, k2, left)
-    rows = slice(SUMS, SUMS + UPPER * RHS)
+def gather_kernel(
+    height, own, r1, r2, r3, sums, flags, k1, k1q, k2, left, residues, rest, lp, lq
+):
+    choose_rows(flag(flags, height - 1), own, r1, k1, lp)
+    choose_rows(flag(flags, OTHER_PAIR[height]), r2, r3, k1q, lq)
+    choose_rows(flag(flags, height), lp, lq, k2, left)
+    rows = slice(SUMS, SUMS + sums.shape[0])
     near = sums[...] + r1[rows].astype(F32)
     other = r2[rows].astype(F32) + r3[rows].astype(F32)
     half, near = eliminate(near, k1)
@@ -279,23 +300,21 @@
     pass_on(flags, value, left)
 
 
-def climb_low(own, r1, r2, r3, sums, flags):
+def gather(height, own, came, sums, flags):
     message = jax.ShapeDtypeStruct((ROWS, W), BF16)
-    return pl.pallas_call(
-        climb_low_kernel,
+    *results, residues, rest = pl.pallas_call(
+        functools.partial(gather_kernel, height),
         in_specs=[VMEM] * 6,
         out_specs=[VMEM] * 6,
-        out_shape=[
-            message,
-            message,
-            message,
-            message,
+        out_shape=[message] * 4
+        + [
             jax.ShapeDtypeStruct((3 * RHS, W), BF16),
-            jax.ShapeDtypeStruct(((UPPER - LOW) * RHS, W), F32),
+            jax.ShapeDtypeStruct((sums.shape[0] - 2 * RHS, W), F32),
         ],
         scratch_shapes=[pltpu.VMEM((ROWS, W), BF16)] * 2,
         compiler_params=PARAMS,
-    )(own, r1, r2, r3, sums, flags)
+    )(own, *came, sums, flags)
+    return results[:3], results[3], residues, rest
 
 
 def climb_kernel(height, own, came, sums, flags, chosen, left, residue, rest):
@@ -335,22 +354,23 @@
     ).astype(BF16)
 
 
-def top_kernel(vectors, root, mine, came, flags, *refs):
-    ups, (near_out, other_out) = (refs[:-2], refs[-2:])
+def top_kernel(
+    vectors, root, mine, came, flags, u3, u3q, u4, u5, u6, u7, near_out, other_out
+):
     wide = jnp.concatenate([flag(flags, UPPER - 1)] * 16, axis=0)
     last = choose(wide, mine[2 * W : 3 * W], came[...])
-    residue = part(vectors, UPPER).astype(F32) + root[...].astype(F32)
+    residue = part(vectors, 10).astype(F32) + root[...].astype(F32)
     above = [times(residue.astype(BF16), last).astype(BF16)]
-    for v in range(UPPER - 1, LOW - 1, -1):
-        above = [separator(part(vectors, v), ups[v], above)] + above
-    for k, out in ((0, near_out), (1, other_out)):
-        out[:RHS] = separator(part(vectors, k), ups[k], above)
+    for index, up in ((9, u7), (7, u6), (6, u5), (5, u4)):
+        above = [separator(part(vectors, index), up, above)] + above
+    for index, up, out in ((3, u3, near_out), (4, u3q, other_out)):
+        out[:RHS] = separator(part(vectors, index), up, above)
         for step, value in enumerate(above, 1):
             out[step * RHS : (step + 1) * RHS] = value
 
 
-def top(vectors, root, mine, came, flags, ups):
-    known = jax.ShapeDtypeStruct((UPPER * RHS, W), BF16)
+def top(vectors, root, mine, came, flags, *ups):
+    known = jax.ShapeDtypeStruct(((UPPER - LOW) * RHS, W), BF16)
     return pl.pallas_call(
         top_kernel,
         in_specs=[VMEM] * (5 + len(ups)),
@@ -358,6 +378,44 @@
         out_shape=[known, known],
         compiler_params=PARAMS,
     )(vectors, root, mine, came, flags, *ups)
+
+
+def select_known(cases, known):
+    for test, ref in cases:
+
+        @pl.when(test)
+        def _():
+            known[...] = ref[...]
+
+
+def bottom_kernel(vectors, own, a, b, c, u1, u1q, u2, near_out, other_out, known):
+    z = lax.axis_index("col") // 4
+    first, last = LEADERS
+    select_known(
+        [
+            ((z == (first ^ k)) | (z == (last ^ k)), ref)
+            for k, ref in enumerate((own, a, b, c))
+        ],
+        known,
+    )
+    above = [part(known, k) for k in range(UPPER - LOW)]
+    above = [separator(part(vectors, 2), u2, above)] + above
+    for index, up, out in ((0, u1, near_out), (1, u1q, other_out)):
+        out[:RHS] = separator(part(vectors, index), up, above)
+        for step, value in enumerate(above, 1):
+            out[step * RHS : (step + 1) * RHS] = value
+
+
+def bottom(vectors, own, a, b, c, u1, u1q, u2):
+    known = jax.ShapeDtypeStruct((UPPER * RHS, W), BF16)
+    return pl.pallas_call(
+        bottom_kernel,
+        in_specs=[VMEM] * 8,
+        out_specs=[VMEM] * 2,
+        out_shape=[known, known],
+        scratch_shapes=[pltpu.VMEM(((UPPER - LOW) * RHS, W), BF16)],
+        compiler_params=PARAMS,
+    )(vectors, own, a, b, c, u1, u1q, u2)
 
 
 def descend_kernel(
@@ -389,12 +447,9 @@
     for copy in copies:
         copy.start()
     place = (lax.axis_index("col") % 4 + 2 * lax.axis_index("gz")) % 4
-    for seated, ref in ((0, a), (1, own), (2, b), (3, c)):
-
-        @pl.when(place == seated)
-        def _():
-            known[...] = ref[...]
-
+    select_known(
+        [(place == seated, ref) for seated, ref in enumerate((a, own, b, c))], known
+    )
     above = [part(known, k) for k in range(UPPER)]
     own_value = jnp.zeros((RHS, W), F32)
     for k, value in enumerate(above):
@@ -441,22 +496,30 @@
     first, second, solved, sums, flags, level = begin(
         rights, linv, uinv, lblk, ublk, widths, far, owner_level.reshape(1, DEVICES)
     )
-    r1 = send(second, seats(((1, 0), (0, 1))))
-    r2 = send(first, seats(((2, 0), (3, 1))))
-    r3 = send(second, seats(((3, 0), (2, 1))))
-    near, other, above, message, residues, sums = climb_low(first, r1, r2, r3, sums, flags)
-    ups = [near, other, above]
-    vectors = [residues]
-    for height in range(LOW + 1, UPPER):
-        came = send(message, across(height))
-        chosen, message, residue, sums = climb(height, message, came, sums, flags)
-        ups.append(chosen)
-        vectors.append(residue)
+    came = (
+        send(second, seats(((1, 0), (0, 1)))),
+        send(first, seats(((2, 0), (3, 1)))),
+        send(second, seats(((3, 0), (2, 1)))),
+    )
+    ups_y, message, residues_y, sums = gather(1, first, came, sums, flags)
+    came = [send(message, to_leaders(k)) for k in (1, 2, 3)]
+    ups_z, message, residues_z, sums = gather(3, message, came, sums, flags)
+    came = send(message, across(4 * (LEADERS[0] ^ LEADERS[1])))
+    up_5, message, residue_5, sums = climb(5, message, came, sums, flags)
+    came = [send(message, across(32 * k)) for k in (1, 2, 3)]
+    ups_x, message, residues_x, sums = gather(6, message, came, sums, flags)
     root = sums.astype(BF16)
     root_came = send(root, layers(0, 1))
-    vectors = send(jnp.concatenate(vectors + [root], axis=0), seats(((0, 1),)))
+    vectors = jnp.concatenate([residues_y, residues_z, residue_5, residues_x, root], axis=0)
+    vectors = send(vectors, seats(((0, 1),)))
     last_came = send(message[2 * W : 3 * W], layers(1, 1))
-    known, known_other = top(vectors, root_came, message, last_came, flags, ups)
+    known, known_other = top(
+        vectors, root_came, message, last_came, flags, *ups_z, up_5, ups_x[0], ups_x[2]
+    )
+    a = send(known, from_leaders(1))
+    b = send(known_other, from_leaders(2))
+    c = send(known_other, from_leaders(3))
+    known, known_other = bottom(vectors, known, a, b, c, *ups_y)
     a = send(known, seats(((1, 0),)))
     b = send(known_other, seats(((1, 2),)))
     c = send(known_other, seats(((1, 3),)))

time: 115 us -> 107 us (0.930); the launches traced: 115 us -> 105 us
  waiting for transfers between devices: 83.8 us -> 71.1 us
  starting transfers between devices: 16.6 us -> 20.1 us
  local copies, waits for them, and re-layouts: 6.76 us -> 3.48 us
  Pallas kernels: 7.09 us -> 9.93 us
    ppermute x14 -> x19, waiting for transfers between devices: 83.8 us -> 71.1 us  [send(): return lax.ppermute(value, AXES, pairs)]
    ppermute x14 -> x19, starting transfers between devices: 16.6 us -> 20.1 us  [send(): return lax.ppermute(value, AXES, pairs)]
    unnamed x26 -> x24, local copies, waits for them, and re-layouts: 6.75 us -> 3.47 us
    pallas_call x1 -> x4, Pallas kernels: 0.59 us -> 2.79 us  [the longest x3 2.41 us: gather(): pl.pallas_call(functools.partial(gather_kernel, height), in_specs=[VMEM]...]
    pallas_call x1, Pallas kernels: 2.08 us -> 4.1 us  [begin(): pl.pallas_call(begin_kernel, in_specs=[HBM] * 7 + [VMEM], out_specs=[VMEM...]
  transfers between devices with their start and end apart: 14 -> 19, of which waited for: 3 -> 3; matrix products, arithmetic and copies ran while one was open for 0% -> 0% of each run, Pallas kernels for 0% -> 0%
where the time goes in v3:
time: 107 us; the launch traced here: 105 us
  waiting for transfers between devices  71.1 us (66%)
  starting transfers between devices  20.1 us (19%)
  Pallas kernels  9.93 us (9%)
  local copies, waits for them, and re-layouts  3.48 us (3%)
    ppermute x19, waiting for transfers between devices, send(): return lax.ppermute(value, AXES, pairs)  71.1 us
    ppermute x19, starting transfers between devices, send(): return lax.ppermute(value, AXES, pairs)  20.1 us
    pallas_call x1, Pallas kernels, begin(): pl.pallas_call(begin_kernel, in_specs=[HBM] * 7 + [VMEM], out_specs=[VMEM...  4.1 us
    unnamed x24, local copies, waits for them, and re-layouts  3.47 us
    pallas_call x3, Pallas kernels, gather(): pl.pallas_call(functools.partial(gather_kernel, height), in_specs=[VMEM]...  2.41 us
  transfers between devices with their start and end apart: 19, of which 3 were waited for; matrix products, arithmetic and copies ran while one was open for 0% of the time, Pallas kernels for 0%

profile of v3, /device:TPU:24, one launch (start us, length us, event | category | flops | bytes accessed | tf_op | source)
XLA Modules:
  0.0 105.1 jit_solution(14896066549141882701)
XLA Ops:
  0.0 4.1 %shard_map.82 = (bf16[784,256]{1,0:T(8,128)(2,1)}, bf16[784,256]{1,0:T(8,128)(2,1)}, f32[3,16,256]{2,1,0:T(8,128)}, f32[128,256]{1,0:T(8,128)}, bf16[192,256]{1,0:T(8,128)(2,1)}, /*index=5*/f32[16,256]{1,0:T(8,128)}) custom-call(f32[1,4,16,256]{3,2,1,0:T(8,128)} %rights_in.1, bf16[1,4,256,256]{3,2,1,0:T(8,128)(2,1)} %linv_in.1, ...), custom_call_target="tpu_custom_call" | custom-call | tf_op jit(solution)/shard_map/pallas_call | solution.py:220
  4.1 0.7 collective-permute-start
  4.8 6.6 %collective-permute-start.1 = (bf16[784,256]{1,0:T(8,128)(2,1)}, bf16[784,256]{1,0:T(8,128)(2,1)S(1)}, u32[]{:S(2)}, u32[]{:S(2)}) collective-permute-start(bf16[784,256]{1,0:T(8,128)(2,1)} %get-tuple-element.38.own), channel_id=1, source_target_pairs={{2,0},{3,1},{6,4},{7,5},{10,8},{11,9},{14,12},{15,13},{18,16},{19,... | collective-permute-start | bytes 1204232 | tf_op jit(solution)/shard_map/ppermute | solution.py:43
  11.4 1.3 %collective-permute-start.2 = (bf16[784,256]{1,0:T(8,128)(2,1)}, bf16[784,256]{1,0:T(8,128)(2,1)S(1)}, u32[]{:S(2)}, u32[]{:S(2)}) collective-permute-start(bf16[784,256]{1,0:T(8,128)(2,1)} %get-tuple-element.39), channel_id=1, source_target_pairs={{3,0},{2,1},{7,4},{6,5},{11,8},{10,9},{15,12},{14,13},{19,16},{18,... | collective-permute-start | bytes 1204232 | tf_op jit(solution)/shard_map/ppermute | solution.py:43
  12.7 0.0 collective-permute-done.r1
  12.7 4.4 %collective-permute-done.1.r2 = bf16[784,256]{1,0:T(8,128)(2,1)S(1)} collective-permute-done((bf16[784,256]{1,0:T(8,128)(2,1)}, bf16[784,256]{1,0:T(8,128)(2,1)S(1)}, u32[]{:S(2)}, u32[]{:S(2)}) %collective-permute-start.1) | collective-permute-done | bytes 401440 | tf_op jit(solution)/shard_map/ppermute | solution.py:43
  17.1 3.5 %collective-permute-done.2.r3 = bf16[784,256]{1,0:T(8,128)(2,1)S(1)} collective-permute-done((bf16[784,256]{1,0:T(8,128)(2,1)}, bf16[784,256]{1,0:T(8,128)(2,1)S(1)}, u32[]{:S(2)}, u32[]{:S(2)}) %collective-permute-start.2) | collective-permute-done | bytes 401440 | tf_op jit(solution)/shard_map/ppermute | solution.py:43
  20.6 0.0 copy-start.1
  20.6 0.9 copy-done.1
  21.5 0.0 copy-start.4
  21.5 1.0 copy-done.4
  22.5 0.0 copy-start.5
  22.5 0.9 copy-done.5
  23.4 0.0 copy-start.2
  23.4 0.6 shard_map.83
  24.0 0.7 collective-permute-start.3
  24.7 0.7 collective-permute-start.4
  25.4 0.7 collective-permute-start.5
  26.1 0.0 collective-permute-done.3.r1
  26.1 0.0 collective-permute-done.4.r2
  26.1 0.0 collective-permute-done.5.r3
  26.1 0.0 copy-done.2
  26.1 0.6 shard_map.84
  26.7 0.7 collective-permute-start.6
  27.4 0.0 collective-permute-done.6.came
  27.4 0.3 shard_map.85
  27.7 0.7 collective-permute-start.7
  28.4 0.7 collective-permute-start.8
  29.1 0.7 collective-permute-start.9
  29.8 0.0 collective-permute-done.7.r1
  29.8 0.0 collective-permute-done.8.r2
  29.8 0.0 collective-permute-done.9.r3
  29.9 1.2 %shard_map.86 = (bf16[784,256]{1,0:T(8,128)(2,1)S(1)}, bf16[784,256]{1,0:T(8,128)(2,1)}, bf16[784,256]{1,0:T(8,128)(2,1)S(1)}, bf16[784,256]{1,0:T(8,128)(2,1)S(...) custom-call(bf16[784,256]{1,0:T(8,128)(2,1)S(1)} %get-tuple-element.49.own, ...), custom_call_target="tpu_custom_call" | custom-call | tf_op jit(solution)/shard_map/pallas_call | solution.py:305
  31.1 0.7 collective-permute-start.12
  31.8 0.7 collective-permute-start.10
  32.5 0.7 collective-permute-start.11
  33.2 0.0 collective-permute-done.11.root
  33.2 0.0 collective-permute-done.10.vectors
  33.2 0.0 collective-permute-done.12.came
  33.2 0.0 copy-start.3
  33.2 0.8 shard_map.87
  34.0 0.0 copy-start
  34.0 0.8 collective-permute-start.13
  34.8 0.7 collective-permute-start.14
  35.5 0.7 collective-permute-start.15
  36.2 0.0 collective-permute-done.13.a
  36.2 0.0 collective-permute-done.14.b
  36.2 0.0 collective-permute-done.15.c
  36.2 0.0 copy-start.6
  36.2 0.0 copy-start.7
  36.2 0.4 shard_map.88
  36.6 0.7 collective-permute-start.16
  37.3 0.7 collective-permute-start.17
  38.0 1.3 %collective-permute-start.18 = (bf16[128,256]{1,0:T(8,128)(2,1)S(1)}, bf16[128,256]{1,0:T(8,128)(2,1)S(1)}, u32[]{:S(2)}, u32[]{:S(2)}) collective-permute-start(bf16[128,256]{1,0:T(8,128)(2,1)S(1)} %get-tuple-element.66), channel_id=1, source_target_pairs={{1,3},{5,7},{9,11},{13,15},{17,19},{21,23},{25,27},{29,31},{33,35}... | collective-permute-start | bytes 196616 | tf_op jit(solution)/shard_map/ppermute | solution.py:43
  39.3 0.0 collective-permute-done.16.a
  39.3 0.0 collective-permute-done.17.b
  39.3 63.2 %collective-permute-done.18.c = bf16[128,256]{1,0:T(8,128)(2,1)S(1)} collective-permute-done((bf16[128,256]{1,0:T(8,128)(2,1)S(1)}, bf16[128,256]{1,0:T(8,128)(2,1)S(1)}, u32[]{:S(2)}, u32[]{:S(2)}) %collective-permute-start.18) | collective-permute-done | bytes 65568 | tf_op jit(solution)/shard_map/ppermute | solution.py:43
  102.5 0.0 copy-done.3
  102.5 0.0 copy-done
  102.5 0.0 copy-done.6
  102.5 0.0 copy-done.7
  102.5 0.6 copy-done.8
  103.1 0.0 copy-done.9
  103.1 1.9 %shard_map.89 = f32[1,4,16,256]{3,2,1,0:T(8,128)} custom-call(bf16[1,4,256,256]{3,2,1,0:T(8,128)(2,1)S(1)} %copy-done.3, bf16[1,4,2,256,256]{4,3,2,1,0:T(8,128)(2,1)S(1)} %copy-done, s32[1,4]{1,0:T(1,128)S(1)} %copy-done.8, s32[1,4]{1,0:T(1,128)S(1)} %copy-done.9, f32[16,256]{1,0:T(8,128)S(1)} %copy-done.7, f32[3,16,256]{2,1,0:T(8,128)S(1)} %copy-done.6, ...), custom_call_target="tpu_custom_call" | custom-call | tf_op jit(solution)/shard_map/pallas_call | solution.py:478
  (8 shorter events, 0.0 us)
Async XLA Ops:
  4.1 8.6 %collective-permute-start = (bf16[784,256]{1,0:T(8,128)(2,1)}, bf16[784,256]{1,0:T(8,128)(2,1)S(1)}, u32[]{:S(2)}, u32[]{:S(2)}) collective-permute-start(bf16[784,256]{1,0:T(8,128)(2,1)} %get-tuple-element.39), channel_id=1, source_target_pairs={{1,0},{0,1},{5,4},{4,5},{9,8},{8,9},{13,12},{12,13},{17,16},{16,17... | collective-permute-start | bytes 1204232 | tf_op jit(solution)/shard_map/ppermute | solution.py:43
  4.8 12.3 %collective-permute-start.1 = (bf16[784,256]{1,0:T(8,128)(2,1)}, bf16[784,256]{1,0:T(8,128)(2,1)S(1)}, u32[]{:S(2)}, u32[]{:S(2)}) collective-permute-start(bf16[784,256]{1,0:T(8,128)(2,1)} %get-tuple-element.38.own), channel_id=1, source_target_pairs={{2,0},{3,1},{6,4},{7,5},{10,8},{11,9},{14,12},{15,13},{18,16},{19,... | collective-permute-start | bytes 1204232 | tf_op jit(solution)/shard_map/ppermute | solution.py:43
  11.4 9.3 %collective-permute-start.2 = (bf16[784,256]{1,0:T(8,128)(2,1)}, bf16[784,256]{1,0:T(8,128)(2,1)S(1)}, u32[]{:S(2)}, u32[]{:S(2)}) collective-permute-start(bf16[784,256]{1,0:T(8,128)(2,1)} %get-tuple-element.39), channel_id=1, source_target_pairs={{3,0},{2,1},{7,4},{6,5},{11,8},{10,9},{15,12},{14,13},{19,16},{18,... | collective-permute-start | bytes 1204232 | tf_op jit(solution)/shard_map/ppermute | solution.py:43
  20.6 0.9 copy-start.1
  21.5 1.0 copy-start.4
  22.5 0.9 copy-start.5
  23.4 2.7 %copy-start.2 = (bf16[192,256]{1,0:T(8,128)(2,1)S(1)}, bf16[192,256]{1,0:T(8,128)(2,1)}, u32[]{:S(2)}) copy-start(bf16[192,256]{1,0:T(8,128)(2,1)} %get-tuple-element.41.flags) | copy-start | bytes 294916
  24.0 2.1 %collective-permute-start.3 = (bf16[784,256]{1,0:T(8,128)(2,1)S(1)}, bf16[784,256]{1,0:T(8,128)(2,1)S(1)}, u32[]{:S(2)}, u32[]{:S(2)}) collective-permute-start(bf16[784,256]{1,0:T(8,128)(2,1)S(1)} %get-tuple-element.43.own), channel_id=1, source_target_pairs={{0,4},{1,5},{28,24},{29,25},{32,36},{33,37},{60,56},{61,57},{64,68... | collective-permute-start | bytes 1204232 | tf_op jit(solution)/shard_map/ppermute | solution.py:43
  24.7 1.4 %collective-permute-start.4 = (bf16[784,256]{1,0:T(8,128)(2,1)S(1)}, bf16[784,256]{1,0:T(8,128)(2,1)S(1)}, u32[]{:S(2)}, u32[]{:S(2)}) collective-permute-start(bf16[784,256]{1,0:T(8,128)(2,1)S(1)} %get-tuple-element.43.own), channel_id=1, source_target_pairs={{12,4},{13,5},{16,24},{17,25},{44,36},{45,37},{48,56},{49,57},{76,... | collective-permute-start | bytes 1204232 | tf_op jit(solution)/shard_map/ppermute | solution.py:43
  25.4 0.7 collective-permute-start.5
  26.7 0.7 collective-permute-start.6
  27.7 2.1 %collective-permute-start.7 = (bf16[784,256]{1,0:T(8,128)(2,1)S(1)}, bf16[784,256]{1,0:T(8,128)(2,1)S(1)}, u32[]{:S(2)}, u32[]{:S(2)}) collective-permute-start(bf16[784,256]{1,0:T(8,128)(2,1)S(1)} %get-tuple-element.49.own), channel_id=1, source_target_pairs={{4,36},{5,37},{24,56},{25,57},{36,4},{37,5},{56,24},{57,25},{68,10... | collective-permute-start | bytes 1204232 | tf_op jit(solution)/shard_map/ppermute | solution.py:43
  28.4 1.4 %collective-permute-start.8 = (bf16[784,256]{1,0:T(8,128)(2,1)S(1)}, bf16[784,256]{1,0:T(8,128)(2,1)S(1)}, u32[]{:S(2)}, u32[]{:S(2)}) collective-permute-start(bf16[784,256]{1,0:T(8,128)(2,1)S(1)} %get-tuple-element.49.own), channel_id=1, source_target_pairs={{4,68},{5,69},{24,88},{25,89},{36,100},{37,101},{56,120},{57,121},... | collective-permute-start | bytes 1204232 | tf_op jit(solution)/shard_map/ppermute | solution.py:43
  29.1 0.8 collective-permute-start.9
  31.1 2.1 %collective-permute-start.12 = (bf16[256,256]{1,0:T(8,128)(2,1)S(1)}, bf16[256,256]{1,0:T(8,128)(2,1)S(1)}, u32[]{:S(2)}, u32[]{:S(2)}) collective-permute-start(bf16[256,256]{1,0:T(8,128)(2,1)S(1)} %slice.3), channel_id=1, source_target_pairs={{5,135},{25,155},{37,167},{57,187},{69,199},{89,219},{101,231},{12... | collective-permute-start | bytes 393224 | tf_op jit(solution)/shard_map/ppermute | solution.py:43
  31.8 1.4 %collective-permute-start.10 = (bf16[176,256]{1,0:T(8,128)(2,1)S(1)}, bf16[176,256]{1,0:T(8,128)(2,1)S(1)}, u32[]{:S(2)}, u32[]{:S(2)}) collective-permute-start(bf16[176,256]{1,0:T(8,128)(2,1)S(1)} %get-tuple-element.67), channel_id=1, source_target_pairs={{0,1},{4,5},{8,9},{12,13},{16,17},{20,21},{24,25},{28,29},{32,33},... | collective-permute-start | bytes 270344 | tf_op jit(solution)/shard_map/ppermute | solution.py:43
  32.5 0.7 collective-permute-start.11
  33.2 69.3 %copy-start.3 = (bf16[1,4,256,256]{3,2,1,0:T(8,128)(2,1)S(1)}, bf16[1,4,256,256]{3,2,1,0:T(8,128)(2,1)}, u32[]{:S(2)}) copy-start(bf16[1,4,256,256]{3,2,1,0:T(8,128)(2,1)} %uinv_in.3) | copy-start | bytes 1572868
  34.0 68.5 %copy-start = (bf16[1,4,2,256,256]{4,3,2,1,0:T(8,128)(2,1)S(1)}, bf16[1,4,2,256,256]{4,3,2,1,0:T(8,128)(2,1)}, u32[]{:S(2)}) copy-start(bf16[1,4,2,256,256]{4,3,2,1,0:T(8,128)(2,1)} %ublk_in.3) | copy-start | bytes 3145732
  34.0 2.2 %collective-permute-start.13 = (bf16[96,256]{1,0:T(8,128)(2,1)S(1)}, bf16[96,256]{1,0:T(8,128)(2,1)S(1)}, u32[]{:S(2)}, u32[]{:S(2)}) collective-permute-start(bf16[96,256]{1,0:T(8,128)(2,1)S(1)} %get-tuple-element.60.own), channel_id=1, source_target_pairs={{5,1},{25,29},{37,33},{57,61},{69,65},{89,93},{101,97},{121,125},{... | collective-permute-start | bytes 147464 | tf_op jit(solution)/shard_map/ppermute | solution.py:43
  34.8 1.4 %collective-permute-start.14 = (bf16[96,256]{1,0:T(8,128)(2,1)S(1)}, bf16[96,256]{1,0:T(8,128)(2,1)S(1)}, u32[]{:S(2)}, u32[]{:S(2)}) collective-permute-start(bf16[96,256]{1,0:T(8,128)(2,1)S(1)} %get-tuple-element.61), channel_id=1, source_target_pairs={{5,13},{25,17},{37,45},{57,49},{69,77},{89,81},{101,109},{121,113}... | collective-permute-start | bytes 147464 | tf_op jit(solution)/shard_map/ppermute | solution.py:43
  35.5 0.7 collective-permute-start.15
  36.2 66.3 %copy-start.6 = (f32[3,16,256]{2,1,0:T(8,128)S(1)}, f32[3,16,256]{2,1,0:T(8,128)}, u32[]{:S(2)}) copy-start(f32[3,16,256]{2,1,0:T(8,128)} %get-tuple-element.37.solved) | copy-start | bytes 147460
  36.2 66.3 %copy-start.7 = (f32[16,256]{1,0:T(8,128)S(1)}, f32[16,256]{1,0:T(8,128)}, u32[]{:S(2)}) copy-start(f32[16,256]{1,0:T(8,128)} %get-tuple-element.36.level) | copy-start | bytes 49156
  36.6 2.7 %collective-permute-start.16 = (bf16[128,256]{1,0:T(8,128)(2,1)S(1)}, bf16[128,256]{1,0:T(8,128)(2,1)S(1)}, u32[]{:S(2)}, u32[]{:S(2)}) collective-permute-start(bf16[128,256]{1,0:T(8,128)(2,1)S(1)} %get-tuple-element.65.own), channel_id=1, source_target_pairs={{1,0},{5,4},{9,8},{13,12},{17,16},{21,20},{25,24},{29,28},{33,32},... | collective-permute-start | bytes 196616 | tf_op jit(solution)/shard_map/ppermute | solution.py:43
  37.3 2.0 %collective-permute-start.17 = (bf16[128,256]{1,0:T(8,128)(2,1)S(1)}, bf16[128,256]{1,0:T(8,128)(2,1)S(1)}, u32[]{:S(2)}, u32[]{:S(2)}) collective-permute-start(bf16[128,256]{1,0:T(8,128)(2,1)S(1)} %get-tuple-element.66), channel_id=1, source_target_pairs={{1,2},{5,6},{9,10},{13,14},{17,18},{21,22},{25,26},{29,30},{33,34}... | collective-permute-start | bytes 196616 | tf_op jit(solution)/shard_map/ppermute | solution.py:43
  38.0 64.5 %collective-permute-start.18 = (bf16[128,256]{1,0:T(8,128)(2,1)S(1)}, bf16[128,256]{1,0:T(8,128)(2,1)S(1)}, u32[]{:S(2)}, u32[]{:S(2)}) collective-permute-start(bf16[128,256]{1,0:T(8,128)(2,1)S(1)} %get-tuple-element.66), channel_id=1, source_target_pairs={{1,3},{5,7},{9,11},{13,15},{17,19},{21,23},{25,27},{29,31},{33,35}... | collective-permute-start | bytes 196616 | tf_op jit(solution)/shard_map/ppermute | solution.py:43
  102.5 0.7 copy-start.8
  102.5 0.7 copy-start.9

commit v4 on v3

--- a/solution.py
+++ b/solution.py
@@ -24,11 +24,10 @@
 OTHER_PAIR = {low: UPPER + k for k, low in enumerate(GATHERS)}
 ROLE_A = UPPER + len(GATHERS)
 FLAGS = ROLE_A + 1
-LEADERS = (1, 6)
+LEADERS = (2, 5)
 VMEM = pl.BlockSpec(memory_space=pltpu.VMEM)
 HBM = pl.BlockSpec(memory_space=pltpu.HBM)
 PARAMS = pltpu.CompilerParams(vmem_limit_bytes=24 * 1024 * 1024)
-BEGIN_PARAMS = pltpu.CompilerParams(vmem_limit_bytes=60 * 1024 * 1024)
 
 
 def seat(t):
@@ -95,13 +94,14 @@
     ublk_in,
     widths_in,
     far_in,
-    owner,
+    owner_in,
     first,
     second,
     solved,
     sums,
     flags,
     level,
+    slots,
     rights,
     linv,
     uinv,
@@ -109,6 +109,7 @@
     ublk,
     widths,
     far,
+    owner,
     sems,
 ):
     own = pl.ds(LOCAL_COUNT, 1)
@@ -117,6 +118,8 @@
         pltpu.make_async_copy(widths_in, widths, sems.at[0]),
         pltpu.make_async_copy(far_in, far, sems.at[1]),
     ]
+    owner_copy = pltpu.make_async_copy(owner_in, owner, sems.at[9])
+    owner_copy.start()
     mine = [
         pltpu.make_async_copy(linv_in.at[0, own], linv.at[own], sems.at[2]),
         pltpu.make_async_copy(lblk_in.at[0, own], lblk.at[own], sems.at[3]),
@@ -136,6 +139,7 @@
     y = col % 4
     place = (y + 2 * gz) % 4
     everyone = lax.broadcasted_iota(jnp.int32, (1, DEVICES), 1)
+    owner_copy.wait()
     owners = owner[...]
 
     def spread(value):
@@ -179,10 +183,13 @@
         residue = rights[slot]
         if slot == LOCAL_COUNT - 1:
             residue = residue - pending
-        forward = jnp.where(
-            row_pad(widths[0, slot]), times_rows(residue.astype(BF16), linv[slot]), 0.0
-        )
+        inside = jnp.broadcast_to(row_pad(widths[0, slot]), (RHS, W))
+        forward = jnp.where(inside, times_rows(residue.astype(BF16), linv[slot]), 0.0)
         solved[slot] = forward
+        slots[slot * RHS : (slot + 1) * RHS] = jnp.where(inside, 1.0, 0.0)
+        slots[(LOCAL_COUNT + slot) * RHS : (LOCAL_COUNT + slot + 1) * RHS] = jnp.full(
+            (RHS, W), far[0, slot], jnp.int32
+        ).astype(F32)
         half = forward.astype(BF16)
         near = times_rows(half, lblk[slot, 0])
         away = times_rows(half, lblk[slot, 1])
@@ -219,8 +226,8 @@
 def begin(rights, linv, uinv, lblk, ublk, widths, far, owner):
     return pl.pallas_call(
         begin_kernel,
-        in_specs=[HBM] * 7 + [VMEM],
-        out_specs=[VMEM] * 6,
+        in_specs=[HBM] * 8,
+        out_specs=[VMEM] * 7,
         out_shape=[
             jax.ShapeDtypeStruct((ROWS, W), BF16),
             jax.ShapeDtypeStruct((ROWS, W), BF16),
@@ -228,6 +235,7 @@
             jax.ShapeDtypeStruct((UPPER * RHS, W), F32),
             jax.ShapeDtypeStruct((FLAGS * RHS, W), BF16),
             jax.ShapeDtypeStruct((RHS, W), F32),
+            jax.ShapeDtypeStruct((2 * LOCAL_COUNT * RHS, W), F32),
         ],
         scratch_shapes=[
             pltpu.VMEM((4, RHS, W), F32),
@@ -237,10 +245,16 @@
             pltpu.VMEM((1, 2, W, W), BF16),
             pltpu.SMEM((1, 4), jnp.int32),
             pltpu.SMEM((1, 4), jnp.int32),
-            pltpu.SemaphoreType.DMA((9,)),
+            pltpu.VMEM((1, DEVICES), jnp.int32),
+            pltpu.SemaphoreType.DMA((10,)),
         ],
-        compiler_params=BEGIN_PARAMS,
-    )(rights, linv, uinv, lblk, ublk, widths, far, owner)
+        compiler_params=PARAMS,
+    )(
+        *[
+            pltpu.with_memory_space_constraint(value, pltpu.HBM)
+            for value in (rights, linv, uinv, lblk, ublk, widths, far, owner)
+        ]
+    )
 
 
 def flag(flags, index):
@@ -282,7 +296,7 @@
 
 
 def gather_kernel(
-    height, own, r1, r2, r3, sums, flags, k1, k1q, k2, left, residues, rest, lp, lq
+    height, own, r1, r2, r3, sums, flags, left, residues, rest, k1, k2, k1q, lp, lq
 ):
     choose_rows(flag(flags, height - 1), own, r1, k1, lp)
     choose_rows(flag(flags, OTHER_PAIR[height]), r2, r3, k1q, lq)
@@ -300,21 +314,23 @@
     pass_on(flags, value, left)
 
 
-def gather(height, own, came, sums, flags):
+def gather(height, own, came, sums, flags, both=True):
     message = jax.ShapeDtypeStruct((ROWS, W), BF16)
-    *results, residues, rest = pl.pallas_call(
+    kept = 3 if both else 2
+    left, residues, rest, *ups = pl.pallas_call(
         functools.partial(gather_kernel, height),
         in_specs=[VMEM] * 6,
-        out_specs=[VMEM] * 6,
-        out_shape=[message] * 4
-        + [
+        out_specs=[VMEM] * (3 + kept),
+        out_shape=[
+            message,
             jax.ShapeDtypeStruct((3 * RHS, W), BF16),
             jax.ShapeDtypeStruct((sums.shape[0] - 2 * RHS, W), F32),
-        ],
-        scratch_shapes=[pltpu.VMEM((ROWS, W), BF16)] * 2,
+        ]
+        + [message] * kept,
+        scratch_shapes=[pltpu.VMEM((ROWS, W), BF16)] * (5 - kept),
         compiler_params=PARAMS,
     )(own, *came, sums, flags)
-    return results[:3], results[3], residues, rest
+    return ups, left, residues, rest
 
 
 def climb_kernel(height, own, came, sums, flags, chosen, left, residue, rest):
@@ -355,7 +371,7 @@
 
 
 def top_kernel(
-    vectors, root, mine, came, flags, u3, u3q, u4, u5, u6, u7, near_out, other_out
+    vectors, root, mine, came, flags, u3, u4, u3q, u5, u6, u7, near_out, other_out
 ):
     wide = jnp.concatenate([flag(flags, UPPER - 1)] * 16, axis=0)
     last = choose(wide, mine[2 * W : 3 * W], came[...])
@@ -388,7 +404,7 @@
             known[...] = ref[...]
 
 
-def bottom_kernel(vectors, own, a, b, c, u1, u1q, u2, near_out, other_out, known):
+def bottom_kernel(vectors, own, a, b, c, u1, u2, u1q, near_out, other_out, known):
     z = lax.axis_index("col") // 4
     first, last = LEADERS
     select_known(
@@ -406,7 +422,7 @@
             out[step * RHS : (step + 1) * RHS] = value
 
 
-def bottom(vectors, own, a, b, c, u1, u1q, u2):
+def bottom(vectors, own, a, b, c, u1, u2, u1q):
     known = jax.ShapeDtypeStruct((UPPER * RHS, W), BF16)
     return pl.pallas_call(
         bottom_kernel,
@@ -415,37 +431,10 @@
         out_shape=[known, known],
         scratch_shapes=[pltpu.VMEM(((UPPER - LOW) * RHS, W), BF16)],
         compiler_params=PARAMS,
-    )(vectors, own, a, b, c, u1, u1q, u2)
-
-
-def descend_kernel(
-    uinv_in,
-    ublk_in,
-    widths_in,
-    far_in,
-    level,
-    solved,
-    own,
-    a,
-    b,
-    c,
-    out,
-    uinv,
-    ublk,
-    widths,
-    far,
-    known,
-    sems,
-):
-    rest = pl.ds(0, LOCAL_COUNT)
-    copies = [
-        pltpu.make_async_copy(widths_in, widths, sems.at[0]),
-        pltpu.make_async_copy(far_in, far, sems.at[1]),
-        pltpu.make_async_copy(uinv_in.at[0, rest], uinv, sems.at[2]),
-        pltpu.make_async_copy(ublk_in.at[0, rest], ublk, sems.at[3]),
-    ]
-    for copy in copies:
-        copy.start()
+    )(vectors, own, a, b, c, u1, u2, u1q)
+
+
+def descend_kernel(uinv, ublk, slots, level, solved, own, a, b, c, out, known):
     place = (lax.axis_index("col") % 4 + 2 * lax.axis_index("gz")) % 4
     select_known(
         [(place == seated, ref) for seated, ref in enumerate((a, own, b, c))], known
@@ -453,47 +442,39 @@
     above = [part(known, k) for k in range(UPPER)]
     own_value = jnp.zeros((RHS, W), F32)
     for k, value in enumerate(above):
-        own_value = jnp.where(level[...] == k + 1, value.astype(F32), own_value)
+        own_value = jnp.where(level[...] == float(k + 1), value.astype(F32), own_value)
     out[0, LOCAL_COUNT] = own_value
-    for copy in copies:
-        copy.wait()
     for slot in (2, 1, 0):
+        distance = part(slots, LOCAL_COUNT + slot)
         distant = jnp.zeros((RHS, W), F32)
         for step, value in enumerate(above, 1):
-            distant = distant + jnp.where(far[0, slot] == step, value.astype(F32), 0.0)
+            distant = distant + jnp.where(distance == float(step), value.astype(F32), 0.0)
         residue = (
             solved[slot]
-            - times_rows(above[0], ublk[slot, 0])
-            - times_rows(distant.astype(BF16), ublk[slot, 1])
+            - times_rows(above[0], ublk[0, slot, 0])
+            - times_rows(distant.astype(BF16), ublk[0, slot, 1])
         )
         value = jnp.where(
-            row_pad(widths[0, slot]), times_rows(residue.astype(BF16), uinv[slot]), 0.0
+            part(slots, slot) > 0.5, times_rows(residue.astype(BF16), uinv[0, slot]), 0.0
         )
         out[0, slot] = value
         if slot == 2:
             above = [value.astype(BF16)] + above
 
 
-def descend(uinv, ublk, widths, far, level, solved, own, a, b, c):
+def descend(uinv, ublk, slots, level, solved, own, a, b, c):
     return pl.pallas_call(
         descend_kernel,
-        in_specs=[HBM] * 4 + [VMEM] * 6,
+        in_specs=[VMEM] * 9,
         out_specs=VMEM,
         out_shape=jax.ShapeDtypeStruct((1, 4, RHS, W), F32),
-        scratch_shapes=[
-            pltpu.VMEM((LOCAL_COUNT, W, W), BF16),
-            pltpu.VMEM((LOCAL_COUNT, 2, W, W), BF16),
-            pltpu.SMEM((1, 4), jnp.int32),
-            pltpu.SMEM((1, 4), jnp.int32),
-            pltpu.VMEM((UPPER * RHS, W), BF16),
-            pltpu.SemaphoreType.DMA((4,)),
-        ],
+        scratch_shapes=[pltpu.VMEM((UPPER * RHS, W), BF16)],
         compiler_params=PARAMS,
-    )(uinv, ublk, widths, far, level, solved, own, a, b, c)
+    )(uinv, ublk, slots, level, solved, own, a, b, c)
 
 
 def local(rights, linv, uinv, lblk, ublk, widths, far, owner_level):
-    first, second, solved, sums, flags, level = begin(
+    first, second, solved, sums, flags, level, slots = begin(
         rights, linv, uinv, lblk, ublk, widths, far, owner_level.reshape(1, DEVICES)
     )
     came = (
@@ -507,14 +488,14 @@
     came = send(message, across(4 * (LEADERS[0] ^ LEADERS[1])))
     up_5, message, residue_5, sums = climb(5, message, came, sums, flags)
     came = [send(message, across(32 * k)) for k in (1, 2, 3)]
-    ups_x, message, residues_x, sums = gather(6, message, came, sums, flags)
+    ups_x, message, residues_x, sums = gather(6, message, came, sums, flags, False)
     root = sums.astype(BF16)
     root_came = send(root, layers(0, 1))
     vectors = jnp.concatenate([residues_y, residues_z, residue_5, residues_x, root], axis=0)
     vectors = send(vectors, seats(((0, 1),)))
     last_came = send(message[2 * W : 3 * W], layers(1, 1))
     known, known_other = top(
-        vectors, root_came, message, last_came, flags, *ups_z, up_5, ups_x[0], ups_x[2]
+        vectors, root_came, message, last_came, flags, *ups_z, up_5, *ups_x
     )
     a = send(known, from_leaders(1))
     b = send(known_other, from_leaders(2))
@@ -523,7 +504,7 @@
     a = send(known, seats(((1, 0),)))
     b = send(known_other, seats(((1, 2),)))
     c = send(known_other, seats(((1, 3),)))
-    return descend(uinv, ublk, widths, far, level, solved, known, a, b, c)
+    return descend(uinv, ublk, slots, level, solved, known, a, b, c)
 
 
 def solution(mesh):

time: 107 us -> 101 us (0.944); the launches traced: 105 us -> 100 us
  local copies, waits for them, and re-layouts: 3.48 us -> 0.04 us
  Pallas kernels: 9.93 us -> 7.13 us
  waiting for transfers between devices: 71.1 us -> 72.7 us
    unnamed x24 -> x8, local copies, waits for them, and re-layouts: 3.47 us -> 0.03 us
    pallas_call x2, Pallas kernels: 6.05 us -> 3.85 us  [the longest x1 2.47 us: begin(): pl.pallas_call(begin_kernel, in_specs=[HBM] * 8, out_specs=[VMEM] * 7, ou...]
    ppermute x19, waiting for transfers between devices: 71.1 us -> 72.7 us  [send(): return lax.ppermute(value, AXES, pairs)]
where the time goes in v4:
time: 101 us; the launch traced here: 100 us
  waiting for transfers between devices  72.7 us (72%)
  starting transfers between devices  20.1 us (20%)
  Pallas kernels  7.13 us (7%)
    ppermute x19, waiting for transfers between devices, send(): return lax.ppermute(value, AXES, pairs)  72.7 us
    ppermute x19, starting transfers between devices, send(): return lax.ppermute(value, AXES, pairs)  20.1 us
    pallas_call x1, Pallas kernels, begin(): pl.pallas_call(begin_kernel, in_specs=[HBM] * 8, out_specs=[VMEM] * 7, ou...  2.47 us
  transfers between devices with their start and end apart: 19, of which 3 were waited for; matrix products, arithmetic and copies ran while one was open for 0% of the time, Pallas kernels for 0%

profile of v4, /device:TPU:24, one launch (start us, length us, event | category | flops | bytes accessed | tf_op | source)
XLA Modules:
  0.0 100.4 jit_solution(12939456592907566552)
XLA Ops:
  0.0 2.5 %shard_map.82 = (bf16[784,256]{1,0:T(8,128)(2,1)S(1)}, bf16[784,256]{1,0:T(8,128)(2,1)S(1)}, f32[3,16,256]{2,1,0:T(8,128)S(1)}, f32[128,256]{1,0:T(8,128)S(1)}, ...) custom-call(f32[1,4,16,256]{3,2,1,0:T(8,128)} %rights_in.1, ...), custom_call_target="tpu_custom_call" | custom-call | tf_op jit(solution)/shard_map/pallas_call | solution.py:227
  2.5 0.7 collective-permute-start
  3.2 6.6 %collective-permute-start.1 = (bf16[784,256]{1,0:T(8,128)(2,1)S(1)}, bf16[784,256]{1,0:T(8,128)(2,1)S(1)}, u32[]{:S(2)}, u32[]{:S(2)}) collective-permute-start(bf16[784,256]{1,0:T(8,128)(2,1)S(1)} %get-tuple-element.40.own), channel_id=1, source_target_pairs={{2,0},{3,1},{6,4},{7,5},{10,8},{11,9},{14,12},{15,13},{18,16},{19,... | collective-permute-start | bytes 1204232 | tf_op jit(solution)/shard_map/ppermute | solution.py:42
  9.8 1.3 %collective-permute-start.2 = (bf16[784,256]{1,0:T(8,128)(2,1)S(1)}, bf16[784,256]{1,0:T(8,128)(2,1)S(1)}, u32[]{:S(2)}, u32[]{:S(2)}) collective-permute-start(bf16[784,256]{1,0:T(8,128)(2,1)S(1)} %get-tuple-element.41), channel_id=1, source_target_pairs={{3,0},{2,1},{7,4},{6,5},{11,8},{10,9},{15,12},{14,13},{19,16},{18,... | collective-permute-start | bytes 1204232 | tf_op jit(solution)/shard_map/ppermute | solution.py:42
  11.1 0.0 collective-permute-done.r1
  11.1 4.1 %collective-permute-done.1.r2 = bf16[784,256]{1,0:T(8,128)(2,1)S(1)} collective-permute-done((bf16[784,256]{1,0:T(8,128)(2,1)S(1)}, bf16[784,256]{1,0:T(8,128)(2,1)S(1)}, u32[]{:S(2)}, u32[]{:S(2)}) %collective-permute-start.1) | collective-permute-done | bytes 401440 | tf_op jit(solution)/shard_map/ppermute | solution.py:42
  15.1 3.5 %collective-permute-done.2.r3 = bf16[784,256]{1,0:T(8,128)(2,1)S(1)} collective-permute-done((bf16[784,256]{1,0:T(8,128)(2,1)S(1)}, bf16[784,256]{1,0:T(8,128)(2,1)S(1)}, u32[]{:S(2)}, u32[]{:S(2)}) %collective-permute-start.2) | collective-permute-done | bytes 401440 | tf_op jit(solution)/shard_map/ppermute | solution.py:42
  18.7 0.6 shard_map.83
  19.3 0.7 collective-permute-start.3
  20.0 0.7 collective-permute-start.4
  20.7 0.7 collective-permute-start.5
  21.4 0.0 collective-permute-done.3.r1
  21.4 0.0 collective-permute-done.4.r2
  21.4 0.0 collective-permute-done.5.r3
  21.4 0.6 shard_map.84
  22.0 0.7 collective-permute-start.6
  22.7 0.0 collective-permute-done.6.came
  22.7 0.3 shard_map.85
  23.0 0.7 collective-permute-start.7
  23.6 0.7 collective-permute-start.8
  24.3 0.7 collective-permute-start.9
  25.1 0.0 collective-permute-done.7.r1
  25.1 0.0 collective-permute-done.8.r2
  25.1 0.0 collective-permute-done.9.r3
  25.1 0.6 shard_map.86
  25.8 0.7 collective-permute-start.12
  26.5 0.7 collective-permute-start.10
  27.1 0.7 collective-permute-start.11
  27.8 0.0 collective-permute-done.11.root
  27.8 0.0 collective-permute-done.10.vectors
  27.8 0.0 collective-permute-done.12.came
  27.8 0.0 copy-start.1
  27.8 0.8 shard_map.87
  28.7 0.0 copy-start
  28.7 0.8 collective-permute-start.13
  29.5 0.7 collective-permute-start.14
  30.1 0.7 collective-permute-start.15
  30.8 0.0 collective-permute-done.13.a
  30.8 0.0 collective-permute-done.14.b
  30.8 0.0 collective-permute-done.15.c
  30.8 0.4 shard_map.88
  31.2 0.7 collective-permute-start.16
  31.9 0.7 collective-permute-start.17
  32.6 1.3 %collective-permute-start.18 = (bf16[128,256]{1,0:T(8,128)(2,1)S(1)}, bf16[128,256]{1,0:T(8,128)(2,1)S(1)}, u32[]{:S(2)}, u32[]{:S(2)}) collective-permute-start(bf16[128,256]{1,0:T(8,128)(2,1)S(1)} %get-tuple-element.68), channel_id=1, source_target_pairs={{1,3},{5,7},{9,11},{13,15},{17,19},{21,23},{25,27},{29,31},{33,35}... | collective-permute-start | bytes 196616 | tf_op jit(solution)/shard_map/ppermute | solution.py:42
  33.9 0.0 collective-permute-done.16.a
  33.9 0.0 collective-permute-done.17.b
  33.9 65.1 %collective-permute-done.18.c = bf16[128,256]{1,0:T(8,128)(2,1)S(1)} collective-permute-done((bf16[128,256]{1,0:T(8,128)(2,1)S(1)}, bf16[128,256]{1,0:T(8,128)(2,1)S(1)}, u32[]{:S(2)}, u32[]{:S(2)}) %collective-permute-start.18) | collective-permute-done | bytes 65568 | tf_op jit(solution)/shard_map/ppermute | solution.py:42
  99.0 0.0 copy-done.1
  99.0 0.0 copy-done
  99.0 1.4 %shard_map.89 = f32[1,4,16,256]{3,2,1,0:T(8,128)} custom-call(bf16[1,4,256,256]{3,2,1,0:T(8,128)(2,1)S(1)} %copy-done.1, bf16[1,4,2,256,256]{4,3,2,1,0:T(8,128)(2,1)S(1)} %copy-done, f32[96,256]{1,0:T(8,128)S(1)} %get-tuple-element.37.slots, f32[16,256]{1,0:T(8,128)S(1)} %get-tuple-element.38.level, f32[3,16,256]{2,1,0:T(8,128)S(1)} %get-tuple-element.39.solved, ...), custom_call_target="tpu_custom_call" | custom-call | tf_op jit(solution)/shard_map/pallas_call | solution.py:466
  (6 shorter events, 0.0 us)
Async XLA Ops:
  2.5 8.6 %collective-permute-start = (bf16[784,256]{1,0:T(8,128)(2,1)S(1)}, bf16[784,256]{1,0:T(8,128)(2,1)S(1)}, u32[]{:S(2)}, u32[]{:S(2)}) collective-permute-start(bf16[784,256]{1,0:T(8,128)(2,1)S(1)} %get-tuple-element.41), channel_id=1, source_target_pairs={{1,0},{0,1},{5,4},{4,5},{9,8},{8,9},{13,12},{12,13},{17,16},{16,17... | collective-permute-start | bytes 1204232 | tf_op jit(solution)/shard_map/ppermute | solution.py:42
  3.2 12.0 %collective-permute-start.1 = (bf16[784,256]{1,0:T(8,128)(2,1)S(1)}, bf16[784,256]{1,0:T(8,128)(2,1)S(1)}, u32[]{:S(2)}, u32[]{:S(2)}) collective-permute-start(bf16[784,256]{1,0:T(8,128)(2,1)S(1)} %get-tuple-element.40.own), channel_id=1, source_target_pairs={{2,0},{3,1},{6,4},{7,5},{10,8},{11,9},{14,12},{15,13},{18,16},{19,... | collective-permute-start | bytes 1204232 | tf_op jit(solution)/shard_map/ppermute | solution.py:42
  9.8 8.9 %collective-permute-start.2 = (bf16[784,256]{1,0:T(8,128)(2,1)S(1)}, bf16[784,256]{1,0:T(8,128)(2,1)S(1)}, u32[]{:S(2)}, u32[]{:S(2)}) collective-permute-start(bf16[784,256]{1,0:T(8,128)(2,1)S(1)} %get-tuple-element.41), channel_id=1, source_target_pairs={{3,0},{2,1},{7,4},{6,5},{11,8},{10,9},{15,12},{14,13},{19,16},{18,... | collective-permute-start | bytes 1204232 | tf_op jit(solution)/shard_map/ppermute | solution.py:42
  19.3 2.1 %collective-permute-start.3 = (bf16[784,256]{1,0:T(8,128)(2,1)S(1)}, bf16[784,256]{1,0:T(8,128)(2,1)S(1)}, u32[]{:S(2)}, u32[]{:S(2)}) collective-permute-start(bf16[784,256]{1,0:T(8,128)(2,1)S(1)} %get-tuple-element.45.own), channel_id=1, source_target_pairs={{12,8},{13,9},{16,20},{17,21},{44,40},{45,41},{48,52},{49,53},{76,... | collective-permute-start | bytes 1204232 | tf_op jit(solution)/shard_map/ppermute | solution.py:42
  20.0 1.4 %collective-permute-start.4 = (bf16[784,256]{1,0:T(8,128)(2,1)S(1)}, bf16[784,256]{1,0:T(8,128)(2,1)S(1)}, u32[]{:S(2)}, u32[]{:S(2)}) collective-permute-start(bf16[784,256]{1,0:T(8,128)(2,1)S(1)} %get-tuple-element.45.own), channel_id=1, source_target_pairs={{0,8},{1,9},{28,20},{29,21},{32,40},{33,41},{60,52},{61,53},{64,72... | collective-permute-start | bytes 1204232 | tf_op jit(solution)/shard_map/ppermute | solution.py:42
  20.7 0.7 collective-permute-start.5
  22.0 0.7 collective-permute-start.6
  23.0 2.1 %collective-permute-start.7 = (bf16[784,256]{1,0:T(8,128)(2,1)S(1)}, bf16[784,256]{1,0:T(8,128)(2,1)S(1)}, u32[]{:S(2)}, u32[]{:S(2)}) collective-permute-start(bf16[784,256]{1,0:T(8,128)(2,1)S(1)} %get-tuple-element.51.own), channel_id=1, source_target_pairs={{8,40},{9,41},{20,52},{21,53},{40,8},{41,9},{52,20},{53,21},{72,10... | collective-permute-start | bytes 1204232 | tf_op jit(solution)/shard_map/ppermute | solution.py:42
  23.6 1.4 %collective-permute-start.8 = (bf16[784,256]{1,0:T(8,128)(2,1)S(1)}, bf16[784,256]{1,0:T(8,128)(2,1)S(1)}, u32[]{:S(2)}, u32[]{:S(2)}) collective-permute-start(bf16[784,256]{1,0:T(8,128)(2,1)S(1)} %get-tuple-element.51.own), channel_id=1, source_target_pairs={{8,72},{9,73},{20,84},{21,85},{40,104},{41,105},{52,116},{53,117},... | collective-permute-start | bytes 1204232 | tf_op jit(solution)/shard_map/ppermute | solution.py:42
  24.3 0.8 collective-permute-start.9
  25.8 2.1 %collective-permute-start.12 = (bf16[256,256]{1,0:T(8,128)(2,1)S(1)}, bf16[256,256]{1,0:T(8,128)(2,1)S(1)}, u32[]{:S(2)}, u32[]{:S(2)}) collective-permute-start(bf16[256,256]{1,0:T(8,128)(2,1)S(1)} %slice.3), channel_id=1, source_target_pairs={{9,139},{21,151},{41,171},{53,183},{73,203},{85,215},{105,235},{11... | collective-permute-start | bytes 393224 | tf_op jit(solution)/shard_map/ppermute | solution.py:42
  26.5 1.4 %collective-permute-start.10 = (bf16[176,256]{1,0:T(8,128)(2,1)S(1)}, bf16[176,256]{1,0:T(8,128)(2,1)S(1)}, u32[]{:S(2)}, u32[]{:S(2)}) collective-permute-start(bf16[176,256]{1,0:T(8,128)(2,1)S(1)} %get-tuple-element.69), channel_id=1, source_target_pairs={{0,1},{4,5},{8,9},{12,13},{16,17},{20,21},{24,25},{28,29},{32,33},... | collective-permute-start | bytes 270344 | tf_op jit(solution)/shard_map/ppermute | solution.py:42
  27.1 0.7 collective-permute-start.11
  27.8 71.2 %copy-start.1 = (bf16[1,4,256,256]{3,2,1,0:T(8,128)(2,1)S(1)}, bf16[1,4,256,256]{3,2,1,0:T(8,128)(2,1)}, u32[]{:S(2)}) copy-start(bf16[1,4,256,256]{3,2,1,0:T(8,128)(2,1)} %uinv.1) | copy-start | bytes 1572868
  28.7 70.4 %copy-start = (bf16[1,4,2,256,256]{4,3,2,1,0:T(8,128)(2,1)S(1)}, bf16[1,4,2,256,256]{4,3,2,1,0:T(8,128)(2,1)}, u32[]{:S(2)}) copy-start(bf16[1,4,2,256,256]{4,3,2,1,0:T(8,128)(2,1)} %ublk.1) | copy-start | bytes 3145732
  28.7 2.2 %collective-permute-start.13 = (bf16[96,256]{1,0:T(8,128)(2,1)S(1)}, bf16[96,256]{1,0:T(8,128)(2,1)S(1)}, u32[]{:S(2)}, u32[]{:S(2)}) collective-permute-start(bf16[96,256]{1,0:T(8,128)(2,1)S(1)} %get-tuple-element.62.own), channel_id=1, source_target_pairs={{9,13},{21,17},{41,45},{53,49},{73,77},{85,81},{105,109},{117,113}... | collective-permute-start | bytes 147464 | tf_op jit(solution)/shard_map/ppermute | solution.py:42
  29.5 1.4 %collective-permute-start.14 = (bf16[96,256]{1,0:T(8,128)(2,1)S(1)}, bf16[96,256]{1,0:T(8,128)(2,1)S(1)}, u32[]{:S(2)}, u32[]{:S(2)}) collective-permute-start(bf16[96,256]{1,0:T(8,128)(2,1)S(1)} %get-tuple-element.63), channel_id=1, source_target_pairs={{9,1},{21,29},{41,33},{53,61},{73,65},{85,93},{105,97},{117,125},{... | collective-permute-start | bytes 147464 | tf_op jit(solution)/shard_map/ppermute | solution.py:42
  30.1 0.7 collective-permute-start.15
  31.2 2.7 %collective-permute-start.16 = (bf16[128,256]{1,0:T(8,128)(2,1)S(1)}, bf16[128,256]{1,0:T(8,128)(2,1)S(1)}, u32[]{:S(2)}, u32[]{:S(2)}) collective-permute-start(bf16[128,256]{1,0:T(8,128)(2,1)S(1)} %get-tuple-element.67.own), channel_id=1, source_target_pairs={{1,0},{5,4},{9,8},{13,12},{17,16},{21,20},{25,24},{29,28},{33,32},... | collective-permute-start | bytes 196616 | tf_op jit(solution)/shard_map/ppermute | solution.py:42
  31.9 2.0 %collective-permute-start.17 = (bf16[128,256]{1,0:T(8,128)(2,1)S(1)}, bf16[128,256]{1,0:T(8,128)(2,1)S(1)}, u32[]{:S(2)}, u32[]{:S(2)}) collective-permute-start(bf16[128,256]{1,0:T(8,128)(2,1)S(1)} %get-tuple-element.68), channel_id=1, source_target_pairs={{1,2},{5,6},{9,10},{13,14},{17,18},{21,22},{25,26},{29,30},{33,34}... | collective-permute-start | bytes 196616 | tf_op jit(solution)/shard_map/ppermute | solution.py:42
  32.6 66.4 %collective-permute-start.18 = (bf16[128,256]{1,0:T(8,128)(2,1)S(1)}, bf16[128,256]{1,0:T(8,128)(2,1)S(1)}, u32[]{:S(2)}, u32[]{:S(2)}) collective-permute-start(bf16[128,256]{1,0:T(8,128)(2,1)S(1)} %get-tuple-element.68), channel_id=1, source_target_pairs={{1,3},{5,7},{9,11},{13,15},{17,19},{21,23},{25,27},{29,31},{33,35}... | collective-permute-start | bytes 196616 | tf_op jit(solution)/shard_map/ppermute | solution.py:42

commit v5 on v4

--- a/solution.py
+++ b/solution.py
@@ -205,8 +205,11 @@
     halves = sums[...].astype(BF16)
 
     def write(low, up):
-        for b in range(2):
-            low[b * W : (b + 1) * W] = low_blocks[b]
+        wide = jnp.concatenate([my_level] * (W // RHS), axis=0)
+        low[:W] = jnp.where(
+            wide == float(UPPER), up_blocks[2].astype(F32), low_blocks[0].astype(F32)
+        ).astype(BF16)
+        low[W : 2 * W] = low_blocks[1]
         low[FAR_A : FAR_A + RHS] = distance
         low[SUMS : SUMS + UPPER * RHS] = halves
         low[SUMS + UPPER * RHS :] = jnp.zeros((ROWS - SUMS - UPPER * RHS, W), BF16)
@@ -296,7 +299,7 @@
 
 
 def gather_kernel(
-    height, own, r1, r2, r3, sums, flags, left, residues, rest, k1, k2, k1q, lp, lq
+    height, own, r2, r1, r3, sums, flags, left, residues, rest, k1, k2, k1q, lp, lq
 ):
     choose_rows(flag(flags, height - 1), own, r1, k1, lp)
     choose_rows(flag(flags, OTHER_PAIR[height]), r2, r3, k1q, lq)
@@ -329,7 +332,7 @@
         + [message] * kept,
         scratch_shapes=[pltpu.VMEM((ROWS, W), BF16)] * (5 - kept),
         compiler_params=PARAMS,
-    )(own, *came, sums, flags)
+    )(own, came[1], came[0], came[2], sums, flags)
     return ups, left, residues, rest
 
 
@@ -371,11 +374,11 @@
 
 
 def top_kernel(
-    vectors, root, mine, came, flags, u3, u4, u3q, u5, u6, u7, near_out, other_out
+    vectors, came, mine, flags, u3, u4, u3q, u5, u6, u7, near_out, other_out
 ):
     wide = jnp.concatenate([flag(flags, UPPER - 1)] * 16, axis=0)
-    last = choose(wide, mine[2 * W : 3 * W], came[...])
-    residue = part(vectors, 10).astype(F32) + root[...].astype(F32)
+    last = choose(wide, mine[2 * W : 3 * W], came[:W])
+    residue = part(vectors, 10).astype(F32) + came[W:].astype(F32)
     above = [times(residue.astype(BF16), last).astype(BF16)]
     for index, up in ((9, u7), (7, u6), (6, u5), (5, u4)):
         above = [separator(part(vectors, index), up, above)] + above
@@ -385,15 +388,15 @@
             out[step * RHS : (step + 1) * RHS] = value
 
 
-def top(vectors, root, mine, came, flags, *ups):
+def top(vectors, came, mine, flags, *ups):
     known = jax.ShapeDtypeStruct(((UPPER - LOW) * RHS, W), BF16)
     return pl.pallas_call(
         top_kernel,
-        in_specs=[VMEM] * (5 + len(ups)),
+        in_specs=[VMEM] * (4 + len(ups)),
         out_specs=[VMEM] * 2,
         out_shape=[known, known],
         compiler_params=PARAMS,
-    )(vectors, root, mine, came, flags, *ups)
+    )(vectors, came, mine, flags, *ups)
 
 
 def select_known(cases, known):
@@ -477,25 +480,24 @@
     first, second, solved, sums, flags, level, slots = begin(
         rights, linv, uinv, lblk, ublk, widths, far, owner_level.reshape(1, DEVICES)
     )
-    came = (
-        send(second, seats(((1, 0), (0, 1)))),
-        send(first, seats(((2, 0), (3, 1)))),
-        send(second, seats(((3, 0), (2, 1)))),
-    )
+    r2 = send(first, seats(((2, 0), (3, 1))))
+    r1 = send(second, seats(((1, 0), (0, 1))))
+    r3 = send(second, seats(((3, 0), (2, 1))))
+    came = (r1, r2, r3)
     ups_y, message, residues_y, sums = gather(1, first, came, sums, flags)
     came = [send(message, to_leaders(k)) for k in (1, 2, 3)]
     ups_z, message, residues_z, sums = gather(3, message, came, sums, flags)
     came = send(message, across(4 * (LEADERS[0] ^ LEADERS[1])))
     up_5, message, residue_5, sums = climb(5, message, came, sums, flags)
-    came = [send(message, across(32 * k)) for k in (1, 2, 3)]
+    came = {k: send(message, across(32 * k)) for k in (2, 1, 3)}
+    came = [came[k] for k in (1, 2, 3)]
     ups_x, message, residues_x, sums = gather(6, message, came, sums, flags, False)
     root = sums.astype(BF16)
-    root_came = send(root, layers(0, 1))
+    across_came = send(jnp.concatenate([message[:W], root], axis=0), layers(0, 1))
     vectors = jnp.concatenate([residues_y, residues_z, residue_5, residues_x, root], axis=0)
     vectors = send(vectors, seats(((0, 1),)))
-    last_came = send(message[2 * W : 3 * W], layers(1, 1))
     known, known_other = top(
-        vectors, root_came, message, last_came, flags, *ups_z, up_5, *ups_x
+        vectors, across_came, message, flags, *ups_z, up_5, *ups_x
     )
     a = send(known, from_leaders(1))
     b = send(known_other, from_leaders(2))

time: 101 us -> 93.6 us (0.927)
  waiting for transfers between devices: 72.7 us -> 67.6 us
  starting transfers between devices: 20.1 us -> 18 us
    ppermute x19 -> x18, waiting for transfers between devices: 72.7 us -> 67.6 us  [send(): return lax.ppermute(value, AXES, pairs)]
    ppermute x19 -> x18, starting transfers between devices: 20.1 us -> 18 us  [send(): return lax.ppermute(value, AXES, pairs)]
  transfers between devices with their start and end apart: 19 -> 18, of which waited for: 3 -> 3; matrix products, arithmetic and copies ran while one was open for 0% -> 0% of each run, Pallas kernels for 0% -> 0%
where the time goes in v5:
time: 93.6 us; the launch traced here: 93.1 us
  waiting for transfers between devices  67.6 us (72%)
  starting transfers between devices  18 us (19%)
  Pallas kernels  7.16 us (8%)
    ppermute x18, waiting for transfers between devices, send(): return lax.ppermute(value, AXES, pairs)  67.6 us
    ppermute x18, starting transfers between devices, send(): return lax.ppermute(value, AXES, pairs)  18 us
    pallas_call x1, Pallas kernels, begin(): pl.pallas_call(begin_kernel, in_specs=[HBM] * 8, out_specs=[VMEM] * 7, ou...  2.51 us
  transfers between devices with their start and end apart: 18, of which 3 were waited for; matrix products, arithmetic and copies ran while one was open for 0% of the time, Pallas kernels for 0%

profile of v5, /device:TPU:24, one launch (start us, length us, event | category | flops | bytes accessed | tf_op | source)
XLA Modules:
  0.0 93.1 jit_solution(2407993873931570995)
XLA Ops:
  0.0 2.5 %shard_map.82 = (bf16[784,256]{1,0:T(8,128)(2,1)S(1)}, bf16[784,256]{1,0:T(8,128)(2,1)S(1)}, f32[3,16,256]{2,1,0:T(8,128)S(1)}, f32[128,256]{1,0:T(8,128)S(1)}, ...) custom-call(f32[1,4,16,256]{3,2,1,0:T(8,128)} %rights_in.1, ...), custom_call_target="tpu_custom_call" | custom-call | tf_op jit(solution)/shard_map/pallas_call | solution.py:230
  2.5 3.2 %collective-permute-start = (bf16[784,256]{1,0:T(8,128)(2,1)S(1)}, bf16[784,256]{1,0:T(8,128)(2,1)S(1)}, u32[]{:S(2)}, u32[]{:S(2)}) collective-permute-start(bf16[784,256]{1,0:T(8,128)(2,1)S(1)} %get-tuple-element.40.own), channel_id=1, source_target_pairs={{2,0},{3,1},{6,4},{7,5},{10,8},{11,9},{14,12},{15,13},{18,16},{19,... | collective-permute-start | bytes 1204232 | tf_op jit(solution)/shard_map/ppermute | solution.py:42
  5.7 0.7 collective-permute-start.1
  6.4 3.3 %collective-permute-start.2 = (bf16[784,256]{1,0:T(8,128)(2,1)S(1)}, bf16[784,256]{1,0:T(8,128)(2,1)S(1)}, u32[]{:S(2)}, u32[]{:S(2)}) collective-permute-start(bf16[784,256]{1,0:T(8,128)(2,1)S(1)} %get-tuple-element.41), channel_id=1, source_target_pairs={{3,0},{2,1},{7,4},{6,5},{11,8},{10,9},{15,12},{14,13},{19,16},{18,... | collective-permute-start | bytes 1204232 | tf_op jit(solution)/shard_map/ppermute | solution.py:42
  9.6 5.4 %collective-permute-done.r2 = bf16[784,256]{1,0:T(8,128)(2,1)S(1)} collective-permute-done((bf16[784,256]{1,0:T(8,128)(2,1)S(1)}, bf16[784,256]{1,0:T(8,128)(2,1)S(1)}, u32[]{:S(2)}, u32[]{:S(2)}) %collective-permute-start) | collective-permute-done | bytes 401440 | tf_op jit(solution)/shard_map/ppermute | solution.py:42
  15.0 0.0 collective-permute-done.1.r1
  15.0 2.8 %collective-permute-done.2.r3 = bf16[784,256]{1,0:T(8,128)(2,1)S(1)} collective-permute-done((bf16[784,256]{1,0:T(8,128)(2,1)S(1)}, bf16[784,256]{1,0:T(8,128)(2,1)S(1)}, u32[]{:S(2)}, u32[]{:S(2)}) %collective-permute-start.2) | collective-permute-done | bytes 401440 | tf_op jit(solution)/shard_map/ppermute | solution.py:42
  17.8 0.6 shard_map.83
  18.4 0.7 collective-permute-start.3
  19.1 0.7 collective-permute-start.4
  19.8 0.7 collective-permute-start.5
  20.5 0.0 collective-permute-done.3.r2
  20.5 0.0 collective-permute-done.4.r1
  20.5 0.0 collective-permute-done.5.r3
  20.5 0.6 shard_map.84
  21.1 0.7 collective-permute-start.6
  21.8 0.0 collective-permute-done.6.came
  21.8 0.3 shard_map.85
  22.1 0.7 collective-permute-start.7
  22.7 0.7 collective-permute-start.8
  23.4 0.7 collective-permute-start.9
  24.2 0.0 collective-permute-done.7.r2
  24.2 0.0 collective-permute-done.8.r1
  24.2 0.0 collective-permute-done.9.r3
  24.2 0.6 shard_map.86
  24.9 0.7 collective-permute-start.11
  25.6 0.7 collective-permute-start.10
  26.2 0.0 collective-permute-done.10.vectors
  26.3 0.0 collective-permute-done.11.came
  26.3 0.0 copy-start.1
  26.3 0.8 shard_map.87
  27.1 0.0 copy-start
  27.1 0.8 collective-permute-start.12
  27.9 0.7 collective-permute-start.13
  28.6 0.7 collective-permute-start.14
  29.3 0.0 collective-permute-done.12.a
  29.3 0.0 collective-permute-done.13.b
  29.3 0.0 collective-permute-done.14.c
  29.3 0.4 shard_map.88
  29.7 0.7 collective-permute-start.15
  30.4 0.7 collective-permute-start.16
  31.0 1.3 %collective-permute-start.17 = (bf16[128,256]{1,0:T(8,128)(2,1)S(1)}, bf16[128,256]{1,0:T(8,128)(2,1)S(1)}, u32[]{:S(2)}, u32[]{:S(2)}) collective-permute-start(bf16[128,256]{1,0:T(8,128)(2,1)S(1)} %get-tuple-element.68), channel_id=1, source_target_pairs={{1,3},{5,7},{9,11},{13,15},{17,19},{21,23},{25,27},{29,31},{33,35}... | collective-permute-start | bytes 196616 | tf_op jit(solution)/shard_map/ppermute | solution.py:42
  32.3 0.0 collective-permute-done.15.a
  32.3 0.0 collective-permute-done.16.b
  32.3 59.4 %collective-permute-done.17.c = bf16[128,256]{1,0:T(8,128)(2,1)S(1)} collective-permute-done((bf16[128,256]{1,0:T(8,128)(2,1)S(1)}, bf16[128,256]{1,0:T(8,128)(2,1)S(1)}, u32[]{:S(2)}, u32[]{:S(2)}) %collective-permute-start.17) | collective-permute-done | bytes 65568 | tf_op jit(solution)/shard_map/ppermute | solution.py:42
  91.8 0.0 copy-done.1
  91.8 0.0 copy-done
  91.8 1.4 %shard_map.89 = f32[1,4,16,256]{3,2,1,0:T(8,128)} custom-call(bf16[1,4,256,256]{3,2,1,0:T(8,128)(2,1)S(1)} %copy-done.1, bf16[1,4,2,256,256]{4,3,2,1,0:T(8,128)(2,1)S(1)} %copy-done, f32[96,256]{1,0:T(8,128)S(1)} %get-tuple-element.37.slots, f32[16,256]{1,0:T(8,128)S(1)} %get-tuple-element.38.level, f32[3,16,256]{2,1,0:T(8,128)S(1)} %get-tuple-element.39.solved, ...), custom_call_target="tpu_custom_call" | custom-call | tf_op jit(solution)/shard_map/pallas_call | solution.py:469
  (7 shorter events, 0.0 us)
Async XLA Ops:
  2.5 12.5 %collective-permute-start = (bf16[784,256]{1,0:T(8,128)(2,1)S(1)}, bf16[784,256]{1,0:T(8,128)(2,1)S(1)}, u32[]{:S(2)}, u32[]{:S(2)}) collective-permute-start(bf16[784,256]{1,0:T(8,128)(2,1)S(1)} %get-tuple-element.40.own), channel_id=1, source_target_pairs={{2,0},{3,1},{6,4},{7,5},{10,8},{11,9},{14,12},{15,13},{18,16},{19,... | collective-permute-start | bytes 1204232 | tf_op jit(solution)/shard_map/ppermute | solution.py:42
  5.7 9.3 %collective-permute-start.1 = (bf16[784,256]{1,0:T(8,128)(2,1)S(1)}, bf16[784,256]{1,0:T(8,128)(2,1)S(1)}, u32[]{:S(2)}, u32[]{:S(2)}) collective-permute-start(bf16[784,256]{1,0:T(8,128)(2,1)S(1)} %get-tuple-element.41), channel_id=1, source_target_pairs={{1,0},{0,1},{5,4},{4,5},{9,8},{8,9},{13,12},{12,13},{17,16},{16,17... | collective-permute-start | bytes 1204232 | tf_op jit(solution)/shard_map/ppermute | solution.py:42
  6.4 11.4 %collective-permute-start.2 = (bf16[784,256]{1,0:T(8,128)(2,1)S(1)}, bf16[784,256]{1,0:T(8,128)(2,1)S(1)}, u32[]{:S(2)}, u32[]{:S(2)}) collective-permute-start(bf16[784,256]{1,0:T(8,128)(2,1)S(1)} %get-tuple-element.41), channel_id=1, source_target_pairs={{3,0},{2,1},{7,4},{6,5},{11,8},{10,9},{15,12},{14,13},{19,16},{18,... | collective-permute-start | bytes 1204232 | tf_op jit(solution)/shard_map/ppermute | solution.py:42
  18.4 2.1 %collective-permute-start.3 = (bf16[784,256]{1,0:T(8,128)(2,1)S(1)}, bf16[784,256]{1,0:T(8,128)(2,1)S(1)}, u32[]{:S(2)}, u32[]{:S(2)}) collective-permute-start(bf16[784,256]{1,0:T(8,128)(2,1)S(1)} %get-tuple-element.45.own), channel_id=1, source_target_pairs={{0,8},{1,9},{28,20},{29,21},{32,40},{33,41},{60,52},{61,53},{64,72... | collective-permute-start | bytes 1204232 | tf_op jit(solution)/shard_map/ppermute | solution.py:42
  19.1 1.4 %collective-permute-start.4 = (bf16[784,256]{1,0:T(8,128)(2,1)S(1)}, bf16[784,256]{1,0:T(8,128)(2,1)S(1)}, u32[]{:S(2)}, u32[]{:S(2)}) collective-permute-start(bf16[784,256]{1,0:T(8,128)(2,1)S(1)} %get-tuple-element.45.own), channel_id=1, source_target_pairs={{12,8},{13,9},{16,20},{17,21},{44,40},{45,41},{48,52},{49,53},{76,... | collective-permute-start | bytes 1204232 | tf_op jit(solution)/shard_map/ppermute | solution.py:42
  19.8 0.7 collective-permute-start.5
  21.1 0.7 collective-permute-start.6
  22.1 2.1 %collective-permute-start.7 = (bf16[784,256]{1,0:T(8,128)(2,1)S(1)}, bf16[784,256]{1,0:T(8,128)(2,1)S(1)}, u32[]{:S(2)}, u32[]{:S(2)}) collective-permute-start(bf16[784,256]{1,0:T(8,128)(2,1)S(1)} %get-tuple-element.51.own), channel_id=1, source_target_pairs={{8,72},{9,73},{20,84},{21,85},{40,104},{41,105},{52,116},{53,117},... | collective-permute-start | bytes 1204232 | tf_op jit(solution)/shard_map/ppermute | solution.py:42
  22.7 1.4 %collective-permute-start.8 = (bf16[784,256]{1,0:T(8,128)(2,1)S(1)}, bf16[784,256]{1,0:T(8,128)(2,1)S(1)}, u32[]{:S(2)}, u32[]{:S(2)}) collective-permute-start(bf16[784,256]{1,0:T(8,128)(2,1)S(1)} %get-tuple-element.51.own), channel_id=1, source_target_pairs={{8,40},{9,41},{20,52},{21,53},{40,8},{41,9},{52,20},{53,21},{72,10... | collective-permute-start | bytes 1204232 | tf_op jit(solution)/shard_map/ppermute | solution.py:42
  23.4 0.8 collective-permute-start.9
  24.9 1.4 %collective-permute-start.11 = (bf16[272,256]{1,0:T(8,128)(2,1)S(1)}, bf16[272,256]{1,0:T(8,128)(2,1)S(1)}, u32[]{:S(2)}, u32[]{:S(2)}) collective-permute-start(bf16[272,256]{1,0:T(8,128)(2,1)S(1)} %pad_maximum_fusion), channel_id=1, source_target_pairs={{8,139},{20,151},{40,171},{52,183},{72,203},{84,215},{104,235},{11... | collective-permute-start | bytes 417800 | tf_op jit(solution)/shard_map/ppermute | solution.py:42
  25.6 0.7 collective-permute-start.10
  26.3 65.5 %copy-start.1 = (bf16[1,4,256,256]{3,2,1,0:T(8,128)(2,1)S(1)}, bf16[1,4,256,256]{3,2,1,0:T(8,128)(2,1)}, u32[]{:S(2)}) copy-start(bf16[1,4,256,256]{3,2,1,0:T(8,128)(2,1)} %uinv.1) | copy-start | bytes 1572868
  27.1 64.7 %copy-start = (bf16[1,4,2,256,256]{4,3,2,1,0:T(8,128)(2,1)S(1)}, bf16[1,4,2,256,256]{4,3,2,1,0:T(8,128)(2,1)}, u32[]{:S(2)}) copy-start(bf16[1,4,2,256,256]{4,3,2,1,0:T(8,128)(2,1)} %ublk.1) | copy-start | bytes 3145732
  27.1 2.2 %collective-permute-start.12 = (bf16[96,256]{1,0:T(8,128)(2,1)S(1)}, bf16[96,256]{1,0:T(8,128)(2,1)S(1)}, u32[]{:S(2)}, u32[]{:S(2)}) collective-permute-start(bf16[96,256]{1,0:T(8,128)(2,1)S(1)} %get-tuple-element.62.own), channel_id=1, source_target_pairs={{9,13},{21,17},{41,45},{53,49},{73,77},{85,81},{105,109},{117,113}... | collective-permute-start | bytes 147464 | tf_op jit(solution)/shard_map/ppermute | solution.py:42
  27.9 1.4 %collective-permute-start.13 = (bf16[96,256]{1,0:T(8,128)(2,1)S(1)}, bf16[96,256]{1,0:T(8,128)(2,1)S(1)}, u32[]{:S(2)}, u32[]{:S(2)}) collective-permute-start(bf16[96,256]{1,0:T(8,128)(2,1)S(1)} %get-tuple-element.63), channel_id=1, source_target_pairs={{9,1},{21,29},{41,33},{53,61},{73,65},{85,93},{105,97},{117,125},{... | collective-permute-start | bytes 147464 | tf_op jit(solution)/shard_map/ppermute | solution.py:42
  28.6 0.7 collective-permute-start.14
  29.7 2.7 %collective-permute-start.15 = (bf16[128,256]{1,0:T(8,128)(2,1)S(1)}, bf16[128,256]{1,0:T(8,128)(2,1)S(1)}, u32[]{:S(2)}, u32[]{:S(2)}) collective-permute-start(bf16[128,256]{1,0:T(8,128)(2,1)S(1)} %get-tuple-element.67.own), channel_id=1, source_target_pairs={{1,0},{5,4},{9,8},{13,12},{17,16},{21,20},{25,24},{29,28},{33,32},... | collective-permute-start | bytes 196616 | tf_op jit(solution)/shard_map/ppermute | solution.py:42
  30.4 2.0 %collective-permute-start.16 = (bf16[128,256]{1,0:T(8,128)(2,1)S(1)}, bf16[128,256]{1,0:T(8,128)(2,1)S(1)}, u32[]{:S(2)}, u32[]{:S(2)}) collective-permute-start(bf16[128,256]{1,0:T(8,128)(2,1)S(1)} %get-tuple-element.68), channel_id=1, source_target_pairs={{1,2},{5,6},{9,10},{13,14},{17,18},{21,22},{25,26},{29,30},{33,34}... | collective-permute-start | bytes 196616 | tf_op jit(solution)/shard_map/ppermute | solution.py:42
  31.0 60.7 %collective-permute-start.17 = (bf16[128,256]{1,0:T(8,128)(2,1)S(1)}, bf16[128,256]{1,0:T(8,128)(2,1)S(1)}, u32[]{:S(2)}, u32[]{:S(2)}) collective-permute-start(bf16[128,256]{1,0:T(8,128)(2,1)S(1)} %get-tuple-element.68), channel_id=1, source_target_pairs={{1,3},{5,7},{9,11},{13,15},{17,19},{21,23},{25,27},{29,31},{33,35}... | collective-permute-start | bytes 196616 | tf_op jit(solution)/shard_map/ppermute | solution.py:42

commit v6 on v5

--- a/solution.py
+++ b/solution.py
@@ -16,10 +16,13 @@
 AXES = ("gz", "row", "col")
 BF16 = jnp.bfloat16
 F32 = jnp.float32
+SHARE = 64
 FAR_A = 2 * W
-SUMS = 2 * W + RHS
-FAR_B = 3 * W
-ROWS = 3 * W + RHS
+GAIN_A = FAR_A + RHS
+SUMS = GAIN_A + SHARE
+GAIN_B = 2 * W
+FAR_B = GAIN_B + W - SHARE
+ROWS = FAR_B + RHS
 GATHERS = (1, 3, 6)
 OTHER_PAIR = {low: UPPER + k for k, low in enumerate(GATHERS)}
 ROLE_A = UPPER + len(GATHERS)
@@ -205,16 +208,16 @@
     halves = sums[...].astype(BF16)
 
     def write(low, up):
-        wide = jnp.concatenate([my_level] * (W // RHS), axis=0)
-        low[:W] = jnp.where(
-            wide == float(UPPER), up_blocks[2].astype(F32), low_blocks[0].astype(F32)
-        ).astype(BF16)
+        wide = jnp.concatenate([my_level] * (W // RHS), axis=0) == float(UPPER)
+        low[:W] = choose(wide, up_blocks[2], low_blocks[0])
         low[W : 2 * W] = low_blocks[1]
-        low[FAR_A : FAR_A + RHS] = distance
-        low[SUMS : SUMS + UPPER * RHS] = halves
-        low[SUMS + UPPER * RHS :] = jnp.zeros((ROWS - SUMS - UPPER * RHS, W), BF16)
-        for b in range(3):
-            up[b * W : (b + 1) * W] = up_blocks[b]
+        low[FAR_A:GAIN_A] = distance
+        low[GAIN_A:SUMS] = up_blocks[2][:SHARE]
+        low[SUMS:] = halves
+        up[:SHARE] = choose(wide[:SHARE], up_blocks[2][:SHARE], up_blocks[0][:SHARE])
+        up[SHARE:W] = up_blocks[0][SHARE:]
+        up[W : 2 * W] = up_blocks[1]
+        up[GAIN_B:FAR_B] = up_blocks[2][SHARE:]
         up[FAR_B:] = distance
 
     @pl.when(place % 2 == 0)
@@ -289,7 +292,8 @@
         if step == 1:
             value = value - near
         rest.append(value - jnp.where(distance == float(step), away, 0.0))
-    return half, jnp.concatenate(rest, axis=0)
+    gain = times(half[:, :SHARE], low[GAIN_A:SUMS]).astype(BF16)
+    return half, gain, jnp.concatenate(rest, axis=0)
 
 
 def pass_on(flags, rest, left):
@@ -307,12 +311,11 @@
     rows = slice(SUMS, SUMS + sums.shape[0])
     near = sums[...] + r1[rows].astype(F32)
     other = r2[rows].astype(F32) + r3[rows].astype(F32)
-    half, near = eliminate(near, k1)
-    residues[:RHS] = half
-    half, other = eliminate(other, k1q)
-    residues[RHS : 2 * RHS] = half
-    half, value = eliminate(near + other, k2)
-    residues[2 * RHS :] = half
+    half_1, gain_1, near = eliminate(near, k1)
+    half_1q, gain_1q, other = eliminate(other, k1q)
+    half_2, gain_2, value = eliminate(near + other, k2)
+    for k, block in enumerate((half_1, gain_1, half_1q, gain_1q, half_2, gain_2)):
+        residues[k * RHS : (k + 1) * RHS] = block
     rest[...] = value
     pass_on(flags, value, left)
 
@@ -326,7 +329,7 @@
         out_specs=[VMEM] * (3 + kept),
         out_shape=[
             message,
-            jax.ShapeDtypeStruct((3 * RHS, W), BF16),
+            jax.ShapeDtypeStruct((6 * RHS, W), BF16),
             jax.ShapeDtypeStruct((sums.shape[0] - 2 * RHS, W), F32),
         ]
         + [message] * kept,
@@ -339,8 +342,9 @@
 def climb_kernel(height, own, came, sums, flags, chosen, left, residue, rest):
     choose_rows(flag(flags, height - 1), own, came, chosen, left)
     total = sums[...] + came[SUMS : SUMS + sums.shape[0]].astype(F32)
-    half, value = eliminate(total, chosen)
-    residue[...] = half
+    half, gain, value = eliminate(total, chosen)
+    residue[:RHS] = half
+    residue[RHS:] = gain
     rest[...] = value
     pass_on(flags, value, left)
 
@@ -354,49 +358,52 @@
         out_shape=[
             message,
             message,
-            jax.ShapeDtypeStruct((RHS, W), BF16),
+            jax.ShapeDtypeStruct((2 * RHS, W), BF16),
             jax.ShapeDtypeStruct((sums.shape[0] - RHS, W), F32),
         ],
         compiler_params=PARAMS,
     )(own, came, sums, flags)
 
 
-def separator(residue, up, above):
+def separator(vectors, index, up, above):
     distance = up[FAR_B : FAR_B + RHS].astype(F32)
     known = jnp.zeros((RHS, W), F32)
     for step, value in enumerate(above, 1):
         known = known + jnp.where(distance == float(step), value.astype(F32), 0.0)
+    gain = jnp.concatenate([jnp.zeros((SHARE, W), BF16), up[GAIN_B:FAR_B]], axis=0)
     return (
-        times(residue, up[2 * W : 3 * W])
+        part(vectors, 2 * index + 1).astype(F32)
+        + times(part(vectors, 2 * index), gain)
         - times(above[0], up[:W])
         - times(known.astype(BF16), up[W : 2 * W])
     ).astype(BF16)
 
 
 def top_kernel(
-    vectors, came, mine, flags, u3, u4, u3q, u5, u6, u7, near_out, other_out
+    vectors, late, came, mine, flags, u3, u4, u3q, u5, u6, u7, near_out, other_out
 ):
     wide = jnp.concatenate([flag(flags, UPPER - 1)] * 16, axis=0)
-    last = choose(wide, mine[2 * W : 3 * W], came[:W])
-    residue = part(vectors, 10).astype(F32) + came[W:].astype(F32)
+    own = jnp.concatenate([mine[:SHARE], mine[GAIN_B:FAR_B]], axis=0)
+    last = choose(wide, own, came[:W])
+    residue = part(late, 6).astype(F32) + came[W:].astype(F32)
     above = [times(residue.astype(BF16), last).astype(BF16)]
-    for index, up in ((9, u7), (7, u6), (6, u5), (5, u4)):
-        above = [separator(part(vectors, index), up, above)] + above
+    for source, index, up in ((late, 2, u7), (late, 0, u6), (vectors, 6, u5), (vectors, 5, u4)):
+        above = [separator(source, index, up, above)] + above
     for index, up, out in ((3, u3, near_out), (4, u3q, other_out)):
-        out[:RHS] = separator(part(vectors, index), up, above)
+        out[:RHS] = separator(vectors, index, up, above)
         for step, value in enumerate(above, 1):
             out[step * RHS : (step + 1) * RHS] = value
 
 
-def top(vectors, came, mine, flags, *ups):
+def top(vectors, late, came, mine, flags, *ups):
     known = jax.ShapeDtypeStruct(((UPPER - LOW) * RHS, W), BF16)
     return pl.pallas_call(
         top_kernel,
-        in_specs=[VMEM] * (4 + len(ups)),
+        in_specs=[VMEM] * (5 + len(ups)),
         out_specs=[VMEM] * 2,
         out_shape=[known, known],
         compiler_params=PARAMS,
-    )(vectors, came, mine, flags, *ups)
+    )(vectors, late, came, mine, flags, *ups)
 
 
 def select_known(cases, known):
@@ -418,9 +425,9 @@
         known,
     )
     above = [part(known, k) for k in range(UPPER - LOW)]
-    above = [separator(part(vectors, 2), u2, above)] + above
+    above = [separator(vectors, 2, u2, above)] + above
     for index, up, out in ((0, u1, near_out), (1, u1q, other_out)):
-        out[:RHS] = separator(part(vectors, index), up, above)
+        out[:RHS] = separator(vectors, index, up, above)
         for step, value in enumerate(above, 1):
             out[step * RHS : (step + 1) * RHS] = value
 
@@ -490,14 +497,16 @@
     came = send(message, across(4 * (LEADERS[0] ^ LEADERS[1])))
     up_5, message, residue_5, sums = climb(5, message, came, sums, flags)
     came = {k: send(message, across(32 * k)) for k in (2, 1, 3)}
+    vectors = jnp.concatenate([residues_y, residues_z, residue_5], axis=0)
+    vectors = send(vectors, seats(((0, 1),)))
     came = [came[k] for k in (1, 2, 3)]
     ups_x, message, residues_x, sums = gather(6, message, came, sums, flags, False)
     root = sums.astype(BF16)
     across_came = send(jnp.concatenate([message[:W], root], axis=0), layers(0, 1))
-    vectors = jnp.concatenate([residues_y, residues_z, residue_5, residues_x, root], axis=0)
-    vectors = send(vectors, seats(((0, 1),)))
+    late = jnp.concatenate([residues_x, root], axis=0)
+    late = send(late, seats(((0, 1),)))
     known, known_other = top(
-        vectors, across_came, message, flags, *ups_z, up_5, *ups_x
+        vectors, late, across_came, message, flags, *ups_z, up_5, *ups_x
     )
     a = send(known, from_leaders(1))
     b = send(known_other, from_leaders(2))

time: 93.6 us -> 89.5 us (0.956)
  waiting for transfers between devices: 67.6 us -> 63.4 us
    ppermute x18 -> x19, waiting for transfers between devices: 67.6 us -> 63.4 us  [send(): return lax.ppermute(value, AXES, pairs)]
    ppermute x18 -> x19, starting transfers between devices: 18 us -> 17.4 us  [send(): return lax.ppermute(value, AXES, pairs)]
  transfers between devices with their start and end apart: 18 -> 19, of which waited for: 3 -> 3; matrix products, arithmetic and copies ran while one was open for 0% -> 0% of each run, Pallas kernels for 0% -> 1%
where the time goes in v6:
time: 89.5 us; the launch traced here: 88.3 us
  waiting for transfers between devices  63.4 us (71%)
  starting transfers between devices  17.4 us (19%)
  Pallas kernels  7.04 us (8%)
    ppermute x19, waiting for transfers between devices, send(): return lax.ppermute(value, AXES, pairs)  63.4 us
    ppermute x19, starting transfers between devices, send(): return lax.ppermute(value, AXES, pairs)  17.4 us
    pallas_call x1, Pallas kernels, begin(): pl.pallas_call(begin_kernel, in_specs=[HBM] * 8, out_specs=[VMEM] * 7, ou...  2.54 us
  transfers between devices with their start and end apart: 19, of which 3 were waited for; matrix products, arithmetic and copies ran while one was open for 0% of the time, Pallas kernels for 1%

profile of v6, /device:TPU:24, one launch (start us, length us, event | category | flops | bytes accessed | tf_op | source)
XLA Modules:
  0.0 88.3 jit_solution(8091721037976235782)
XLA Ops:
  0.0 2.5 %shard_map.82 = (bf16[720,256]{1,0:T(8,128)(2,1)S(1)}, bf16[720,256]{1,0:T(8,128)(2,1)S(1)}, f32[3,16,256]{2,1,0:T(8,128)S(1)}, f32[128,256]{1,0:T(8,128)S(1)}, ...) custom-call(f32[1,4,16,256]{3,2,1,0:T(8,128)} %rights_in.1, ...), custom_call_target="tpu_custom_call" | custom-call | tf_op jit(solution)/shard_map/pallas_call | solution.py:233
  2.5 3.2 %collective-permute-start = (bf16[720,256]{1,0:T(8,128)(2,1)S(1)}, bf16[720,256]{1,0:T(8,128)(2,1)S(1)}, u32[]{:S(2)}, u32[]{:S(2)}) collective-permute-start(bf16[720,256]{1,0:T(8,128)(2,1)S(1)} %get-tuple-element.40.own), channel_id=1, source_target_pairs={{2,0},{3,1},{6,4},{7,5},{10,8},{11,9},{14,12},{15,13},{18,16},{19,... | collective-permute-start | bytes 1105928 | tf_op jit(solution)/shard_map/ppermute | solution.py:45
  5.7 2.0 %collective-permute-start.2 = (bf16[720,256]{1,0:T(8,128)(2,1)S(1)}, bf16[720,256]{1,0:T(8,128)(2,1)S(1)}, u32[]{:S(2)}, u32[]{:S(2)}) collective-permute-start(bf16[720,256]{1,0:T(8,128)(2,1)S(1)} %get-tuple-element.41), channel_id=1, source_target_pairs={{3,0},{2,1},{7,4},{6,5},{11,8},{10,9},{15,12},{14,13},{19,16},{18,... | collective-permute-start | bytes 1105928 | tf_op jit(solution)/shard_map/ppermute | solution.py:45
  7.7 0.7 collective-permute-start.1
  8.4 5.3 %collective-permute-done.r2 = bf16[720,256]{1,0:T(8,128)(2,1)S(1)} collective-permute-done((bf16[720,256]{1,0:T(8,128)(2,1)S(1)}, bf16[720,256]{1,0:T(8,128)(2,1)S(1)}, u32[]{:S(2)}, u32[]{:S(2)}) %collective-permute-start) | collective-permute-done | bytes 368672 | tf_op jit(solution)/shard_map/ppermute | solution.py:45
  13.7 2.2 %collective-permute-done.2.r3 = bf16[720,256]{1,0:T(8,128)(2,1)S(1)} collective-permute-done((bf16[720,256]{1,0:T(8,128)(2,1)S(1)}, bf16[720,256]{1,0:T(8,128)(2,1)S(1)}, u32[]{:S(2)}, u32[]{:S(2)}) %collective-permute-start.2) | collective-permute-done | bytes 368672 | tf_op jit(solution)/shard_map/ppermute | solution.py:45
  15.9 0.0 collective-permute-done.1.r1
  15.9 0.5 shard_map.83
  16.4 0.7 collective-permute-start.5
  17.1 0.7 collective-permute-start.4
  17.8 0.7 collective-permute-start.3
  18.5 0.0 collective-permute-done.5.r3
  18.5 0.0 collective-permute-done.4.r1
  18.5 0.0 collective-permute-done.3.r2
  18.5 0.5 shard_map.84
  19.1 0.7 collective-permute-start.6
  19.8 0.0 collective-permute-done.6.came
  19.8 0.2 shard_map.85
  20.0 0.7 collective-permute-start.10
  20.7 0.7 collective-permute-start.9
  21.4 0.7 collective-permute-start.8
  22.1 0.7 collective-permute-start.7
  22.8 0.0 collective-permute-done.10.r3
  22.8 0.0 collective-permute-done.9.r1
  22.8 0.0 collective-permute-done.8.r2
  22.8 0.6 shard_map.86
  23.4 0.7 collective-permute-start.12
  24.1 0.7 collective-permute-start.11
  24.8 0.0 collective-permute-done.7.vectors
  24.8 0.0 collective-permute-done.11.late
  24.8 0.0 collective-permute-done.12.came
  24.8 0.0 copy-start.1
  24.9 0.8 shard_map.87
  25.7 0.0 copy-start
  25.7 0.8 collective-permute-start.13
  26.5 0.7 collective-permute-start.15
  27.2 0.7 collective-permute-start.14
  27.8 0.0 collective-permute-done.13.a
  27.8 0.0 collective-permute-done.15.c
  27.8 0.0 collective-permute-done.14.b
  27.9 0.4 shard_map.88
  28.2 0.7 collective-permute-start.16
  28.9 1.3 %collective-permute-start.18 = (bf16[128,256]{1,0:T(8,128)(2,1)S(1)}, bf16[128,256]{1,0:T(8,128)(2,1)S(1)}, u32[]{:S(2)}, u32[]{:S(2)}) collective-permute-start(bf16[128,256]{1,0:T(8,128)(2,1)S(1)} %get-tuple-element.68), channel_id=1, source_target_pairs={{1,3},{5,7},{9,11},{13,15},{17,19},{21,23},{25,27},{29,31},{33,35}... | collective-permute-start | bytes 196616 | tf_op jit(solution)/shard_map/ppermute | solution.py:45
  30.2 0.7 collective-permute-start.17
  30.9 0.0 collective-permute-done.16.a
  30.9 55.9 %collective-permute-done.18.c = bf16[128,256]{1,0:T(8,128)(2,1)S(1)} collective-permute-done((bf16[128,256]{1,0:T(8,128)(2,1)S(1)}, bf16[128,256]{1,0:T(8,128)(2,1)S(1)}, u32[]{:S(2)}, u32[]{:S(2)}) %collective-permute-start.18) | collective-permute-done | bytes 65568 | tf_op jit(solution)/shard_map/ppermute | solution.py:45
  86.8 0.0 collective-permute-done.17.b
  86.8 0.0 copy-done.1
  86.9 0.0 copy-done
  86.9 1.4 %shard_map.89 = f32[1,4,16,256]{3,2,1,0:T(8,128)} custom-call(bf16[1,4,256,256]{3,2,1,0:T(8,128)(2,1)S(1)} %copy-done.1, bf16[1,4,2,256,256]{4,3,2,1,0:T(8,128)(2,1)S(1)} %copy-done, f32[96,256]{1,0:T(8,128)S(1)} %get-tuple-element.37.slots, f32[16,256]{1,0:T(8,128)S(1)} %get-tuple-element.38.level, f32[3,16,256]{2,1,0:T(8,128)S(1)} %get-tuple-element.39.solved, ...), custom_call_target="tpu_custom_call" | custom-call | tf_op jit(solution)/shard_map/pallas_call | solution.py:476
  (5 shorter events, 0.0 us)
Async XLA Ops:
  2.5 11.1 %collective-permute-start = (bf16[720,256]{1,0:T(8,128)(2,1)S(1)}, bf16[720,256]{1,0:T(8,128)(2,1)S(1)}, u32[]{:S(2)}, u32[]{:S(2)}) collective-permute-start(bf16[720,256]{1,0:T(8,128)(2,1)S(1)} %get-tuple-element.40.own), channel_id=1, source_target_pairs={{2,0},{3,1},{6,4},{7,5},{10,8},{11,9},{14,12},{15,13},{18,16},{19,... | collective-permute-start | bytes 1105928 | tf_op jit(solution)/shard_map/ppermute | solution.py:45
  5.7 10.2 %collective-permute-start.2 = (bf16[720,256]{1,0:T(8,128)(2,1)S(1)}, bf16[720,256]{1,0:T(8,128)(2,1)S(1)}, u32[]{:S(2)}, u32[]{:S(2)}) collective-permute-start(bf16[720,256]{1,0:T(8,128)(2,1)S(1)} %get-tuple-element.41), channel_id=1, source_target_pairs={{3,0},{2,1},{7,4},{6,5},{11,8},{10,9},{15,12},{14,13},{19,16},{18,... | collective-permute-start | bytes 1105928 | tf_op jit(solution)/shard_map/ppermute | solution.py:45
  7.7 8.2 %collective-permute-start.1 = (bf16[720,256]{1,0:T(8,128)(2,1)S(1)}, bf16[720,256]{1,0:T(8,128)(2,1)S(1)}, u32[]{:S(2)}, u32[]{:S(2)}) collective-permute-start(bf16[720,256]{1,0:T(8,128)(2,1)S(1)} %get-tuple-element.41), channel_id=1, source_target_pairs={{1,0},{0,1},{5,4},{4,5},{9,8},{8,9},{13,12},{12,13},{17,16},{16,17... | collective-permute-start | bytes 1105928 | tf_op jit(solution)/shard_map/ppermute | solution.py:45
  16.4 2.1 %collective-permute-start.5 = (bf16[720,256]{1,0:T(8,128)(2,1)S(1)}, bf16[720,256]{1,0:T(8,128)(2,1)S(1)}, u32[]{:S(2)}, u32[]{:S(2)}) collective-permute-start(bf16[720,256]{1,0:T(8,128)(2,1)S(1)} %get-tuple-element.45.own), channel_id=1, source_target_pairs={{4,8},{5,9},{24,20},{25,21},{36,40},{37,41},{56,52},{57,53},{68,72... | collective-permute-start | bytes 1105928 | tf_op jit(solution)/shard_map/ppermute | solution.py:45
  17.1 1.4 %collective-permute-start.4 = (bf16[720,256]{1,0:T(8,128)(2,1)S(1)}, bf16[720,256]{1,0:T(8,128)(2,1)S(1)}, u32[]{:S(2)}, u32[]{:S(2)}) collective-permute-start(bf16[720,256]{1,0:T(8,128)(2,1)S(1)} %get-tuple-element.45.own), channel_id=1, source_target_pairs={{12,8},{13,9},{16,20},{17,21},{44,40},{45,41},{48,52},{49,53},{76,... | collective-permute-start | bytes 1105928 | tf_op jit(solution)/shard_map/ppermute | solution.py:45
  17.8 0.7 collective-permute-start.3
  19.1 0.7 collective-permute-start.6
  20.0 2.8 %collective-permute-start.10 = (bf16[720,256]{1,0:T(8,128)(2,1)S(1)}, bf16[720,256]{1,0:T(8,128)(2,1)S(1)}, u32[]{:S(2)}, u32[]{:S(2)}) collective-permute-start(bf16[720,256]{1,0:T(8,128)(2,1)S(1)} %get-tuple-element.51.own), channel_id=1, source_target_pairs={{8,104},{9,105},{20,116},{21,117},{40,72},{41,73},{52,84},{53,85},... | collective-permute-start | bytes 1105928 | tf_op jit(solution)/shard_map/ppermute | solution.py:45
  20.7 2.1 %collective-permute-start.9 = (bf16[720,256]{1,0:T(8,128)(2,1)S(1)}, bf16[720,256]{1,0:T(8,128)(2,1)S(1)}, u32[]{:S(2)}, u32[]{:S(2)}) collective-permute-start(bf16[720,256]{1,0:T(8,128)(2,1)S(1)} %get-tuple-element.51.own), channel_id=1, source_target_pairs={{8,40},{9,41},{20,52},{21,53},{40,8},{41,9},{52,20},{53,21},{72,10... | collective-permute-start | bytes 1105928 | tf_op jit(solution)/shard_map/ppermute | solution.py:45
  21.4 1.4 %collective-permute-start.8 = (bf16[720,256]{1,0:T(8,128)(2,1)S(1)}, bf16[720,256]{1,0:T(8,128)(2,1)S(1)}, u32[]{:S(2)}, u32[]{:S(2)}) collective-permute-start(bf16[720,256]{1,0:T(8,128)(2,1)S(1)} %get-tuple-element.51.own), channel_id=1, source_target_pairs={{8,72},{9,73},{20,84},{21,85},{40,104},{41,105},{52,116},{53,117},... | collective-permute-start | bytes 1105928 | tf_op jit(solution)/shard_map/ppermute | solution.py:45
  22.1 2.7 %collective-permute-start.7 = (bf16[224,256]{1,0:T(8,128)(2,1)S(1)}, bf16[224,256]{1,0:T(8,128)(2,1)S(1)}, u32[]{:S(2)}, u32[]{:S(2)}) collective-permute-start(bf16[224,256]{1,0:T(8,128)(2,1)S(1)} %pad_maximum_fusion.1), channel_id=1, source_target_pairs={{0,1},{4,5},{8,9},{12,13},{16,17},{20,21},{24,25},{28,29},{32,33},... | collective-permute-start | bytes 344072 | tf_op jit(solution)/shard_map/ppermute | solution.py:45
  23.4 1.4 %collective-permute-start.12 = (bf16[272,256]{1,0:T(8,128)(2,1)S(1)}, bf16[272,256]{1,0:T(8,128)(2,1)S(1)}, u32[]{:S(2)}, u32[]{:S(2)}) collective-permute-start(bf16[272,256]{1,0:T(8,128)(2,1)S(1)} %pad_maximum_fusion), channel_id=1, source_target_pairs={{8,139},{20,151},{40,171},{52,183},{72,203},{84,215},{104,235},{11... | collective-permute-start | bytes 417800 | tf_op jit(solution)/shard_map/ppermute | solution.py:45
  24.1 0.7 collective-permute-start.11
  24.8 62.0 %copy-start.1 = (bf16[1,4,256,256]{3,2,1,0:T(8,128)(2,1)S(1)}, bf16[1,4,256,256]{3,2,1,0:T(8,128)(2,1)}, u32[]{:S(2)}) copy-start(bf16[1,4,256,256]{3,2,1,0:T(8,128)(2,1)} %uinv.1) | copy-start | bytes 1572868
  25.7 61.2 %copy-start = (bf16[1,4,2,256,256]{4,3,2,1,0:T(8,128)(2,1)S(1)}, bf16[1,4,2,256,256]{4,3,2,1,0:T(8,128)(2,1)}, u32[]{:S(2)}) copy-start(bf16[1,4,2,256,256]{4,3,2,1,0:T(8,128)(2,1)} %ublk.1) | copy-start | bytes 3145732
  25.7 2.2 %collective-permute-start.13 = (bf16[96,256]{1,0:T(8,128)(2,1)S(1)}, bf16[96,256]{1,0:T(8,128)(2,1)S(1)}, u32[]{:S(2)}, u32[]{:S(2)}) collective-permute-start(bf16[96,256]{1,0:T(8,128)(2,1)S(1)} %get-tuple-element.62.own), channel_id=1, source_target_pairs={{9,13},{21,17},{41,45},{53,49},{73,77},{85,81},{105,109},{117,113}... | collective-permute-start | bytes 147464 | tf_op jit(solution)/shard_map/ppermute | solution.py:45
  26.5 1.4 %collective-permute-start.15 = (bf16[96,256]{1,0:T(8,128)(2,1)S(1)}, bf16[96,256]{1,0:T(8,128)(2,1)S(1)}, u32[]{:S(2)}, u32[]{:S(2)}) collective-permute-start(bf16[96,256]{1,0:T(8,128)(2,1)S(1)} %get-tuple-element.63), channel_id=1, source_target_pairs={{9,5},{21,25},{41,37},{53,57},{73,69},{85,89},{105,101},{117,121},... | collective-permute-start | bytes 147464 | tf_op jit(solution)/shard_map/ppermute | solution.py:45
  27.2 0.7 collective-permute-start.14
  28.2 2.7 %collective-permute-start.16 = (bf16[128,256]{1,0:T(8,128)(2,1)S(1)}, bf16[128,256]{1,0:T(8,128)(2,1)S(1)}, u32[]{:S(2)}, u32[]{:S(2)}) collective-permute-start(bf16[128,256]{1,0:T(8,128)(2,1)S(1)} %get-tuple-element.67.own), channel_id=1, source_target_pairs={{1,0},{5,4},{9,8},{13,12},{17,16},{21,20},{25,24},{29,28},{33,32},... | collective-permute-start | bytes 196616 | tf_op jit(solution)/shard_map/ppermute | solution.py:45
  28.9 57.9 %collective-permute-start.18 = (bf16[128,256]{1,0:T(8,128)(2,1)S(1)}, bf16[128,256]{1,0:T(8,128)(2,1)S(1)}, u32[]{:S(2)}, u32[]{:S(2)}) collective-permute-start(bf16[128,256]{1,0:T(8,128)(2,1)S(1)} %get-tuple-element.68), channel_id=1, source_target_pairs={{1,3},{5,7},{9,11},{13,15},{17,19},{21,23},{25,27},{29,31},{33,35}... | collective-permute-start | bytes 196616 | tf_op jit(solution)/shard_map/ppermute | solution.py:45
  30.2 56.6 %collective-permute-start.17 = (bf16[128,256]{1,0:T(8,128)(2,1)S(1)}, bf16[128,256]{1,0:T(8,128)(2,1)S(1)}, u32[]{:S(2)}, u32[]{:S(2)}) collective-permute-start(bf16[128,256]{1,0:T(8,128)(2,1)S(1)} %get-tuple-element.68), channel_id=1, source_target_pairs={{1,2},{5,6},{9,10},{13,14},{17,18},{21,22},{25,26},{29,30},{33,34}... | collective-permute-start | bytes 196616 | tf_op jit(solution)/shard_map/ppermute | solution.py:45

commit v7 on v6

--- a/solution.py
+++ b/solution.py
@@ -21,9 +21,10 @@
 GAIN_A = FAR_A + RHS
 SUMS = GAIN_A + SHARE
 GAIN_B = 2 * W
-FAR_B = GAIN_B + W - SHARE
-ROWS = FAR_B + RHS
+ROWS = GAIN_B + W - SHARE
+ROWS_Y = SUMS + UPPER * RHS
 GATHERS = (1, 3, 6)
+ORDER = {1: (2, 1, 3), 3: (2, 1, 3), 6: (1, 2, 3)}
 OTHER_PAIR = {low: UPPER + k for k, low in enumerate(GATHERS)}
 ROLE_A = UPPER + len(GATHERS)
 FLAGS = ROLE_A + 1
@@ -217,8 +218,8 @@
         up[:SHARE] = choose(wide[:SHARE], up_blocks[2][:SHARE], up_blocks[0][:SHARE])
         up[SHARE:W] = up_blocks[0][SHARE:]
         up[W : 2 * W] = up_blocks[1]
-        up[GAIN_B:FAR_B] = up_blocks[2][SHARE:]
-        up[FAR_B:] = distance
+        up[GAIN_B:ROWS] = up_blocks[2][SHARE:]
+        up[ROWS:] = jnp.zeros((ROWS_Y - ROWS, W), BF16)
 
     @pl.when(place % 2 == 0)
     def _():
@@ -235,8 +236,8 @@
         in_specs=[HBM] * 8,
         out_specs=[VMEM] * 7,
         out_shape=[
-            jax.ShapeDtypeStruct((ROWS, W), BF16),
-            jax.ShapeDtypeStruct((ROWS, W), BF16),
+            jax.ShapeDtypeStruct((ROWS_Y, W), BF16),
+            jax.ShapeDtypeStruct((ROWS_Y, W), BF16),
             jax.ShapeDtypeStruct((LOCAL_COUNT, RHS, W), F32),
             jax.ShapeDtypeStruct((UPPER * RHS, W), F32),
             jax.ShapeDtypeStruct((FLAGS * RHS, W), BF16),
@@ -303,8 +304,9 @@
 
 
 def gather_kernel(
-    height, own, r2, r1, r3, sums, flags, left, residues, rest, k1, k2, k1q, lp, lq
+    height, own, a, b, c, sums, flags, left, residues, rest, k1, k2, k1q, lp, lq
 ):
+    r1, r2, r3 = (dict(zip(ORDER[height], (a, b, c)))[k] for k in (1, 2, 3))
     choose_rows(flag(flags, height - 1), own, r1, k1, lp)
     choose_rows(flag(flags, OTHER_PAIR[height]), r2, r3, k1q, lq)
     choose_rows(flag(flags, height), lp, lq, k2, left)
@@ -316,6 +318,11 @@
     half_2, gain_2, value = eliminate(near + other, k2)
     for k, block in enumerate((half_1, gain_1, half_1q, gain_1q, half_2, gain_2)):
         residues[k * RHS : (k + 1) * RHS] = block
+    row = lax.broadcasted_iota(jnp.int32, (RHS, W), 0)
+    far_1, far_1q, far_2 = (k[FAR_A:GAIN_A].astype(F32) for k in (k1, k1q, k2))
+    residues[6 * RHS :] = jnp.where(
+        row == 0, far_1, jnp.where(row == 1, far_1q, far_2)
+    ).astype(BF16)
     rest[...] = value
     pass_on(flags, value, left)
 
@@ -329,13 +336,13 @@
         out_specs=[VMEM] * (3 + kept),
         out_shape=[
             message,
-            jax.ShapeDtypeStruct((6 * RHS, W), BF16),
+            jax.ShapeDtypeStruct((7 * RHS, W), BF16),
             jax.ShapeDtypeStruct((sums.shape[0] - 2 * RHS, W), F32),
         ]
         + [message] * kept,
         scratch_shapes=[pltpu.VMEM((ROWS, W), BF16)] * (5 - kept),
         compiler_params=PARAMS,
-    )(own, came[1], came[0], came[2], sums, flags)
+    )(own, *[came[k - 1] for k in ORDER[height]], sums, flags)
     return ups, left, residues, rest
 
 
@@ -344,7 +351,8 @@
     total = sums[...] + came[SUMS : SUMS + sums.shape[0]].astype(F32)
     half, gain, value = eliminate(total, chosen)
     residue[:RHS] = half
-    residue[RHS:] = gain
+    residue[RHS : 2 * RHS] = gain
+    residue[2 * RHS :] = chosen[FAR_A:GAIN_A]
     rest[...] = value
     pass_on(flags, value, left)
 
@@ -358,22 +366,23 @@
         out_shape=[
             message,
             message,
-            jax.ShapeDtypeStruct((2 * RHS, W), BF16),
+            jax.ShapeDtypeStruct((3 * RHS, W), BF16),
             jax.ShapeDtypeStruct((sums.shape[0] - RHS, W), F32),
         ],
         compiler_params=PARAMS,
     )(own, came, sums, flags)
 
 
-def separator(vectors, index, up, above):
-    distance = up[FAR_B : FAR_B + RHS].astype(F32)
+def separator(vectors, place, up, above):
+    start, distances, index = place
+    distance = part(vectors, distances).astype(F32)[index : index + 1]
     known = jnp.zeros((RHS, W), F32)
     for step, value in enumerate(above, 1):
         known = known + jnp.where(distance == float(step), value.astype(F32), 0.0)
-    gain = jnp.concatenate([jnp.zeros((SHARE, W), BF16), up[GAIN_B:FAR_B]], axis=0)
+    gain = jnp.concatenate([jnp.zeros((SHARE, W), BF16), up[GAIN_B:ROWS]], axis=0)
     return (
-        part(vectors, 2 * index + 1).astype(F32)
-        + times(part(vectors, 2 * index), gain)
+        part(vectors, start + 2 * index + 1).astype(F32)
+        + times(part(vectors, start + 2 * index), gain)
         - times(above[0], up[:W])
         - times(known.astype(BF16), up[W : 2 * W])
     ).astype(BF16)
@@ -383,13 +392,18 @@
     vectors, late, came, mine, flags, u3, u4, u3q, u5, u6, u7, near_out, other_out
 ):
     wide = jnp.concatenate([flag(flags, UPPER - 1)] * 16, axis=0)
-    own = jnp.concatenate([mine[:SHARE], mine[GAIN_B:FAR_B]], axis=0)
+    own = jnp.concatenate([mine[:SHARE], mine[GAIN_B:ROWS]], axis=0)
     last = choose(wide, own, came[:W])
-    residue = part(late, 6).astype(F32) + came[W:].astype(F32)
+    residue = part(late, 7).astype(F32) + came[W:].astype(F32)
     above = [times(residue.astype(BF16), last).astype(BF16)]
-    for source, index, up in ((late, 2, u7), (late, 0, u6), (vectors, 6, u5), (vectors, 5, u4)):
+    for source, index, up in (
+        (late, (0, 6, 2), u7),
+        (late, (0, 6, 0), u6),
+        (vectors, (14, 16, 0), u5),
+        (vectors, (7, 13, 2), u4),
+    ):
         above = [separator(source, index, up, above)] + above
-    for index, up, out in ((3, u3, near_out), (4, u3q, other_out)):
+    for index, up, out in (((7, 13, 0), u3, near_out), ((7, 13, 1), u3q, other_out)):
         out[:RHS] = separator(vectors, index, up, above)
         for step, value in enumerate(above, 1):
             out[step * RHS : (step + 1) * RHS] = value
@@ -425,8 +439,8 @@
         known,
     )
     above = [part(known, k) for k in range(UPPER - LOW)]
-    above = [separator(vectors, 2, u2, above)] + above
-    for index, up, out in ((0, u1, near_out), (1, u1q, other_out)):
+    above = [separator(vectors, (0, 6, 2), u2, above)] + above
+    for index, up, out in (((0, 6, 0), u1, near_out), ((0, 6, 1), u1q, other_out)):
         out[:RHS] = separator(vectors, index, up, above)
         for step, value in enumerate(above, 1):
             out[step * RHS : (step + 1) * RHS] = value

time: 89.5 us -> 88.5 us (0.989)
  waiting for transfers between devices: 63.4 us -> 62.5 us
    ppermute x19, waiting for transfers between devices: 63.4 us -> 62.5 us  [send(): return lax.ppermute(value, AXES, pairs)]
where the time goes in v7:
time: 88.5 us; the launch traced here: 87.3 us
  waiting for transfers between devices  62.5 us (71%)
  starting transfers between devices  17.4 us (20%)
  Pallas kernels  7.03 us (8%)
    ppermute x19, waiting for transfers between devices, send(): return lax.ppermute(value, AXES, pairs)  62.5 us
    ppermute x19, starting transfers between devices, send(): return lax.ppermute(value, AXES, pairs)  17.4 us
    pallas_call x1, Pallas kernels, begin(): pl.pallas_call(begin_kernel, in_specs=[HBM] * 8, out_specs=[VMEM] * 7, ou...  2.54 us
  transfers between devices with their start and end apart: 19, of which 3 were waited for; matrix products, arithmetic and copies ran while one was open for 0% of the time, Pallas kernels for 1%

profile of v7, /device:TPU:24, one launch (start us, length us, event | category | flops | bytes accessed | tf_op | source)
XLA Modules:
  0.0 87.3 jit_solution(10375197692626690056)
XLA Ops:
  0.0 2.5 %shard_map.82 = (bf16[720,256]{1,0:T(8,128)(2,1)S(1)}, bf16[720,256]{1,0:T(8,128)(2,1)S(1)}, f32[3,16,256]{2,1,0:T(8,128)S(1)}, f32[128,256]{1,0:T(8,128)S(1)}, ...) custom-call(f32[1,4,16,256]{3,2,1,0:T(8,128)} %rights_in.1, ...), custom_call_target="tpu_custom_call" | custom-call | tf_op jit(solution)/shard_map/pallas_call | solution.py:234
  2.5 3.2 %collective-permute-start = (bf16[720,256]{1,0:T(8,128)(2,1)S(1)}, bf16[720,256]{1,0:T(8,128)(2,1)S(1)}, u32[]{:S(2)}, u32[]{:S(2)}) collective-permute-start(bf16[720,256]{1,0:T(8,128)(2,1)S(1)} %get-tuple-element.40.own), channel_id=1, source_target_pairs={{2,0},{3,1},{6,4},{7,5},{10,8},{11,9},{14,12},{15,13},{18,16},{19,... | collective-permute-start | bytes 1105928 | tf_op jit(solution)/shard_map/ppermute | solution.py:46
  5.7 2.0 %collective-permute-start.2 = (bf16[720,256]{1,0:T(8,128)(2,1)S(1)}, bf16[720,256]{1,0:T(8,128)(2,1)S(1)}, u32[]{:S(2)}, u32[]{:S(2)}) collective-permute-start(bf16[720,256]{1,0:T(8,128)(2,1)S(1)} %get-tuple-element.41), channel_id=1, source_target_pairs={{3,0},{2,1},{7,4},{6,5},{11,8},{10,9},{15,12},{14,13},{19,16},{18,... | collective-permute-start | bytes 1105928 | tf_op jit(solution)/shard_map/ppermute | solution.py:46
  7.7 0.7 collective-permute-start.1
  8.4 5.3 %collective-permute-done.a = bf16[720,256]{1,0:T(8,128)(2,1)S(1)} collective-permute-done((bf16[720,256]{1,0:T(8,128)(2,1)S(1)}, bf16[720,256]{1,0:T(8,128)(2,1)S(1)}, u32[]{:S(2)}, u32[]{:S(2)}) %collective-permute-start) | collective-permute-done | bytes 368672 | tf_op jit(solution)/shard_map/ppermute | solution.py:46
  13.7 2.2 %collective-permute-done.2.c = bf16[720,256]{1,0:T(8,128)(2,1)S(1)} collective-permute-done((bf16[720,256]{1,0:T(8,128)(2,1)S(1)}, bf16[720,256]{1,0:T(8,128)(2,1)S(1)}, u32[]{:S(2)}, u32[]{:S(2)}) %collective-permute-start.2) | collective-permute-done | bytes 368672 | tf_op jit(solution)/shard_map/ppermute | solution.py:46
  15.9 0.0 collective-permute-done.1.b
  15.9 0.5 shard_map.83
  16.4 0.7 collective-permute-start.5
  17.1 0.7 collective-permute-start.4
  17.8 0.7 collective-permute-start.3
  18.5 0.0 collective-permute-done.5.c
  18.5 0.0 collective-permute-done.4.b
  18.5 0.0 collective-permute-done.3.a
  18.5 0.5 shard_map.84
  19.1 0.7 collective-permute-start.6
  19.7 0.0 collective-permute-done.6.came
  19.8 0.2 shard_map.85
  20.0 0.7 collective-permute-start.10
  20.7 0.7 collective-permute-start.9
  21.4 0.7 collective-permute-start.8
  22.1 0.7 collective-permute-start.7
  22.8 0.0 collective-permute-done.10.c
  22.8 0.0 collective-permute-done.9.b
  22.8 0.0 collective-permute-done.8.a
  22.8 0.6 shard_map.86
  23.4 0.7 collective-permute-start.12
  24.1 0.7 collective-permute-start.11
  24.8 0.0 collective-permute-done.7.vectors
  24.8 0.0 collective-permute-done.11.late
  24.8 0.0 collective-permute-done.12.came
  24.8 0.0 copy-start.1
  24.8 0.8 shard_map.87
  25.6 0.0 copy-start
  25.7 0.8 collective-permute-start.13
  26.5 0.7 collective-permute-start.15
  27.1 0.7 collective-permute-start.14
  27.8 0.0 collective-permute-done.13.a
  27.8 0.0 collective-permute-done.15.c
  27.8 0.0 collective-permute-done.14.b
  27.8 0.4 shard_map.88
  28.2 0.7 collective-permute-start.16
  28.9 1.3 %collective-permute-start.18 = (bf16[128,256]{1,0:T(8,128)(2,1)S(1)}, bf16[128,256]{1,0:T(8,128)(2,1)S(1)}, u32[]{:S(2)}, u32[]{:S(2)}) collective-permute-start(bf16[128,256]{1,0:T(8,128)(2,1)S(1)} %get-tuple-element.68), channel_id=1, source_target_pairs={{1,3},{5,7},{9,11},{13,15},{17,19},{21,23},{25,27},{29,31},{33,35}... | collective-permute-start | bytes 196616 | tf_op jit(solution)/shard_map/ppermute | solution.py:46
  30.2 0.7 collective-permute-start.17
  30.9 0.0 collective-permute-done.16.a
  30.9 55.0 %collective-permute-done.18.c = bf16[128,256]{1,0:T(8,128)(2,1)S(1)} collective-permute-done((bf16[128,256]{1,0:T(8,128)(2,1)S(1)}, bf16[128,256]{1,0:T(8,128)(2,1)S(1)}, u32[]{:S(2)}, u32[]{:S(2)}) %collective-permute-start.18) | collective-permute-done | bytes 65568 | tf_op jit(solution)/shard_map/ppermute | solution.py:46
  85.9 0.0 collective-permute-done.17.b
  85.9 0.0 copy-done.1
  85.9 0.0 copy-done
  85.9 1.4 %shard_map.89 = f32[1,4,16,256]{3,2,1,0:T(8,128)} custom-call(bf16[1,4,256,256]{3,2,1,0:T(8,128)(2,1)S(1)} %copy-done.1, bf16[1,4,2,256,256]{4,3,2,1,0:T(8,128)(2,1)S(1)} %copy-done, f32[96,256]{1,0:T(8,128)S(1)} %get-tuple-element.37.slots, f32[16,256]{1,0:T(8,128)S(1)} %get-tuple-element.38.level, f32[3,16,256]{2,1,0:T(8,128)S(1)} %get-tuple-element.39.solved, ...), custom_call_target="tpu_custom_call" | custom-call | tf_op jit(solution)/shard_map/pallas_call | solution.py:490
  (5 shorter events, 0.0 us)
Async XLA Ops:
  2.5 11.1 %collective-permute-start = (bf16[720,256]{1,0:T(8,128)(2,1)S(1)}, bf16[720,256]{1,0:T(8,128)(2,1)S(1)}, u32[]{:S(2)}, u32[]{:S(2)}) collective-permute-start(bf16[720,256]{1,0:T(8,128)(2,1)S(1)} %get-tuple-element.40.own), channel_id=1, source_target_pairs={{2,0},{3,1},{6,4},{7,5},{10,8},{11,9},{14,12},{15,13},{18,16},{19,... | collective-permute-start | bytes 1105928 | tf_op jit(solution)/shard_map/ppermute | solution.py:46
  5.7 10.2 %collective-permute-start.2 = (bf16[720,256]{1,0:T(8,128)(2,1)S(1)}, bf16[720,256]{1,0:T(8,128)(2,1)S(1)}, u32[]{:S(2)}, u32[]{:S(2)}) collective-permute-start(bf16[720,256]{1,0:T(8,128)(2,1)S(1)} %get-tuple-element.41), channel_id=1, source_target_pairs={{3,0},{2,1},{7,4},{6,5},{11,8},{10,9},{15,12},{14,13},{19,16},{18,... | collective-permute-start | bytes 1105928 | tf_op jit(solution)/shard_map/ppermute | solution.py:46
  7.7 8.2 %collective-permute-start.1 = (bf16[720,256]{1,0:T(8,128)(2,1)S(1)}, bf16[720,256]{1,0:T(8,128)(2,1)S(1)}, u32[]{:S(2)}, u32[]{:S(2)}) collective-permute-start(bf16[720,256]{1,0:T(8,128)(2,1)S(1)} %get-tuple-element.41), channel_id=1, source_target_pairs={{1,0},{0,1},{5,4},{4,5},{9,8},{8,9},{13,12},{12,13},{17,16},{16,17... | collective-permute-start | bytes 1105928 | tf_op jit(solution)/shard_map/ppermute | solution.py:46
  16.4 2.1 %collective-permute-start.5 = (bf16[704,256]{1,0:T(8,128)(2,1)S(1)}, bf16[704,256]{1,0:T(8,128)(2,1)S(1)}, u32[]{:S(2)}, u32[]{:S(2)}) collective-permute-start(bf16[704,256]{1,0:T(8,128)(2,1)S(1)} %get-tuple-element.45.own), channel_id=1, source_target_pairs={{4,8},{5,9},{24,20},{25,21},{36,40},{37,41},{56,52},{57,53},{68,72... | collective-permute-start | bytes 1081352 | tf_op jit(solution)/shard_map/ppermute | solution.py:46
  17.1 1.4 %collective-permute-start.4 = (bf16[704,256]{1,0:T(8,128)(2,1)S(1)}, bf16[704,256]{1,0:T(8,128)(2,1)S(1)}, u32[]{:S(2)}, u32[]{:S(2)}) collective-permute-start(bf16[704,256]{1,0:T(8,128)(2,1)S(1)} %get-tuple-element.45.own), channel_id=1, source_target_pairs={{12,8},{13,9},{16,20},{17,21},{44,40},{45,41},{48,52},{49,53},{76,... | collective-permute-start | bytes 1081352 | tf_op jit(solution)/shard_map/ppermute | solution.py:46
  17.8 0.7 collective-permute-start.3
  19.1 0.7 collective-permute-start.6
  20.0 2.8 %collective-permute-start.10 = (bf16[704,256]{1,0:T(8,128)(2,1)S(1)}, bf16[704,256]{1,0:T(8,128)(2,1)S(1)}, u32[]{:S(2)}, u32[]{:S(2)}) collective-permute-start(bf16[704,256]{1,0:T(8,128)(2,1)S(1)} %get-tuple-element.51.own), channel_id=1, source_target_pairs={{8,104},{9,105},{20,116},{21,117},{40,72},{41,73},{52,84},{53,85},... | collective-permute-start | bytes 1081352 | tf_op jit(solution)/shard_map/ppermute | solution.py:46
  20.7 2.1 %collective-permute-start.9 = (bf16[704,256]{1,0:T(8,128)(2,1)S(1)}, bf16[704,256]{1,0:T(8,128)(2,1)S(1)}, u32[]{:S(2)}, u32[]{:S(2)}) collective-permute-start(bf16[704,256]{1,0:T(8,128)(2,1)S(1)} %get-tuple-element.51.own), channel_id=1, source_target_pairs={{8,72},{9,73},{20,84},{21,85},{40,104},{41,105},{52,116},{53,117},... | collective-permute-start | bytes 1081352 | tf_op jit(solution)/shard_map/ppermute | solution.py:46
  21.4 1.4 %collective-permute-start.8 = (bf16[704,256]{1,0:T(8,128)(2,1)S(1)}, bf16[704,256]{1,0:T(8,128)(2,1)S(1)}, u32[]{:S(2)}, u32[]{:S(2)}) collective-permute-start(bf16[704,256]{1,0:T(8,128)(2,1)S(1)} %get-tuple-element.51.own), channel_id=1, source_target_pairs={{8,40},{9,41},{20,52},{21,53},{40,8},{41,9},{52,20},{53,21},{72,10... | collective-permute-start | bytes 1081352 | tf_op jit(solution)/shard_map/ppermute | solution.py:46
  22.1 2.7 %collective-permute-start.7 = (bf16[272,256]{1,0:T(8,128)(2,1)S(1)}, bf16[272,256]{1,0:T(8,128)(2,1)S(1)}, u32[]{:S(2)}, u32[]{:S(2)}) collective-permute-start(bf16[272,256]{1,0:T(8,128)(2,1)S(1)} %pad_maximum_fusion), channel_id=1, source_target_pairs={{0,1},{4,5},{8,9},{12,13},{16,17},{20,21},{24,25},{28,29},{32,33},... | collective-permute-start | bytes 417800 | tf_op jit(solution)/shard_map/ppermute | solution.py:46
  23.4 1.4 %collective-permute-start.12 = (bf16[272,256]{1,0:T(8,128)(2,1)S(1)}, bf16[272,256]{1,0:T(8,128)(2,1)S(1)}, u32[]{:S(2)}, u32[]{:S(2)}) collective-permute-start(bf16[272,256]{1,0:T(8,128)(2,1)S(1)} %pad_maximum_fusion.1), channel_id=1, source_target_pairs={{8,139},{20,151},{40,171},{52,183},{72,203},{84,215},{104,235},{11... | collective-permute-start | bytes 417800 | tf_op jit(solution)/shard_map/ppermute | solution.py:46
  24.1 0.7 collective-permute-start.11
  24.8 61.1 %copy-start.1 = (bf16[1,4,256,256]{3,2,1,0:T(8,128)(2,1)S(1)}, bf16[1,4,256,256]{3,2,1,0:T(8,128)(2,1)}, u32[]{:S(2)}) copy-start(bf16[1,4,256,256]{3,2,1,0:T(8,128)(2,1)} %uinv.1) | copy-start | bytes 1572868
  25.6 60.3 %copy-start = (bf16[1,4,2,256,256]{4,3,2,1,0:T(8,128)(2,1)S(1)}, bf16[1,4,2,256,256]{4,3,2,1,0:T(8,128)(2,1)}, u32[]{:S(2)}) copy-start(bf16[1,4,2,256,256]{4,3,2,1,0:T(8,128)(2,1)} %ublk.1) | copy-start | bytes 3145732
  25.7 2.2 %collective-permute-start.13 = (bf16[96,256]{1,0:T(8,128)(2,1)S(1)}, bf16[96,256]{1,0:T(8,128)(2,1)S(1)}, u32[]{:S(2)}, u32[]{:S(2)}) collective-permute-start(bf16[96,256]{1,0:T(8,128)(2,1)S(1)} %get-tuple-element.62.own), channel_id=1, source_target_pairs={{9,13},{21,17},{41,45},{53,49},{73,77},{85,81},{105,109},{117,113}... | collective-permute-start | bytes 147464 | tf_op jit(solution)/shard_map/ppermute | solution.py:46
  26.5 1.4 %collective-permute-start.15 = (bf16[96,256]{1,0:T(8,128)(2,1)S(1)}, bf16[96,256]{1,0:T(8,128)(2,1)S(1)}, u32[]{:S(2)}, u32[]{:S(2)}) collective-permute-start(bf16[96,256]{1,0:T(8,128)(2,1)S(1)} %get-tuple-element.63), channel_id=1, source_target_pairs={{9,5},{21,25},{41,37},{53,57},{73,69},{85,89},{105,101},{117,121},... | collective-permute-start | bytes 147464 | tf_op jit(solution)/shard_map/ppermute | solution.py:46
  27.1 0.7 collective-permute-start.14
  28.2 2.7 %collective-permute-start.16 = (bf16[128,256]{1,0:T(8,128)(2,1)S(1)}, bf16[128,256]{1,0:T(8,128)(2,1)S(1)}, u32[]{:S(2)}, u32[]{:S(2)}) collective-permute-start(bf16[128,256]{1,0:T(8,128)(2,1)S(1)} %get-tuple-element.67.own), channel_id=1, source_target_pairs={{1,0},{5,4},{9,8},{13,12},{17,16},{21,20},{25,24},{29,28},{33,32},... | collective-permute-start | bytes 196616 | tf_op jit(solution)/shard_map/ppermute | solution.py:46
  28.9 57.0 %collective-permute-start.18 = (bf16[128,256]{1,0:T(8,128)(2,1)S(1)}, bf16[128,256]{1,0:T(8,128)(2,1)S(1)}, u32[]{:S(2)}, u32[]{:S(2)}) collective-permute-start(bf16[128,256]{1,0:T(8,128)(2,1)S(1)} %get-tuple-element.68), channel_id=1, source_target_pairs={{1,3},{5,7},{9,11},{13,15},{17,19},{21,23},{25,27},{29,31},{33,35}... | collective-permute-start | bytes 196616 | tf_op jit(solution)/shard_map/ppermute | solution.py:46
  30.2 55.7 %collective-permute-start.17 = (bf16[128,256]{1,0:T(8,128)(2,1)S(1)}, bf16[128,256]{1,0:T(8,128)(2,1)S(1)}, u32[]{:S(2)}, u32[]{:S(2)}) collective-permute-start(bf16[128,256]{1,0:T(8,128)(2,1)S(1)} %get-tuple-element.68), channel_id=1, source_target_pairs={{1,2},{5,6},{9,10},{13,14},{17,18},{21,22},{25,26},{29,30},{33,34}... | collective-permute-start | bytes 196616 | tf_op jit(solution)/shard_map/ppermute | solution.py:46

commit v8 on v7

--- a/solution.py
+++ b/solution.py
@@ -175,9 +175,10 @@
     distance = jnp.full((RHS, W), far[0, LOCAL_COUNT], jnp.int32).astype(F32).astype(BF16)
     lower = jnp.where(pad, linv[LOCAL_COUNT].astype(F32), 0.0).astype(BF16)
     upper = jnp.where(pad, uinv[0].astype(F32), 0.0).astype(BF16)
-    low_blocks = [times(lblk[LOCAL_COUNT, b], lower).T.astype(BF16) for b in range(2)]
-    up_blocks = [times(upper, ublk[0, b]).T.astype(BF16) for b in range(2)]
-    up_blocks.append(times(upper, lower).T.astype(BF16))
+    turned = lower.T
+    low_blocks = [times_rows(turned, lblk[LOCAL_COUNT, b]).astype(BF16) for b in range(2)]
+    up_blocks = [times_rows(ublk[0, b].T, upper).astype(BF16) for b in range(2)]
+    up_blocks.append(times_rows(turned, upper).astype(BF16))
     for copy in leaf:
         copy.wait()
     for v in range(1, UPPER + 1):

time: 88.5 us -> 88.4 us (level)
  no operation moved by 1% of the time
where the time goes in v8:
time: 88.4 us; the launch traced here: 87.2 us
  waiting for transfers between devices  62.5 us (71%)
  starting transfers between devices  17.4 us (20%)
  Pallas kernels  6.93 us (8%)
    ppermute x19, waiting for transfers between devices, send(): return lax.ppermute(value, AXES, pairs)  62.5 us
    ppermute x19, starting transfers between devices, send(): return lax.ppermute(value, AXES, pairs)  17.4 us
    pallas_call x1, Pallas kernels, begin(): pl.pallas_call(begin_kernel, in_specs=[HBM] * 8, out_specs=[VMEM] * 7, ou...  2.44 us
  transfers between devices with their start and end apart: 19, of which 3 were waited for; matrix products, arithmetic and copies ran while one was open for 0% of the time, Pallas kernels for 1%

profile of v8, /device:TPU:24, one launch (start us, length us, event | category | flops | bytes accessed | tf_op | source)
XLA Modules:
  0.0 87.2 jit_solution(1393732974501006144)
XLA Ops:
  0.0 2.4 %shard_map.82 = (bf16[720,256]{1,0:T(8,128)(2,1)S(1)}, bf16[720,256]{1,0:T(8,128)(2,1)S(1)}, f32[3,16,256]{2,1,0:T(8,128)S(1)}, f32[128,256]{1,0:T(8,128)S(1)}, ...) custom-call(f32[1,4,16,256]{3,2,1,0:T(8,128)} %rights_in.1, ...), custom_call_target="tpu_custom_call" | custom-call | tf_op jit(solution)/shard_map/pallas_call | solution.py:235
  2.4 3.2 %collective-permute-start = (bf16[720,256]{1,0:T(8,128)(2,1)S(1)}, bf16[720,256]{1,0:T(8,128)(2,1)S(1)}, u32[]{:S(2)}, u32[]{:S(2)}) collective-permute-start(bf16[720,256]{1,0:T(8,128)(2,1)S(1)} %get-tuple-element.40.own), channel_id=1, source_target_pairs={{2,0},{3,1},{6,4},{7,5},{10,8},{11,9},{14,12},{15,13},{18,16},{19,... | collective-permute-start | bytes 1105928 | tf_op jit(solution)/shard_map/ppermute | solution.py:46
  5.6 2.0 %collective-permute-start.2 = (bf16[720,256]{1,0:T(8,128)(2,1)S(1)}, bf16[720,256]{1,0:T(8,128)(2,1)S(1)}, u32[]{:S(2)}, u32[]{:S(2)}) collective-permute-start(bf16[720,256]{1,0:T(8,128)(2,1)S(1)} %get-tuple-element.41), channel_id=1, source_target_pairs={{3,0},{2,1},{7,4},{6,5},{11,8},{10,9},{15,12},{14,13},{19,16},{18,... | collective-permute-start | bytes 1105928 | tf_op jit(solution)/shard_map/ppermute | solution.py:46
  7.6 0.7 collective-permute-start.1
  8.3 5.3 %collective-permute-done.a = bf16[720,256]{1,0:T(8,128)(2,1)S(1)} collective-permute-done((bf16[720,256]{1,0:T(8,128)(2,1)S(1)}, bf16[720,256]{1,0:T(8,128)(2,1)S(1)}, u32[]{:S(2)}, u32[]{:S(2)}) %collective-permute-start) | collective-permute-done | bytes 368672 | tf_op jit(solution)/shard_map/ppermute | solution.py:46
  13.6 2.2 %collective-permute-done.2.c = bf16[720,256]{1,0:T(8,128)(2,1)S(1)} collective-permute-done((bf16[720,256]{1,0:T(8,128)(2,1)S(1)}, bf16[720,256]{1,0:T(8,128)(2,1)S(1)}, u32[]{:S(2)}, u32[]{:S(2)}) %collective-permute-start.2) | collective-permute-done | bytes 368672 | tf_op jit(solution)/shard_map/ppermute | solution.py:46
  15.8 0.0 collective-permute-done.1.b
  15.8 0.5 shard_map.83
  16.3 0.7 collective-permute-start.5
  17.0 0.7 collective-permute-start.4
  17.7 0.7 collective-permute-start.3
  18.4 0.0 collective-permute-done.5.c
  18.4 0.0 collective-permute-done.4.b
  18.4 0.0 collective-permute-done.3.a
  18.4 0.5 shard_map.84
  19.0 0.7 collective-permute-start.6
  19.6 0.0 collective-permute-done.6.came
  19.7 0.2 shard_map.85
  19.9 0.7 collective-permute-start.10
  20.6 0.7 collective-permute-start.9
  21.3 0.7 collective-permute-start.8
  22.0 0.7 collective-permute-start.7
  22.7 0.0 collective-permute-done.10.c
  22.7 0.0 collective-permute-done.9.b
  22.7 0.0 collective-permute-done.8.a
  22.7 0.6 shard_map.86
  23.3 0.7 collective-permute-start.12
  24.0 0.7 collective-permute-start.11
  24.7 0.0 collective-permute-done.7.vectors
  24.7 0.0 collective-permute-done.11.late
  24.7 0.0 collective-permute-done.12.came
  24.7 0.0 copy-start.1
  24.7 0.8 shard_map.87
  25.6 0.0 copy-start
  25.6 0.8 collective-permute-start.13
  26.4 0.7 collective-permute-start.15
  27.0 0.7 collective-permute-start.14
  27.7 0.0 collective-permute-done.13.a
  27.7 0.0 collective-permute-done.15.c
  27.7 0.0 collective-permute-done.14.b
  27.7 0.4 shard_map.88
  28.1 0.7 collective-permute-start.16
  28.8 1.3 %collective-permute-start.18 = (bf16[128,256]{1,0:T(8,128)(2,1)S(1)}, bf16[128,256]{1,0:T(8,128)(2,1)S(1)}, u32[]{:S(2)}, u32[]{:S(2)}) collective-permute-start(bf16[128,256]{1,0:T(8,128)(2,1)S(1)} %get-tuple-element.68), channel_id=1, source_target_pairs={{1,3},{5,7},{9,11},{13,15},{17,19},{21,23},{25,27},{29,31},{33,35}... | collective-permute-start | bytes 196616 | tf_op jit(solution)/shard_map/ppermute | solution.py:46
  30.1 0.7 collective-permute-start.17
  30.8 0.0 collective-permute-done.16.a
  30.8 55.0 %collective-permute-done.18.c = bf16[128,256]{1,0:T(8,128)(2,1)S(1)} collective-permute-done((bf16[128,256]{1,0:T(8,128)(2,1)S(1)}, bf16[128,256]{1,0:T(8,128)(2,1)S(1)}, u32[]{:S(2)}, u32[]{:S(2)}) %collective-permute-start.18) | collective-permute-done | bytes 65568 | tf_op jit(solution)/shard_map/ppermute | solution.py:46
  85.8 0.0 collective-permute-done.17.b
  85.8 0.0 copy-done.1
  85.8 0.0 copy-done
  85.8 1.4 %shard_map.89 = f32[1,4,16,256]{3,2,1,0:T(8,128)} custom-call(bf16[1,4,256,256]{3,2,1,0:T(8,128)(2,1)S(1)} %copy-done.1, bf16[1,4,2,256,256]{4,3,2,1,0:T(8,128)(2,1)S(1)} %copy-done, f32[96,256]{1,0:T(8,128)S(1)} %get-tuple-element.37.slots, f32[16,256]{1,0:T(8,128)S(1)} %get-tuple-element.38.level, f32[3,16,256]{2,1,0:T(8,128)S(1)} %get-tuple-element.39.solved, ...), custom_call_target="tpu_custom_call" | custom-call | tf_op jit(solution)/shard_map/pallas_call | solution.py:491
  (5 shorter events, 0.0 us)
Async XLA Ops:
  2.4 11.1 %collective-permute-start = (bf16[720,256]{1,0:T(8,128)(2,1)S(1)}, bf16[720,256]{1,0:T(8,128)(2,1)S(1)}, u32[]{:S(2)}, u32[]{:S(2)}) collective-permute-start(bf16[720,256]{1,0:T(8,128)(2,1)S(1)} %get-tuple-element.40.own), channel_id=1, source_target_pairs={{2,0},{3,1},{6,4},{7,5},{10,8},{11,9},{14,12},{15,13},{18,16},{19,... | collective-permute-start | bytes 1105928 | tf_op jit(solution)/shard_map/ppermute | solution.py:46
  5.6 10.2 %collective-permute-start.2 = (bf16[720,256]{1,0:T(8,128)(2,1)S(1)}, bf16[720,256]{1,0:T(8,128)(2,1)S(1)}, u32[]{:S(2)}, u32[]{:S(2)}) collective-permute-start(bf16[720,256]{1,0:T(8,128)(2,1)S(1)} %get-tuple-element.41), channel_id=1, source_target_pairs={{3,0},{2,1},{7,4},{6,5},{11,8},{10,9},{15,12},{14,13},{19,16},{18,... | collective-permute-start | bytes 1105928 | tf_op jit(solution)/shard_map/ppermute | solution.py:46
  7.6 8.2 %collective-permute-start.1 = (bf16[720,256]{1,0:T(8,128)(2,1)S(1)}, bf16[720,256]{1,0:T(8,128)(2,1)S(1)}, u32[]{:S(2)}, u32[]{:S(2)}) collective-permute-start(bf16[720,256]{1,0:T(8,128)(2,1)S(1)} %get-tuple-element.41), channel_id=1, source_target_pairs={{1,0},{0,1},{5,4},{4,5},{9,8},{8,9},{13,12},{12,13},{17,16},{16,17... | collective-permute-start | bytes 1105928 | tf_op jit(solution)/shard_map/ppermute | solution.py:46
  16.3 2.1 %collective-permute-start.5 = (bf16[704,256]{1,0:T(8,128)(2,1)S(1)}, bf16[704,256]{1,0:T(8,128)(2,1)S(1)}, u32[]{:S(2)}, u32[]{:S(2)}) collective-permute-start(bf16[704,256]{1,0:T(8,128)(2,1)S(1)} %get-tuple-element.45.own), channel_id=1, source_target_pairs={{4,8},{5,9},{24,20},{25,21},{36,40},{37,41},{56,52},{57,53},{68,72... | collective-permute-start | bytes 1081352 | tf_op jit(solution)/shard_map/ppermute | solution.py:46
  17.0 1.4 %collective-permute-start.4 = (bf16[704,256]{1,0:T(8,128)(2,1)S(1)}, bf16[704,256]{1,0:T(8,128)(2,1)S(1)}, u32[]{:S(2)}, u32[]{:S(2)}) collective-permute-start(bf16[704,256]{1,0:T(8,128)(2,1)S(1)} %get-tuple-element.45.own), channel_id=1, source_target_pairs={{12,8},{13,9},{16,20},{17,21},{44,40},{45,41},{48,52},{49,53},{76,... | collective-permute-start | bytes 1081352 | tf_op jit(solution)/shard_map/ppermute | solution.py:46
  17.7 0.7 collective-permute-start.3
  19.0 0.7 collective-permute-start.6
  19.9 2.8 %collective-permute-start.10 = (bf16[704,256]{1,0:T(8,128)(2,1)S(1)}, bf16[704,256]{1,0:T(8,128)(2,1)S(1)}, u32[]{:S(2)}, u32[]{:S(2)}) collective-permute-start(bf16[704,256]{1,0:T(8,128)(2,1)S(1)} %get-tuple-element.51.own), channel_id=1, source_target_pairs={{8,104},{9,105},{20,116},{21,117},{40,72},{41,73},{52,84},{53,85},... | collective-permute-start | bytes 1081352 | tf_op jit(solution)/shard_map/ppermute | solution.py:46
  20.6 2.1 %collective-permute-start.9 = (bf16[704,256]{1,0:T(8,128)(2,1)S(1)}, bf16[704,256]{1,0:T(8,128)(2,1)S(1)}, u32[]{:S(2)}, u32[]{:S(2)}) collective-permute-start(bf16[704,256]{1,0:T(8,128)(2,1)S(1)} %get-tuple-element.51.own), channel_id=1, source_target_pairs={{8,72},{9,73},{20,84},{21,85},{40,104},{41,105},{52,116},{53,117},... | collective-permute-start | bytes 1081352 | tf_op jit(solution)/shard_map/ppermute | solution.py:46
  21.3 1.4 %collective-permute-start.8 = (bf16[704,256]{1,0:T(8,128)(2,1)S(1)}, bf16[704,256]{1,0:T(8,128)(2,1)S(1)}, u32[]{:S(2)}, u32[]{:S(2)}) collective-permute-start(bf16[704,256]{1,0:T(8,128)(2,1)S(1)} %get-tuple-element.51.own), channel_id=1, source_target_pairs={{8,40},{9,41},{20,52},{21,53},{40,8},{41,9},{52,20},{53,21},{72,10... | collective-permute-start | bytes 1081352 | tf_op jit(solution)/shard_map/ppermute | solution.py:46
  22.0 2.7 %collective-permute-start.7 = (bf16[272,256]{1,0:T(8,128)(2,1)S(1)}, bf16[272,256]{1,0:T(8,128)(2,1)S(1)}, u32[]{:S(2)}, u32[]{:S(2)}) collective-permute-start(bf16[272,256]{1,0:T(8,128)(2,1)S(1)} %pad_maximum_fusion), channel_id=1, source_target_pairs={{0,1},{4,5},{8,9},{12,13},{16,17},{20,21},{24,25},{28,29},{32,33},... | collective-permute-start | bytes 417800 | tf_op jit(solution)/shard_map/ppermute | solution.py:46
  23.3 1.4 %collective-permute-start.12 = (bf16[272,256]{1,0:T(8,128)(2,1)S(1)}, bf16[272,256]{1,0:T(8,128)(2,1)S(1)}, u32[]{:S(2)}, u32[]{:S(2)}) collective-permute-start(bf16[272,256]{1,0:T(8,128)(2,1)S(1)} %pad_maximum_fusion.1), channel_id=1, source_target_pairs={{8,139},{20,151},{40,171},{52,183},{72,203},{84,215},{104,235},{11... | collective-permute-start | bytes 417800 | tf_op jit(solution)/shard_map/ppermute | solution.py:46
  24.0 0.7 collective-permute-start.11
  24.7 61.1 %copy-start.1 = (bf16[1,4,256,256]{3,2,1,0:T(8,128)(2,1)S(1)}, bf16[1,4,256,256]{3,2,1,0:T(8,128)(2,1)}, u32[]{:S(2)}) copy-start(bf16[1,4,256,256]{3,2,1,0:T(8,128)(2,1)} %uinv.1) | copy-start | bytes 1572868
  25.6 60.3 %copy-start = (bf16[1,4,2,256,256]{4,3,2,1,0:T(8,128)(2,1)S(1)}, bf16[1,4,2,256,256]{4,3,2,1,0:T(8,128)(2,1)}, u32[]{:S(2)}) copy-start(bf16[1,4,2,256,256]{4,3,2,1,0:T(8,128)(2,1)} %ublk.1) | copy-start | bytes 3145732
  25.6 2.2 %collective-permute-start.13 = (bf16[96,256]{1,0:T(8,128)(2,1)S(1)}, bf16[96,256]{1,0:T(8,128)(2,1)S(1)}, u32[]{:S(2)}, u32[]{:S(2)}) collective-permute-start(bf16[96,256]{1,0:T(8,128)(2,1)S(1)} %get-tuple-element.62.own), channel_id=1, source_target_pairs={{9,13},{21,17},{41,45},{53,49},{73,77},{85,81},{105,109},{117,113}... | collective-permute-start | bytes 147464 | tf_op jit(solution)/shard_map/ppermute | solution.py:46
  26.4 1.4 %collective-permute-start.15 = (bf16[96,256]{1,0:T(8,128)(2,1)S(1)}, bf16[96,256]{1,0:T(8,128)(2,1)S(1)}, u32[]{:S(2)}, u32[]{:S(2)}) collective-permute-start(bf16[96,256]{1,0:T(8,128)(2,1)S(1)} %get-tuple-element.63), channel_id=1, source_target_pairs={{9,5},{21,25},{41,37},{53,57},{73,69},{85,89},{105,101},{117,121},... | collective-permute-start | bytes 147464 | tf_op jit(solution)/shard_map/ppermute | solution.py:46
  27.0 0.7 collective-permute-start.14
  28.1 2.7 %collective-permute-start.16 = (bf16[128,256]{1,0:T(8,128)(2,1)S(1)}, bf16[128,256]{1,0:T(8,128)(2,1)S(1)}, u32[]{:S(2)}, u32[]{:S(2)}) collective-permute-start(bf16[128,256]{1,0:T(8,128)(2,1)S(1)} %get-tuple-element.67.own), channel_id=1, source_target_pairs={{1,0},{5,4},{9,8},{13,12},{17,16},{21,20},{25,24},{29,28},{33,32},... | collective-permute-start | bytes 196616 | tf_op jit(solution)/shard_map/ppermute | solution.py:46
  28.8 57.0 %collective-permute-start.18 = (bf16[128,256]{1,0:T(8,128)(2,1)S(1)}, bf16[128,256]{1,0:T(8,128)(2,1)S(1)}, u32[]{:S(2)}, u32[]{:S(2)}) collective-permute-start(bf16[128,256]{1,0:T(8,128)(2,1)S(1)} %get-tuple-element.68), channel_id=1, source_target_pairs={{1,3},{5,7},{9,11},{13,15},{17,19},{21,23},{25,27},{29,31},{33,35}... | collective-permute-start | bytes 196616 | tf_op jit(solution)/shard_map/ppermute | solution.py:46
  30.1 55.7 %collective-permute-start.17 = (bf16[128,256]{1,0:T(8,128)(2,1)S(1)}, bf16[128,256]{1,0:T(8,128)(2,1)S(1)}, u32[]{:S(2)}, u32[]{:S(2)}) collective-permute-start(bf16[128,256]{1,0:T(8,128)(2,1)S(1)} %get-tuple-element.68), channel_id=1, source_target_pairs={{1,2},{5,6},{9,10},{13,14},{17,18},{21,22},{25,26},{29,30},{33,34}... | collective-permute-start | bytes 196616 | tf_op jit(solution)/shard_map/ppermute | solution.py:46
